TPU v7x, 256 devices: a whole 4x4x8 slice. The times are simulated.
256 devices in a mesh: row: 16 (over x, z_hi), col: 16 (over y, z_lo, core).
Axes of the slice: x: 4, y: 4, z: 8 (z_hi: 4, z_lo: 2; z = z_hi * 2 + z_lo), core: 2. Of those that a mesh axis runs over, the one named last changes fastest.
Arguments:
- gradient: bfloat16 [8192, 28672], P('row', 'col')
Outputs:
- left_gram: float32 [8192, 2048], P('row', 'col')
- right_gram: float32 [28672, 1792], P(('col', 'row'))
All inputs are finite; a program needn't handle non-finite values.
Results may differ from a plain program's by a relative error of at most 0.0003.
Values may be sent and summed in bfloat16 or wider, within the bound.
No kernel may reach another device: no remote copies, remote signals or barrier semaphores. Data moves between devices by JAX's collectives and lax.ppermute only.
A program may use at most 64 MiB of HBM per device.

v0:
```python
import functools
import itertools

import jax
import jax.numpy as jnp
from jax import lax
from jax.experimental import pallas as pl
from jax.experimental.pallas import tpu as pltpu
from jax.sharding import PartitionSpec as P

F32, BF16 = jnp.float32, jnp.bfloat16

SIZES = (4, 4, 4, 2, 2)
PLACES = list(itertools.product(*(range(n) for n in SIZES)))
STEPS = (1, 3, 2)
Z_STEPS = (1, 7, 2, 6, 3, 5, 4)
FLOPS = 4_000_000_000


def number(place):
    x, zh, y, zl, core = (p % n for p, n in zip(place, SIZES))
    return (4 * x + zh) * 16 + 4 * y + 2 * zl + core


def send(array, to):
    return lax.ppermute(array, ("row", "col"), [(number(p), number(to(*p))) for p in PLACES])


POWER = 13
LIFT = 120 / POWER
LOG_LIFT = LIFT * 0.6931471805599453


def split(norms):
    lead = norms.astype(BF16).astype(F32)
    trail = (norms - lead).astype(BF16).astype(F32)
    return lead, trail, lead + trail


def inverse(norms):
    return jnp.where(norms > 0, 1.0 / jnp.where(norms > 0, norms, 1.0), 0.0)


def raised(value, rows, cols):
    ratio = value * rows * (cols * 2.0**LIFT)
    p2 = ratio * ratio
    p4 = p2 * p2
    return p4 * p4 * (p4 * ratio)


def root(code, rows, cols):
    size = jnp.exp(jnp.log(jnp.abs(code)) * (1.0 / POWER) - LOG_LIFT)
    return jnp.where(code < 0, -size, size) * (rows * cols)


def upright(row):
    parts = [row[:, i : i + 128] for i in range(0, row.shape[1], 128)]
    return jnp.concatenate([jnp.broadcast_to(p, (128, 128)).T for p in parts], 0)


def dot(left, right, dim):
    return lax.dot_general(
        left, right, (((dim,), (dim,)), ((), ())), preferred_element_type=F32
    )


def run(body, outs, scratch, flops, *args):
    smem, vmem = pl.BlockSpec(memory_space=pltpu.SMEM), pl.BlockSpec(memory_space=pltpu.VMEM)
    return pl.pallas_call(
        body,
        out_shape=[jax.ShapeDtypeStruct(shape, dtype) for shape, dtype in outs],
        in_specs=[smem] + [vmem] * (len(args) - 1),
        out_specs=[vmem] * len(outs),
        scratch_shapes=[pltpu.VMEM(shape, dtype) for shape, dtype in scratch],
        cost_estimate=pl.CostEstimate(
            flops=flops, bytes_accessed=sum(a.size * a.dtype.itemsize for a in args), transcendentals=0
        ),
        compiler_params=pltpu.CompilerParams(vmem_limit_bytes=48 * 1024 * 1024),
    )(*args)


BLOCK, CHUNK, TILES, WINDOW, IMAGE = 448, 112, 14, 1408, 384
WIDTH = WINDOW + IMAGE


def first_tile(d):
    return 7 * (d // 2) + 3 * (d % 2)


def lead_in(d):
    return 64 * (d % 2)


def tile(i):
    return pl.ds(pl.multiple_of(i * 128, 128), 128)


HALF_ROWS = BLOCK // 2
PARTS = [slice(i, min(i + 256, WINDOW)) for i in range(0, WINDOW, 256)]


def fill_window(g_ref, w_ref, l_ref, d):
    for t in range(11):
        w_ref[:, t * 128 : (t + 1) * 128] = g_ref[:, tile(lax.rem(first_tile(d) + t, TILES))]
    l_ref[...] = w_ref[:, :512].T


def tile_after(d):
    return pl.ds(pl.multiple_of(128 * (d % 2), 128), IMAGE)


def column_norms(w_ref):
    return jnp.sqrt(jnp.sum(jnp.square(w_ref[...].astype(F32)), 0, keepdims=True))


def padded(rows, count):
    rows = jnp.concatenate(rows, 0)
    return jnp.concatenate([rows, jnp.zeros((count - rows.shape[0], rows.shape[1]), F32)], 0)


def rows_of(r_ref, norms, d, start=0, count=BLOCK):
    r_ref[...] = upright(norms[:, :512])
    return r_ref[pl.ds(pl.multiple_of(lead_in(d) + start, 16), count), :]


def wide(rows, lanes):
    return rows if lanes.stop - lanes.start == 128 else jnp.concatenate([rows, rows], 1)


def product(l_ref, w_ref, lanes, d):
    left = l_ref[pl.ds(pl.multiple_of(lead_in(d), 64), BLOCK), :]
    return jnp.dot(left, w_ref[:, lanes], preferred_element_type=F32)


def right_far(at_ref, g_ref, out_a, out_b, w_ref, l_ref, r_ref):
    d = lax.rem(at_ref[0] + 2, 4)
    fill_window(g_ref, w_ref, l_ref, d)
    lead, trail, norms = split(column_norms(w_ref))
    tail = padded([lead, trail], 16).astype(BF16)
    cols = inverse(norms)
    rows = rows_of(r_ref, cols, d)
    for ref in (out_a, out_b):
        ref[HALF_ROWS:, :] = tail
    for lanes in PARTS:
        code = raised(product(l_ref, w_ref, lanes, d), wide(rows, lanes), cols[:, lanes]).astype(BF16)
        out_a[:HALF_ROWS, lanes] = code[:HALF_ROWS]
        out_b[:HALF_ROWS, lanes] = code[HALF_ROWS:]


def right_near(step, at_ref, g_ref, in_ref, out_ref, w_ref, l_ref, r_ref, p_ref):
    d = lax.rem(at_ref[0] + step, 4)
    start = 0 if step == 1 else HALF_ROWS
    fill_window(g_ref, w_ref, l_ref, d)
    tail = in_ref[HALF_ROWS:, :].astype(F32)
    theirs = tail[0:1] + tail[1:2]
    their_rows = rows_of(r_ref, theirs, d, start, HALF_ROWS)
    lead, trail, norms = split(jnp.sqrt(jnp.square(column_norms(w_ref)) + jnp.square(theirs)))
    out_ref[BLOCK:, :] = padded([lead, trail], 16).astype(BF16)
    cols = inverse(norms)
    rows = rows_of(r_ref, cols, d)
    here = slice(start, start + HALF_ROWS)
    for lanes in PARTS:
        part = p_ref.at[:, : lanes.stop - lanes.start]
        part[...] = product(l_ref, w_ref, lanes, d)
        part[here, :] += root(in_ref[:HALF_ROWS, lanes].astype(F32), wide(their_rows, lanes), theirs[:, lanes])
        out_ref[:BLOCK, lanes] = raised(part[...], wide(rows, lanes), cols[:, lanes]).astype(BF16)


def right_second(at_ref, g_ref, in_1, in_3, out_1, out_3, out_2, own_ref, w_ref, l_ref, r_ref, e_ref, t_ref):
    d, zh = at_ref[0], at_ref[1]
    fill_window(g_ref, w_ref, l_ref, d)
    squares, theirs = jnp.square(column_norms(w_ref)), []
    for ref in (in_1, in_3):
        tail = ref[BLOCK:, :].astype(F32)
        norms = tail[0:1] + tail[1:2]
        squares += jnp.square(norms)
        theirs.append((ref, norms, rows_of(r_ref, norms, d)))
    lead, trail, norms = split(jnp.sqrt(squares))
    cols = inverse(norms)
    rows = rows_of(r_ref, cols, d)
    begin = pl.multiple_of(lead_in(d), 64)
    e_ref[:64, :] = jnp.zeros((64, WINDOW), F32)
    e_ref[BLOCK:, :] = jnp.zeros((64, WINDOW), F32)
    for lanes in PARTS:
        part = product(l_ref, w_ref, lanes, d)
        for ref, their_cols, their_rows in theirs:
            part += root(ref[:BLOCK, lanes].astype(F32), wide(their_rows, lanes), their_cols[:, lanes])
        e_ref[pl.ds(begin, BLOCK), lanes] = raised(part, wide(rows, lanes), cols[:, lanes])
    for i in range(5):
        for j in range(4):
            t_ref[i * 128 : (i + 1) * 128, j * 128 : (j + 1) * 128] = e_ref[
                j * 128 : (j + 1) * 128, 384 + i * 128 : 512 + i * 128
            ].T
    tails = [jnp.concatenate([v[:, t * 128 : (t + 1) * 128] for t in range(11)], 0) for v in (lead, trail, norms)]
    for step, ref in ((1, out_1), (3, out_3), (2, out_2), (0, own_ref)):
        chunk = lax.rem(zh + step, 4) * CHUNK
        piece = e_ref[pl.ds(pl.multiple_of(begin + chunk, 16), CHUNK), :]
        image = t_ref[pl.ds(pl.multiple_of(64 + begin + chunk, 16), CHUNK), tile_after(d)]
        ref[:, :WINDOW] = piece.astype(ref.dtype)
        ref[:, WINDOW:WIDTH] = image.astype(ref.dtype)
        ref[:, WIDTH:] = padded(tails[:2] if step else tails[2:], CHUNK).astype(ref.dtype)


def right_third(scale, at_ref, own_ref, in_1, in_3, in_2, out_ref, image_ref, r_ref, n_ref):
    d, zh = at_ref[0], at_ref[1]
    begin = pl.multiple_of(lead_in(d) + zh * CHUNK, 16)
    for i, ref in enumerate((own_ref, in_1, in_3, in_2)):
        tail = ref[:, WIDTH:].astype(F32)
        n_ref[...] = tail[:11] if i == 0 else tail[:11] + tail[11:22]
        for t in range(8):
            r_ref[t * 128 : (t + 1) * 128, :] = upright(n_ref[t : t + 1, :])
        rows = r_ref[pl.ds(begin, CHUNK), :]
        image_rows = r_ref[pl.ds(pl.multiple_of(448 + begin, 16), CHUNK), :]
        for t in range(14):
            lanes = slice(t * 128, (t + 1) * 128)
            code = ref[:, lanes].astype(F32)
            if t < 11:
                to, here, part = out_ref, lanes, root(code, rows, n_ref[t : t + 1, :])
            else:
                here = slice((t - 11) * 128, (t - 10) * 128)
                cols = n_ref[pl.ds(t - 11 + lax.rem(d, 2), 1), :]
                to, part = image_ref, root(code, image_rows, cols)
            if i == 0:
                to[:, here] = part * scale
            else:
                to[:, here] += part * scale


def right_last(at_ref, base_ref, image_ref, out_ref):
    d = at_ref[0]
    for t in range(14):
        ref, i = (base_ref, t) if t < 11 else (image_ref, t - 11)
        out_ref[:, tile(lax.rem(first_tile(d) + t, TILES))] = ref[:, i * 128 : (i + 1) * 128]


SUB, BASE, ROWS = 128, 1024, 1152


def sub(i):
    return pl.ds(pl.multiple_of(i * SUB, SUB), SUB)


def base_subs(core, b):
    return [4 * a + (core ^ (a > b).astype(jnp.int32)) + 2 * h for a in range(4) for h in (0, 1)]


def slot(i):
    return i // 4 * 4 + 2 * (i % 2) + i // 2 % 2


def more_sub(core, b, zl):
    return 4 * b + lax.rem(2 * zl + core + 1, 4)


def two_cols(ref, core, b):
    return jnp.concatenate([ref[pl.ds(4 * b + core + 2 * zl, 1), :] for zl in (0, 1)], 1)


def left_first(at_ref, far, near, far_2, near_2, out_1, out_3, out_2, own_ref, norm_ref, a_ref, b_ref, i_ref, s_ref):
    zh, y, core = at_ref[1], at_ref[2], at_ref[4]
    for p, ref in enumerate((far, near, far_2, near_2)):
        j = 2 * ((p // 2) ^ core) + lax.rem(p + zh, 2)
        for m in range(4):
            a_ref[sub(4 * j + slot(m)), :] = ref[m * SUB : (m + 1) * SUB, :]
    leads, trails, lanes = [], [], []
    for i in range(16):
        rows = slice(slot(i) * SUB, (slot(i) + 1) * SUB)
        squares = jnp.sum(jnp.square(a_ref[rows, :].astype(F32)), 1, keepdims=True)
        row = jnp.broadcast_to(jnp.sqrt(squares), (SUB, SUB)).T[0:1]
        lead, trail, norms = split(row)
        leads.append(lead), trails.append(trail), lanes.append(norms)
        i_ref[rows, :] = upright(inverse(norms))
    tail = jnp.concatenate([jnp.concatenate(leads, 0), jnp.concatenate(trails, 0)], 1).astype(BF16)
    norm_ref[...] = jnp.concatenate(lanes, 0)
    s_ref[...] = inverse(norm_ref[...])
    for step, out in ((1, out_1), (3, out_3), (2, out_2), (0, own_ref)):
        b = lax.rem(y + step, 4)
        for zl in (0, 1):
            b_ref[zl * SUB : (zl + 1) * SUB, :] = a_ref[sub(slot(4 * b + core + 2 * zl)), :]
        cols = two_cols(s_ref, core, b)
        for k, i in enumerate(base_subs(core, b)[::2]):
            pair = pl.ds(pl.multiple_of(slot(i) * SUB, 2 * SUB), 2 * SUB)
            part = dot(a_ref[pair, :], b_ref[...], 1)
            if step:
                scale = i_ref[pair, :]
                part = raised(part, jnp.concatenate([scale, scale], 1), cols).astype(BF16)
            out[k * 2 * SUB : (k + 1) * 2 * SUB, :] = part
        for zl in (0, 1):
            here = slice(zl * SUB, (zl + 1) * SUB)
            i = slot(more_sub(core, b, zl))
            part = dot(a_ref[sub(i), :], b_ref[here, :], 1)
            if step:
                part = raised(part, i_ref[sub(i), :], cols[:, here]).astype(BF16)
            out[BASE:ROWS, here] = part
        if step:
            out[ROWS:, :] = tail


def left_second(at_ref, own_ref, norm_ref, in_1, in_3, in_2, *refs):
    outs, (e_ref, s_ref, lead_ref, trail_ref, n_ref) = refs[:8], refs[8:]
    zh, y, zl, core = (at_ref[i] for i in (1, 2, 3, 4))
    squares = jnp.square(norm_ref[...])
    for k, ref in enumerate((in_1, in_3, in_2)):
        tail = ref[ROWS:, :].astype(F32)
        norms = tail[:, :SUB] + tail[:, SUB:]
        squares += jnp.square(norms)
        s_ref[k] = norms
    lead_ref[...], trail_ref[...], n_ref[...] = split(jnp.sqrt(squares))
    s_ref[3] = inverse(n_ref[...])
    sources = [(ref, k) for k, ref in enumerate((in_1, in_3, in_2))]
    cols = [two_cols(s_ref.at[k], core, y) for k in range(4)]
    r = lambda k, i: upright(s_ref.at[k][pl.ds(i, 1), :])
    for j, i in enumerate(base_subs(core, y)):
        rows = slice(j * SUB, (j + 1) * SUB)
        part = own_ref[rows, :]
        for ref, k in sources:
            scale = r(k, i)
            part += root(ref[rows, :].astype(F32), jnp.concatenate([scale, scale], 1), cols[k])
        scale = r(3, i)
        e_ref[rows, :] = raised(part, jnp.concatenate([scale, scale], 1), cols[3])
    for l in (0, 1):
        here = slice(l * SUB, (l + 1) * SUB)
        i = more_sub(core, y, l)
        part = own_ref[BASE:ROWS, here]
        for ref, k in sources:
            part += root(ref[BASE:ROWS, here].astype(F32), r(k, i), cols[k][:, here])
        e_ref[BASE:ROWS, here] = raised(part, r(3, i), cols[3][:, here])
    for step, out in zip((*Z_STEPS, 0), outs):
        z = lax.rem(2 * zh + zl + step, 8)
        to_h, to_l = z // 2, lax.rem(z, 2)
        lanes = tile(to_l)
        out[:256, :] = e_ref[pl.ds(pl.multiple_of(to_h * 256, 256), 256), lanes].astype(out.dtype)
        out[256:384, :] = e_ref[BASE:ROWS, lanes].astype(out.dtype)
        first = 4 * to_h + (core ^ (to_h > y).astype(jnp.int32))
        picks = [first, first + 2, more_sub(core, y, to_l), 4 * y + 2 * to_l + core]
        tail = [ref[pl.ds(i, 1), :] for ref in ((lead_ref, trail_ref) if step else (n_ref,)) for i in picks]
        out[384:, :] = padded(tail, 16).astype(out.dtype)


def left_third(scale, at_ref, *refs):
    sources, (base_ref, more_ref, same_ref, other_ref, sum_ref) = refs[:8], refs[8:]
    zh, y, zl = at_ref[1], at_ref[2], at_ref[3]
    for k, ref in enumerate(sources):
        tail = ref[384:, :].astype(F32)
        norms = tail[0:4] if k == 0 else tail[0:4] + tail[4:8]
        for j in range(3):
            rows = slice(j * SUB, (j + 1) * SUB)
            part = root(ref[rows, :].astype(F32), upright(norms[j : j + 1]), norms[3:4]) * scale
            if k == 0:
                sum_ref[rows, :] = part
            else:
                sum_ref[rows, :] += part
    first, second, more = (sum_ref[j * SUB : (j + 1) * SUB, :] for j in range(3))
    base_ref[...] = sum_ref[:256, :]
    more_ref[...] = more
    same_ref[...] = jnp.where(zh == y, more, jnp.where(zl == 0, first, second)).T
    other_ref[...] = jnp.where(zl == 0, second, first).T


def left_last(at_ref, base_ref, more_ref, same_ref, other_ref, out_ref):
    zh, y, zl, core = (at_ref[i] for i in (1, 2, 3, 4))
    n, parity, diagonal = 2 * zl + core, core ^ (zh > y).astype(jnp.int32), zh == y
    out_ref[sub(parity), :] = base_ref[:SUB, :]
    out_ref[sub(parity + 2), :] = base_ref[SUB:, :]
    out_ref[sub(jnp.where(diagonal, lax.rem(n + 3, 4), 2 * zl + 1 - parity)), :] = same_ref[...]
    out_ref[sub(jnp.where(diagonal, lax.rem(n + 1, 4), 2 * (1 - zl) + 1 - parity)), :] = jnp.where(
        diagonal, more_ref[...], other_ref[...]
    )


def mirror(step):
    def to(x, zh, y, zl, core):
        if zh != y:
            return (x, y, zh, zl ^ step, core ^ (zh > y))
        n = (2 * zl + core + 1 - step) % 4
        return (x, zh, y, n // 2, n % 2)

    return to


def along_z(step):
    def to(x, zh, y, zl, core):
        z = (2 * zh + zl + step) % 8
        return (x, z // 2, y, z % 2, core)

    return to


def shards(gradient):
    rows, width = gradient.shape
    row, col = lax.axis_index("row"), lax.axis_index("col")
    x, zh, y, zl, core = row // 4, row % 4, col // 4, col // 2 % 2, col % 2
    at = jnp.stack([x, zh, y, zl, core, x, x, x]).astype(jnp.int32)
    barrier = lax.optimization_barrier
    half = width // 2

    cut = lambda parity: lax.dynamic_slice_in_dim(gradient, parity * half, half, 1)
    near, far, gradient = barrier((cut((zh + 1) % 2), cut(zh % 2), gradient))
    near = send(near, lambda x, zh, y, zl, core: (x, 2 * core + (zh + 1) % 2, y, zl, zh // 2))
    far = send(far, lambda x, zh, y, zl, core: (x, 2 * core + zh % 2, y, zl, zh // 2))

    window = [((rows, WINDOW), BF16), ((512, 512), BF16), ((512, 128), F32)]
    half_part, whole_part = ((HALF_ROWS + 16, WINDOW), BF16), ((BLOCK + 16, WINDOW), BF16)
    over_x = lambda s, v: send(v, lambda x, zh, y, zl, core: (x + s, zh, y, zl, core))
    far_1, far_3 = run(right_far, [half_part] * 2, window, FLOPS, at, gradient)
    far_1, far_3 = over_x(1, far_1), over_x(3, far_3)
    add = lambda s, v: run(
        functools.partial(right_near, s), [whole_part], window + [((BLOCK, 256), F32)], FLOPS, at, gradient, v
    )[0]
    code_1, code_3 = add(1, far_1), add(3, far_3)
    right_1, right_3 = over_x(1, code_1), over_x(3, code_3)
    near, far, _ = barrier((near, far, (code_1, code_3)))

    swap = lambda x, zh, y, zl, core: (x, zh, y, zl, 1 - core)
    far_2, near_2 = send(far, swap), send(near, swap)
    packed = (ROWS + 16, 256)
    left_1, left_3, left_2, left_own, norms = run(
        left_first,
        [(packed, BF16)] * 3 + [((ROWS, 256), F32), ((16, SUB), F32)],
        [((2048, half), BF16), ((256, half), BF16), ((2048, SUB), F32), ((16, SUB), F32)],
        FLOPS,
        at,
        far,
        near,
        far_2,
        near_2,
    )
    right_1, right_3, _ = barrier((right_1, right_3, left_1))
    over_y = lambda s, v: send(v, lambda x, zh, y, zl, core: (x, zh, y + s, zl, core))
    left_1, left_3, left_2 = over_y(1, left_1), over_y(3, left_3), over_y(2, left_2)

    piece = (CHUNK, WIDTH + 128)
    code_1, code_3, code_2, right_own = run(
        right_second,
        [(piece, BF16)] * 3 + [(piece, F32)],
        window + [((512, WINDOW), F32), ((640, 512), F32)],
        FLOPS,
        at,
        gradient,
        right_1,
        right_3,
    )
    over_z = lambda s, v: send(v, lambda x, zh, y, zl, core: (x, zh + s, y, zl, core))
    right_2, right_1 = over_z(2, code_2), over_z(1, code_1)
    code_3, _ = barrier((code_3, left_3))
    right_3 = over_z(3, code_3)
    left_1, left_3, left_2, right_1, right_3, right_2 = barrier(
        (left_1, left_3, left_2, right_1, right_3, right_2)
    )

    piece = (400, SUB)
    codes = run(
        left_second,
        [(piece, BF16)] * 7 + [(piece, F32)],
        [((ROWS, 256), F32), ((4, 16, SUB), F32)] + [((16, SUB), F32)] * 3,
        FLOPS,
        at,
        left_own,
        norms,
        left_1,
        left_3,
        left_2,
    )
    right_1, right_3, _ = barrier((right_1, right_3, codes))
    arrived = [send(code, along_z(s)) for s, code in zip(Z_STEPS, codes)]

    right_base, image = run(
        functools.partial(right_third, 1.0 / (rows * 16)),
        [((CHUNK, WINDOW), F32), ((CHUNK, IMAGE), F32)],
        [((1024, 128), F32), ((11, 128), F32)],
        FLOPS,
        at,
        right_own,
        right_1,
        right_3,
        right_2,
    )
    image = over_x(1, image)
    right_gram = run(right_last, [((CHUNK, width), F32)], [], FLOPS, at, right_base, image)[0]

    square = ((SUB, SUB), F32)
    base, more, same, other = run(
        functools.partial(left_third, 1.0 / (width * 16)),
        [((256, SUB), F32), square, square, square],
        [((384, SUB), F32)],
        FLOPS,
        at,
        codes[7],
        *arrived,
    )
    same, other = send(same, mirror(0)), send(other, mirror(1))
    left_gram = run(left_last, [((512, SUB), F32)], [], FLOPS, at, base, more, same, other)[0]
    return (left_gram, right_gram)


def solution(mesh):
    in_specs = (P("row", "col"),)
    out_specs = (P("row", "col"), P(("col", "row"), None))
    return jax.shard_map(shards, mesh=mesh, in_specs=in_specs, out_specs=out_specs, check_vma=False)
```

profile of v0, /device:TPU:25, one launch (start us, length us, event | category | flops | bytes accessed | tf_op | source)
XLA Modules:
  0.0 187.3 jit_solution(1270608962958362747)
XLA Ops:
  0.8 2.7 %constant_dynamic-slice_fusion = (bf16[512,896]{1,0:T(8,128)(2,1)S(1)}, bf16[512,896]{1,0:T(8,128)(2,1)}) fusion(bf16[512,1792]{1,0:T(8,128)(2,1)} %g_ref.3, s32[]{:T(128)S(6)} %select_n.48, s32[]{:T(128)S(6)} %select_n.46), kind=kLoop, calls=%fused_computation | loop fusion | bytes 3670024 | tf_op jit(solution)/shard_map/dynamic_slice | solution.py:397
  3.5 1.9 %shard_map.30 = (bf16[240,1408]{1,0:T(8,128)(2,1)S(1)}, bf16[240,1408]{1,0:T(8,128)(2,1)S(1)}) custom-call(s32[8]{0:T(128)S(1)} %stack.26.at_ref, bf16[512,1792]{1,0:T(8,128)(2,1)S(1)} %copy-done), custom_call_target="tpu_custom_call" | custom-call | flops 4000000000 | bytes 1835040 | tf_op jit(solution)/shard_map/pallas_call | solution.py:69
  6.7 1.5 collective-permute-start.3
  8.2 7.1 %collective-permute-start = (bf16[512,896]{1,0:T(8,128)(2,1)S(1)}, bf16[512,896]{1,0:T(8,128)(2,1)S(1)}, u32[]{:S(2)}, u32[]{:S(2)}) collective-permute-start(bf16[512,896]{1,0:T(8,128)(2,1)S(1)} %copy-done.2), channel_id=1, source_target_pairs={{0,16},{1,48},{2,18},{3,50},{4,20},{5,52},{6,22},{7,54},{8,24},{9,... | collective-permute-start | bytes 2752520 | tf_op jit(solution)/shard_map/ppermute | solution.py:26
  15.3 2.8 %collective-permute-start.1 = (bf16[512,896]{1,0:T(8,128)(2,1)S(1)}, bf16[512,896]{1,0:T(8,128)(2,1)S(1)}, u32[]{:S(2)}, u32[]{:S(2)}) collective-permute-start(bf16[512,896]{1,0:T(8,128)(2,1)S(1)} %get-tuple-element.44), channel_id=1, source_target_pairs={{0,0},{1,32},{2,2},{3,34},{4,4},{5,36},{6,6},{7,38},{8,8},{9,40},{... | collective-permute-start | bytes 2752520 | tf_op jit(solution)/shard_map/ppermute | solution.py:26
  18.1 4.6 %collective-permute-done.2.in_ref = bf16[240,1408]{1,0:T(8,128)(2,1)S(1)} collective-permute-done((bf16[240,1408]{1,0:T(8,128)(2,1)S(1)}, bf16[240,1408]{1,0:T(8,128)(2,1)S(1)}, u32[]{:S(2)}, u32[]{:S(2)}) %collective-permute-start.2) | collective-permute-done | bytes 675872 | tf_op jit(solution)/shard_map/ppermute | solution.py:26
  22.7 2.5 %shard_map.31 = bf16[464,1408]{1,0:T(8,128)(2,1)S(1)} custom-call(s32[8]{0:T(128)S(1)} %stack.26.at_ref, bf16[512,1792]{1,0:T(8,128)(2,1)S(1)} %copy-done, bf16[240,1408]{1,0:T(8,128)(2,1)S(1)} %collective-permute-done.2.in_ref), custom_call_target="tpu_custom_call" | custom-call | flops 4000000000 | bytes 2510880 | tf_op jit(solution)/shard_map/pallas_call | solution.py:69
  25.3 2.6 %shard_map.32 = bf16[464,1408]{1,0:T(8,128)(2,1)S(1)} custom-call(s32[8]{0:T(128)S(1)} %stack.26.at_ref, bf16[512,1792]{1,0:T(8,128)(2,1)S(1)} %copy-done, bf16[240,1408]{1,0:T(8,128)(2,1)S(1)} %collective-permute-done.3.in_ref), custom_call_target="tpu_custom_call" | custom-call | flops 4000000000 | bytes 2510880 | tf_op jit(solution)/shard_map/pallas_call | solution.py:69
  27.9 27.3 %collective-permute-done.near = bf16[512,896]{1,0:T(8,128)(2,1)S(1)} collective-permute-done((bf16[512,896]{1,0:T(8,128)(2,1)S(1)}, bf16[512,896]{1,0:T(8,128)(2,1)S(1)}, u32[]{:S(2)}, u32[]{:S(2)}) %collective-permute-start) | collective-permute-done | bytes 917536 | tf_op jit(solution)/shard_map/ppermute | solution.py:26
  58.9 5.9 %shard_map.33 = (bf16[1168,256]{1,0:T(8,128)(2,1)S(1)}, bf16[1168,256]{1,0:T(8,128)(2,1)S(1)}, bf16[1168,256]{1,0:T(8,128)(2,1)S(1)}, f32[1152,256]{1,0:T(8,128)}, f32[16,128]{1,0:T(8,128)S(1)}) custom-call(s32[8]{0:T(128)S(1)} %stack.26.at_ref, bf16[512,896]{1,0:T(8,128)(2,1)S(1)} %collective-permute-done.1.far, ...), custom_call_target="tpu_custom_call" | custom-call | flops 4000000000 | bytes 3670048 | tf_op jit(solution)/shard_map/pallas_call | solution.py:69
  65.8 2.1 %collective-permute-start.6 = (bf16[1168,256]{1,0:T(8,128)(2,1)S(1)}, bf16[1168,256]{1,0:T(8,128)(2,1)S(1)}, u32[]{:S(2)}, u32[]{:S(2)}) collective-permute-start(bf16[1168,256]{1,0:T(8,128)(2,1)S(1)} %get-tuple-element.52), channel_id=1, source_target_pairs={{0,4},{1,5},{2,6},{3,7},{4,8},{5,9},{6,10},{7,11},{8,12},{9,13},{1... | collective-permute-start | bytes 1794056 | tf_op jit(solution)/shard_map/ppermute | solution.py:26
  67.8 18.2 %collective-permute-done.10.in_3 = bf16[464,1408]{1,0:T(8,128)(2,1)S(1)} collective-permute-done((bf16[464,1408]{1,0:T(8,128)(2,1)S(1)}, bf16[464,1408]{1,0:T(8,128)(2,1)S(1)}, u32[]{:S(2)}, u32[]{:S(2)}) %collective-permute-start.10) | collective-permute-done | bytes 1306656 | tf_op jit(solution)/shard_map/ppermute | solution.py:26
  86.0 2.2 %collective-permute-done.9.in_1 = bf16[464,1408]{1,0:T(8,128)(2,1)S(1)} collective-permute-done((bf16[464,1408]{1,0:T(8,128)(2,1)S(1)}, bf16[464,1408]{1,0:T(8,128)(2,1)S(1)}, u32[]{:S(2)}, u32[]{:S(2)}) %collective-permute-start.9) | collective-permute-done | bytes 1306656 | tf_op jit(solution)/shard_map/ppermute | solution.py:26
  88.1 5.6 %shard_map.34 = (bf16[112,1920]{1,0:T(8,128)(2,1)S(1)}, bf16[112,1920]{1,0:T(8,128)(2,1)S(1)}, bf16[112,1920]{1,0:T(8,128)(2,1)S(1)}, f32[112,1920]{1,0:T(8,128)S(1)}) custom-call(s32[8]{0:T(128)S(1)} %stack.26.at_ref, bf16[512,1792]{1,0:T(8,128)(2,1)} %g_ref.3, bf16[464,1408]{1,0:T(8,128)(2,1)S(1)} %collective-permute-done.9.in_1, ...), custom_call_target="tpu_custom_call" | custom-call | flops 4000000000 | bytes 4448288 | tf_op jit(solution)/shard_map/pallas_call | solution.py:69
  93.7 2.9 %collective-permute-start.11 = (bf16[112,1920]{1,0:T(8,128)(2,1)S(1)}, bf16[112,1920]{1,0:T(8,128)(2,1)S(1)}, u32[]{:S(2)}, u32[]{:S(2)}) collective-permute-start(bf16[112,1920]{1,0:T(8,128)(2,1)S(1)} %get-tuple-element.57), channel_id=1, source_target_pairs={{0,16},{1,17},{2,18},{3,19},{4,20},{5,21},{6,22},{7,23},{8,24},{9,... | collective-permute-start | bytes 1290248 | tf_op jit(solution)/shard_map/ppermute | solution.py:26
  96.6 3.7 %collective-permute-start.13 = (bf16[112,1920]{1,0:T(8,128)(2,1)S(1)}, bf16[112,1920]{1,0:T(8,128)(2,1)S(1)}, u32[]{:S(2)}, u32[]{:S(2)}) collective-permute-start(bf16[112,1920]{1,0:T(8,128)(2,1)S(1)} %get-tuple-element.60), channel_id=1, source_target_pairs={{0,32},{1,33},{2,34},{3,35},{4,36},{5,37},{6,38},{7,39},{8,40},{9,... | collective-permute-start | bytes 1290248 | tf_op jit(solution)/shard_map/ppermute | solution.py:26
  100.3 16.6 %collective-permute-done.11.in_1 = bf16[112,1920]{1,0:T(8,128)(2,1)S(1)} collective-permute-done((bf16[112,1920]{1,0:T(8,128)(2,1)S(1)}, bf16[112,1920]{1,0:T(8,128)(2,1)S(1)}, u32[]{:S(2)}, u32[]{:S(2)}) %collective-permute-start.11) | collective-permute-done | bytes 430112 | tf_op jit(solution)/shard_map/ppermute | solution.py:26
  116.9 20.6 %collective-permute-done.13.in_2 = bf16[112,1920]{1,0:T(8,128)(2,1)S(1)} collective-permute-done((bf16[112,1920]{1,0:T(8,128)(2,1)S(1)}, bf16[112,1920]{1,0:T(8,128)(2,1)S(1)}, u32[]{:S(2)}, u32[]{:S(2)}) %collective-permute-start.13) | collective-permute-done | bytes 430112 | tf_op jit(solution)/shard_map/ppermute | solution.py:26
  137.6 1.8 collective-permute-done.12.in_3
  139.3 2.6 %shard_map.35 = (bf16[400,128]{1,0:T(8,128)(2,1)S(1)}, bf16[400,128]{1,0:T(8,128)(2,1)S(1)}, bf16[400,128]{1,0:T(8,128)(2,1)S(1)}, bf16[400,128]{1,0:T(8,128)(2,...) custom-call(s32[8]{0:T(128)S(1)} %stack.26.at_ref, ...), custom_call_target="tpu_custom_call" | custom-call | flops 4000000000 | bytes 2981920 | tf_op jit(solution)/shard_map/pallas_call | solution.py:69
  142.1 2.7 %collective-permute-start.15 = (bf16[400,128]{1,0:T(8,128)(2,1)S(1)}, bf16[400,128]{1,0:T(8,128)(2,1)S(1)}, u32[]{:S(2)}, u32[]{:S(2)}) collective-permute-start(bf16[400,128]{1,0:T(8,128)(2,1)S(1)} %get-tuple-element.66), channel_id=1, source_target_pairs={{0,50},{1,51},{2,0},{3,1},{4,54},{5,55},{6,4},{7,5},{8,58},{9,59},... | collective-permute-start | bytes 307208 | tf_op jit(solution)/shard_map/ppermute | solution.py:26
  144.8 3.6 %collective-permute-start.17 = (bf16[400,128]{1,0:T(8,128)(2,1)S(1)}, bf16[400,128]{1,0:T(8,128)(2,1)S(1)}, u32[]{:S(2)}, u32[]{:S(2)}) collective-permute-start(bf16[400,128]{1,0:T(8,128)(2,1)S(1)} %get-tuple-element.68), channel_id=1, source_target_pairs={{0,48},{1,49},{2,50},{3,51},{4,52},{5,53},{6,54},{7,55},{8,56},{9,... | collective-permute-start | bytes 307208 | tf_op jit(solution)/shard_map/ppermute | solution.py:26
  148.3 4.5 %collective-permute-start.19 = (bf16[400,128]{1,0:T(8,128)(2,1)S(1)}, bf16[400,128]{1,0:T(8,128)(2,1)S(1)}, u32[]{:S(2)}, u32[]{:S(2)}) collective-permute-start(bf16[400,128]{1,0:T(8,128)(2,1)S(1)} %get-tuple-element.70), channel_id=1, source_target_pairs={{0,34},{1,35},{2,48},{3,49},{4,38},{5,39},{6,52},{7,53},{8,42},{9,... | collective-permute-start | bytes 307208 | tf_op jit(solution)/shard_map/ppermute | solution.py:26
  152.8 2.3 %collective-permute-start.20 = (bf16[400,128]{1,0:T(8,128)(2,1)S(1)}, bf16[400,128]{1,0:T(8,128)(2,1)S(1)}, u32[]{:S(2)}, u32[]{:S(2)}) collective-permute-start(bf16[400,128]{1,0:T(8,128)(2,1)S(1)} %get-tuple-element.71), channel_id=1, source_target_pairs={{0,32},{1,33},{2,34},{3,35},{4,36},{5,37},{6,38},{7,39},{8,40},{9,... | collective-permute-start | bytes 307208 | tf_op jit(solution)/shard_map/ppermute | solution.py:26
  155.2 2.2 %collective-permute-done.18.refs_5_ = bf16[400,128]{1,0:T(8,128)(2,1)S(1)} collective-permute-done((bf16[400,128]{1,0:T(8,128)(2,1)S(1)}, bf16[400,128]{1,0:T(8,128)(2,1)S(1)}, u32[]{:S(2)}, u32[]{:S(2)}) %collective-permute-start.18) | collective-permute-done | bytes 102432 | tf_op jit(solution)/shard_map/ppermute | solution.py:26
  157.3 3.2 %collective-permute-done.20.refs_7_ = bf16[400,128]{1,0:T(8,128)(2,1)S(1)} collective-permute-done((bf16[400,128]{1,0:T(8,128)(2,1)S(1)}, bf16[400,128]{1,0:T(8,128)(2,1)S(1)}, u32[]{:S(2)}, u32[]{:S(2)}) %collective-permute-start.20) | collective-permute-done | bytes 102432 | tf_op jit(solution)/shard_map/ppermute | solution.py:26
  161.9 5.4 %collective-permute-start.21 = (f32[128,128]{1,0:T(8,128)S(1)}, f32[128,128]{1,0:T(8,128)S(1)}, u32[]{:S(2)}, u32[]{:S(2)}) collective-permute-start(f32[128,128]{1,0:T(8,128)S(1)} %get-tuple-element.74), channel_id=1, source_target_pairs={{0,1},{1,2},{2,3},{3,0},{4,16},{5,17},{6,18},{7,19},{8,32},{9,33},... | collective-permute-start | bytes 196616 | tf_op jit(solution)/shard_map/ppermute | solution.py:26
  167.4 8.2 %collective-permute-start.22 = (f32[128,128]{1,0:T(8,128)S(1)}, f32[128,128]{1,0:T(8,128)S(1)}, u32[]{:S(2)}, u32[]{:S(2)}) collective-permute-start(f32[128,128]{1,0:T(8,128)S(1)} %get-tuple-element.75), channel_id=1, source_target_pairs={{0,0},{1,1},{2,2},{3,3},{4,18},{5,19},{6,16},{7,17},{8,34},{9,35},... | collective-permute-start | bytes 196616 | tf_op jit(solution)/shard_map/ppermute | solution.py:26
  175.6 2.5 %shard_map.38 = (f32[112,1408]{1,0:T(8,128)S(1)}, f32[112,384]{1,0:T(8,128)S(1)}) custom-call(s32[8]{0:T(128)S(1)} %stack.26.at_ref, f32[112,1920]{1,0:T(8,128)S(1)} %get-tuple-element.76.own_ref, bf16[112,1920]{1,0:T(8,128)(2,1)S(1)} %collective-permute-done.11.in_1, bf16[112,1920]{1,0:T(8,128)(2,1)S(1)} %collective-permute-done.12.in_3, ...), custom_call_target="tpu_custom_call" | custom-call | flops 4000000000 | bytes 2150432 | tf_op jit(solution)/shard_map/pallas_call | solution.py:69
  178.2 2.0 %collective-permute-done.22.other_ref = f32[128,128]{1,0:T(8,128)S(1)} collective-permute-done((f32[128,128]{1,0:T(8,128)S(1)}, f32[128,128]{1,0:T(8,128)S(1)}, u32[]{:S(2)}, u32[]{:S(2)}) %collective-permute-start.22) | collective-permute-done | bytes 65568 | tf_op jit(solution)/shard_map/ppermute | solution.py:26
  181.5 4.3 %collective-permute-done.23.image_ref = f32[112,384]{1,0:T(8,128)S(1)} collective-permute-done((f32[112,384]{1,0:T(8,128)S(1)}, f32[112,384]{1,0:T(8,128)S(1)}, u32[]{:S(2)}, u32[]{:S(2)}) %collective-permute-start.23) | collective-permute-done | bytes 172064 | tf_op jit(solution)/shard_map/ppermute | solution.py:26
  185.8 1.5 shard_map.39
  (34 shorter events, 9.0 us)
Async XLA Ops:
  0.7 2.8 %copy-start = (bf16[512,1792]{1,0:T(8,128)(2,1)S(1)}, bf16[512,1792]{1,0:T(8,128)(2,1)}, u32[]{:S(2)}) copy-start(bf16[512,1792]{1,0:T(8,128)(2,1)} %g_ref.3) | copy-start | bytes 5505028
  3.5 4.7 %copy-start.2 = (bf16[512,896]{1,0:T(8,128)(2,1)S(1)}, bf16[512,896]{1,0:T(8,128)(2,1)}, u32[]{:S(2)}) copy-start(bf16[512,896]{1,0:T(8,128)(2,1)} %get-tuple-element.43) | copy-start | bytes 2752516
  5.4 17.3 %collective-permute-start.2 = (bf16[240,1408]{1,0:T(8,128)(2,1)S(1)}, bf16[240,1408]{1,0:T(8,128)(2,1)S(1)}, u32[]{:S(2)}, u32[]{:S(2)}) collective-permute-start(bf16[240,1408]{1,0:T(8,128)(2,1)S(1)} %get-tuple-element.46), channel_id=1, source_target_pairs={{0,64},{1,65},{2,66},{3,67},{4,68},{5,69},{6,70},{7,71},{8,72},{9,... | collective-permute-start | bytes 2027528 | tf_op jit(solution)/shard_map/ppermute | solution.py:26
  6.7 18.5 %collective-permute-start.3 = (bf16[240,1408]{1,0:T(8,128)(2,1)S(1)}, bf16[240,1408]{1,0:T(8,128)(2,1)S(1)}, u32[]{:S(2)}, u32[]{:S(2)}) collective-permute-start(bf16[240,1408]{1,0:T(8,128)(2,1)S(1)} %get-tuple-element.47), channel_id=1, source_target_pairs={{0,192},{1,193},{2,194},{3,195},{4,196},{5,197},{6,198},{7,199},{8... | collective-permute-start | bytes 2027528 | tf_op jit(solution)/shard_map/ppermute | solution.py:26
  8.2 47.0 %collective-permute-start = (bf16[512,896]{1,0:T(8,128)(2,1)S(1)}, bf16[512,896]{1,0:T(8,128)(2,1)S(1)}, u32[]{:S(2)}, u32[]{:S(2)}) collective-permute-start(bf16[512,896]{1,0:T(8,128)(2,1)S(1)} %copy-done.2), channel_id=1, source_target_pairs={{0,16},{1,48},{2,18},{3,50},{4,20},{5,52},{6,22},{7,54},{8,24},{9,... | collective-permute-start | bytes 2752520 | tf_op jit(solution)/shard_map/ppermute | solution.py:26
  15.3 39.8 %collective-permute-start.1 = (bf16[512,896]{1,0:T(8,128)(2,1)S(1)}, bf16[512,896]{1,0:T(8,128)(2,1)S(1)}, u32[]{:S(2)}, u32[]{:S(2)}) collective-permute-start(bf16[512,896]{1,0:T(8,128)(2,1)S(1)} %get-tuple-element.44), channel_id=1, source_target_pairs={{0,0},{1,32},{2,2},{3,34},{4,4},{5,36},{6,6},{7,38},{8,8},{9,40},{... | collective-permute-start | bytes 2752520 | tf_op jit(solution)/shard_map/ppermute | solution.py:26
  55.2 2.5 %collective-permute-start.4 = (bf16[512,896]{1,0:T(8,128)(2,1)S(1)}, bf16[512,896]{1,0:T(8,128)(2,1)S(1)}, u32[]{:S(2)}, u32[]{:S(2)}) collective-permute-start(bf16[512,896]{1,0:T(8,128)(2,1)S(1)} %collective-permute-done.1.far), channel_id=1, source_target_pairs={{0,1},{1,0},{2,3},{3,2},{4,5},{5,4},{6,7},{7,6},{8,9},{9,8},{10,11... | collective-permute-start | bytes 2752520 | tf_op jit(solution)/shard_map/ppermute | solution.py:26
  55.2 3.8 %collective-permute-start.5 = (bf16[512,896]{1,0:T(8,128)(2,1)S(1)}, bf16[512,896]{1,0:T(8,128)(2,1)S(1)}, u32[]{:S(2)}, u32[]{:S(2)}) collective-permute-start(bf16[512,896]{1,0:T(8,128)(2,1)S(1)} %collective-permute-done.near), channel_id=1, source_target_pairs={{0,1},{1,0},{2,3},{3,2},{4,5},{5,4},{6,7},{7,6},{8,9},{9,8},{10,11... | collective-permute-start | bytes 2752520 | tf_op jit(solution)/shard_map/ppermute | solution.py:26
  55.7 30.3 %collective-permute-start.10 = (bf16[464,1408]{1,0:T(8,128)(2,1)S(1)}, bf16[464,1408]{1,0:T(8,128)(2,1)S(1)}, u32[]{:S(2)}, u32[]{:S(2)}) collective-permute-start(bf16[464,1408]{1,0:T(8,128)(2,1)S(1)} %shard_map.32), channel_id=1, source_target_pairs={{0,192},{1,193},{2,194},{3,195},{4,196},{5,197},{6,198},{7,199},{8... | collective-permute-start | bytes 3919880 | tf_op jit(solution)/shard_map/ppermute | solution.py:26
  56.9 31.2 %collective-permute-start.9 = (bf16[464,1408]{1,0:T(8,128)(2,1)S(1)}, bf16[464,1408]{1,0:T(8,128)(2,1)S(1)}, u32[]{:S(2)}, u32[]{:S(2)}) collective-permute-start(bf16[464,1408]{1,0:T(8,128)(2,1)S(1)} %shard_map.31), channel_id=1, source_target_pairs={{0,64},{1,65},{2,66},{3,67},{4,68},{5,69},{6,70},{7,71},{8,72},{9,... | collective-permute-start | bytes 3919880 | tf_op jit(solution)/shard_map/ppermute | solution.py:26
  64.8 35.5 %collective-permute-start.7 = (bf16[1168,256]{1,0:T(8,128)(2,1)S(1)}, bf16[1168,256]{1,0:T(8,128)(2,1)S(1)}, u32[]{:S(2)}, u32[]{:S(2)}) collective-permute-start(bf16[1168,256]{1,0:T(8,128)(2,1)S(1)} %get-tuple-element.53), channel_id=1, source_target_pairs={{0,12},{1,13},{2,14},{3,15},{4,0},{5,1},{6,2},{7,3},{8,4},{9,5},{1... | collective-permute-start | bytes 1794056 | tf_op jit(solution)/shard_map/ppermute | solution.py:26
  65.3 72.3 %collective-permute-start.8 = (bf16[1168,256]{1,0:T(8,128)(2,1)S(1)}, bf16[1168,256]{1,0:T(8,128)(2,1)S(1)}, u32[]{:S(2)}, u32[]{:S(2)}) collective-permute-start(bf16[1168,256]{1,0:T(8,128)(2,1)S(1)} %get-tuple-element.54), channel_id=1, source_target_pairs={{0,8},{1,9},{2,10},{3,11},{4,12},{5,13},{6,14},{7,15},{8,0},{9,1},... | collective-permute-start | bytes 1794056 | tf_op jit(solution)/shard_map/ppermute | solution.py:26
  65.8 73.6 %copy-start.1 = (f32[1152,256]{1,0:T(8,128)S(1)}, f32[1152,256]{1,0:T(8,128)}, u32[]{:S(2)}) copy-start(f32[1152,256]{1,0:T(8,128)} %get-tuple-element.50.own_ref) | copy-start | bytes 3538948
  65.8 71.8 %collective-permute-start.6 = (bf16[1168,256]{1,0:T(8,128)(2,1)S(1)}, bf16[1168,256]{1,0:T(8,128)(2,1)S(1)}, u32[]{:S(2)}, u32[]{:S(2)}) collective-permute-start(bf16[1168,256]{1,0:T(8,128)(2,1)S(1)} %get-tuple-element.52), channel_id=1, source_target_pairs={{0,4},{1,5},{2,6},{3,7},{4,8},{5,9},{6,10},{7,11},{8,12},{9,13},{1... | collective-permute-start | bytes 1794056 | tf_op jit(solution)/shard_map/ppermute | solution.py:26
  93.7 23.2 %collective-permute-start.11 = (bf16[112,1920]{1,0:T(8,128)(2,1)S(1)}, bf16[112,1920]{1,0:T(8,128)(2,1)S(1)}, u32[]{:S(2)}, u32[]{:S(2)}) collective-permute-start(bf16[112,1920]{1,0:T(8,128)(2,1)S(1)} %get-tuple-element.57), channel_id=1, source_target_pairs={{0,16},{1,17},{2,18},{3,19},{4,20},{5,21},{6,22},{7,23},{8,24},{9,... | collective-permute-start | bytes 1290248 | tf_op jit(solution)/shard_map/ppermute | solution.py:26
  96.6 41.0 %collective-permute-start.13 = (bf16[112,1920]{1,0:T(8,128)(2,1)S(1)}, bf16[112,1920]{1,0:T(8,128)(2,1)S(1)}, u32[]{:S(2)}, u32[]{:S(2)}) collective-permute-start(bf16[112,1920]{1,0:T(8,128)(2,1)S(1)} %get-tuple-element.60), channel_id=1, source_target_pairs={{0,32},{1,33},{2,34},{3,35},{4,36},{5,37},{6,38},{7,39},{8,40},{9,... | collective-permute-start | bytes 1290248 | tf_op jit(solution)/shard_map/ppermute | solution.py:26
  100.3 39.1 %collective-permute-start.12 = (bf16[112,1920]{1,0:T(8,128)(2,1)S(1)}, bf16[112,1920]{1,0:T(8,128)(2,1)S(1)}, u32[]{:S(2)}, u32[]{:S(2)}) collective-permute-start(bf16[112,1920]{1,0:T(8,128)(2,1)S(1)} %get-tuple-element.59), channel_id=1, source_target_pairs={{0,48},{1,49},{2,50},{3,51},{4,52},{5,53},{6,54},{7,55},{8,56},{9,... | collective-permute-start | bytes 1290248 | tf_op jit(solution)/shard_map/ppermute | solution.py:26
  142.0 6.3 %collective-permute-start.14 = (bf16[400,128]{1,0:T(8,128)(2,1)S(1)}, bf16[400,128]{1,0:T(8,128)(2,1)S(1)}, u32[]{:S(2)}, u32[]{:S(2)}) collective-permute-start(bf16[400,128]{1,0:T(8,128)(2,1)S(1)} %get-tuple-element.65), channel_id=1, source_target_pairs={{0,2},{1,3},{2,16},{3,17},{4,6},{5,7},{6,20},{7,21},{8,10},{9,11},... | collective-permute-start | bytes 307208 | tf_op jit(solution)/shard_map/ppermute | solution.py:26
  142.1 10.7 %collective-permute-start.15 = (bf16[400,128]{1,0:T(8,128)(2,1)S(1)}, bf16[400,128]{1,0:T(8,128)(2,1)S(1)}, u32[]{:S(2)}, u32[]{:S(2)}) collective-permute-start(bf16[400,128]{1,0:T(8,128)(2,1)S(1)} %get-tuple-element.66), channel_id=1, source_target_pairs={{0,50},{1,51},{2,0},{3,1},{4,54},{5,55},{6,4},{7,5},{8,58},{9,59},... | collective-permute-start | bytes 307208 | tf_op jit(solution)/shard_map/ppermute | solution.py:26
  144.8 10.4 %collective-permute-start.16 = (bf16[400,128]{1,0:T(8,128)(2,1)S(1)}, bf16[400,128]{1,0:T(8,128)(2,1)S(1)}, u32[]{:S(2)}, u32[]{:S(2)}) collective-permute-start(bf16[400,128]{1,0:T(8,128)(2,1)S(1)} %get-tuple-element.67), channel_id=1, source_target_pairs={{0,16},{1,17},{2,18},{3,19},{4,20},{5,21},{6,22},{7,23},{8,24},{9,... | collective-permute-start | bytes 307208 | tf_op jit(solution)/shard_map/ppermute | solution.py:26
  144.8 10.4 %collective-permute-start.17 = (bf16[400,128]{1,0:T(8,128)(2,1)S(1)}, bf16[400,128]{1,0:T(8,128)(2,1)S(1)}, u32[]{:S(2)}, u32[]{:S(2)}) collective-permute-start(bf16[400,128]{1,0:T(8,128)(2,1)S(1)} %get-tuple-element.68), channel_id=1, source_target_pairs={{0,48},{1,49},{2,50},{3,51},{4,52},{5,53},{6,54},{7,55},{8,56},{9,... | collective-permute-start | bytes 307208 | tf_op jit(solution)/shard_map/ppermute | solution.py:26
  148.3 9.0 %collective-permute-start.18 = (bf16[400,128]{1,0:T(8,128)(2,1)S(1)}, bf16[400,128]{1,0:T(8,128)(2,1)S(1)}, u32[]{:S(2)}, u32[]{:S(2)}) collective-permute-start(bf16[400,128]{1,0:T(8,128)(2,1)S(1)} %get-tuple-element.69), channel_id=1, source_target_pairs={{0,18},{1,19},{2,32},{3,33},{4,22},{5,23},{6,36},{7,37},{8,26},{9,... | collective-permute-start | bytes 307208 | tf_op jit(solution)/shard_map/ppermute | solution.py:26
  148.3 9.0 %collective-permute-start.19 = (bf16[400,128]{1,0:T(8,128)(2,1)S(1)}, bf16[400,128]{1,0:T(8,128)(2,1)S(1)}, u32[]{:S(2)}, u32[]{:S(2)}) collective-permute-start(bf16[400,128]{1,0:T(8,128)(2,1)S(1)} %get-tuple-element.70), channel_id=1, source_target_pairs={{0,34},{1,35},{2,48},{3,49},{4,38},{5,39},{6,52},{7,53},{8,42},{9,... | collective-permute-start | bytes 307208 | tf_op jit(solution)/shard_map/ppermute | solution.py:26
  152.8 7.7 %collective-permute-start.20 = (bf16[400,128]{1,0:T(8,128)(2,1)S(1)}, bf16[400,128]{1,0:T(8,128)(2,1)S(1)}, u32[]{:S(2)}, u32[]{:S(2)}) collective-permute-start(bf16[400,128]{1,0:T(8,128)(2,1)S(1)} %get-tuple-element.71), channel_id=1, source_target_pairs={{0,32},{1,33},{2,34},{3,35},{4,36},{5,37},{6,38},{7,39},{8,40},{9,... | collective-permute-start | bytes 307208 | tf_op jit(solution)/shard_map/ppermute | solution.py:26
  161.9 16.3 %collective-permute-start.21 = (f32[128,128]{1,0:T(8,128)S(1)}, f32[128,128]{1,0:T(8,128)S(1)}, u32[]{:S(2)}, u32[]{:S(2)}) collective-permute-start(f32[128,128]{1,0:T(8,128)S(1)} %get-tuple-element.74), channel_id=1, source_target_pairs={{0,1},{1,2},{2,3},{3,0},{4,16},{5,17},{6,18},{7,19},{8,32},{9,33},... | collective-permute-start | bytes 196616 | tf_op jit(solution)/shard_map/ppermute | solution.py:26
  167.4 12.8 %collective-permute-start.22 = (f32[128,128]{1,0:T(8,128)S(1)}, f32[128,128]{1,0:T(8,128)S(1)}, u32[]{:S(2)}, u32[]{:S(2)}) collective-permute-start(f32[128,128]{1,0:T(8,128)S(1)} %get-tuple-element.75), channel_id=1, source_target_pairs={{0,0},{1,1},{2,2},{3,3},{4,18},{5,19},{6,16},{7,17},{8,34},{9,35},... | collective-permute-start | bytes 196616 | tf_op jit(solution)/shard_map/ppermute | solution.py:26
  178.1 7.6 %collective-permute-start.23 = (f32[112,384]{1,0:T(8,128)S(1)}, f32[112,384]{1,0:T(8,128)S(1)}, u32[]{:S(2)}, u32[]{:S(2)}) collective-permute-start(f32[112,384]{1,0:T(8,128)S(1)} %get-tuple-element.83), channel_id=1, source_target_pairs={{0,64},{1,65},{2,66},{3,67},{4,68},{5,69},{6,70},{7,71},{8,72},{9,... | collective-permute-start | bytes 516104 | tf_op jit(solution)/shard_map/ppermute | solution.py:26
where the time goes:
time: 190 us; the launch traced here: 187 us
  waiting for transfers between devices  105 us (55%)
  starting transfers between devices  51.1 us (27%)
  Pallas kernels  27.8 us (15%)
  local copies, waits for them, and re-layouts  2.77 us (1%)
    ppermute x24, waiting for transfers between devices, send(): lax.ppermute(array, ('row', 'col'), [(number(p), number(to(*p))) for p in...  105 us
    ppermute x24, starting transfers between devices, send(): lax.ppermute(array, ('row', 'col'), [(number(p), number(to(*p))) for p in...  51.1 us
    pallas_call x10, Pallas kernels, run(): pl.pallas_call(body, out_shape=[jax.ShapeDtypeStruct(shape, dtype) for sh...  27.8 us
  transfers between devices with their start and end apart: 24, of which 13 were waited for; matrix products, arithmetic and copies ran while one was open for 0% of the time, Pallas kernels for 11%

commit v1 on v0

--- a/solution.py
+++ b/solution.py
@@ -397,22 +397,39 @@
     cut = lambda parity: lax.dynamic_slice_in_dim(gradient, parity * half, half, 1)
     near, far, gradient = barrier((cut((zh + 1) % 2), cut(zh % 2), gradient))
     near = send(near, lambda x, zh, y, zl, core: (x, 2 * core + (zh + 1) % 2, y, zl, zh // 2))
-    far = send(far, lambda x, zh, y, zl, core: (x, 2 * core + zh % 2, y, zl, zh // 2))
 
     window = [((rows, WINDOW), BF16), ((512, 512), BF16), ((512, 128), F32)]
     half_part, whole_part = ((HALF_ROWS + 16, WINDOW), BF16), ((BLOCK + 16, WINDOW), BF16)
     over_x = lambda s, v: send(v, lambda x, zh, y, zl, core: (x + s, zh, y, zl, core))
     far_1, far_3 = run(right_far, [half_part] * 2, window, FLOPS, at, gradient)
     far_1, far_3 = over_x(1, far_1), over_x(3, far_3)
+    near, far, far_1, far_3 = barrier((near, far, far_1, far_3))
+    far = send(far, lambda x, zh, y, zl, core: (x, 2 * core + zh % 2, y, zl, zh // 2))
     add = lambda s, v: run(
         functools.partial(right_near, s), [whole_part], window + [((BLOCK, 256), F32)], FLOPS, at, gradient, v
     )[0]
     code_1, code_3 = add(1, far_1), add(3, far_3)
     right_1, right_3 = over_x(1, code_1), over_x(3, code_3)
-    near, far, _ = barrier((near, far, (code_1, code_3)))
+    near, far, right_1, right_3 = barrier((near, far, right_1, right_3))
 
     swap = lambda x, zh, y, zl, core: (x, zh, y, zl, 1 - core)
     far_2, near_2 = send(far, swap), send(near, swap)
+
+    piece = (CHUNK, WIDTH + 128)
+    code_1, code_3, code_2, right_own = run(
+        right_second,
+        [(piece, BF16)] * 3 + [(piece, F32)],
+        window + [((512, WINDOW), F32), ((640, 512), F32)],
+        FLOPS,
+        at,
+        gradient,
+        right_1,
+        right_3,
+    )
+    over_z = lambda s, v: send(v, lambda x, zh, y, zl, core: (x, zh + s, y, zl, core))
+    right_2 = over_z(2, code_2)
+
+    far, near, far_2, near_2, _ = barrier((far, near, far_2, near_2, code_1))
     packed = (ROWS + 16, 256)
     left_1, left_3, left_2, left_own, norms = run(
         left_first,
@@ -425,28 +442,11 @@
         far_2,
         near_2,
     )
-    right_1, right_3, _ = barrier((right_1, right_3, left_1))
     over_y = lambda s, v: send(v, lambda x, zh, y, zl, core: (x, zh, y + s, zl, core))
-    left_1, left_3, left_2 = over_y(1, left_1), over_y(3, left_3), over_y(2, left_2)
-
-    piece = (CHUNK, WIDTH + 128)
-    code_1, code_3, code_2, right_own = run(
-        right_second,
-        [(piece, BF16)] * 3 + [(piece, F32)],
-        window + [((512, WINDOW), F32), ((640, 512), F32)],
-        FLOPS,
-        at,
-        gradient,
-        right_1,
-        right_3,
-    )
-    over_z = lambda s, v: send(v, lambda x, zh, y, zl, core: (x, zh + s, y, zl, core))
-    right_2, right_1 = over_z(2, code_2), over_z(1, code_1)
-    code_3, _ = barrier((code_3, left_3))
-    right_3 = over_z(3, code_3)
-    left_1, left_3, left_2, right_1, right_3, right_2 = barrier(
-        (left_1, left_3, left_2, right_1, right_3, right_2)
-    )
+    left_1, left_3 = over_y(1, left_1), over_y(3, left_3)
+    left_1, left_3, left_2, right_2, code_1, code_3 = barrier((left_1, left_3, left_2, right_2, code_1, code_3))
+    left_2, right_1, right_3 = over_y(2, left_2), over_z(1, code_1), over_z(3, code_3)
+    left_2, right_1, right_3 = barrier((left_2, right_1, right_3))
 
     piece = (400, SUB)
     codes = run(
@@ -461,8 +461,8 @@
         left_3,
         left_2,
     )
-    right_1, right_3, _ = barrier((right_1, right_3, codes))
     arrived = [send(code, along_z(s)) for s, code in zip(Z_STEPS, codes)]
+    right_1, right_3, _ = barrier((right_1, right_3, arrived[0]))
 
     right_base, image = run(
         functools.partial(right_third, 1.0 / (rows * 16)),
@@ -478,6 +478,7 @@
     image = over_x(1, image)
     right_gram = run(right_last, [((CHUNK, width), F32)], [], FLOPS, at, right_base, image)[0]
 
+    arrived, right_gram = barrier((arrived, right_gram))
     square = ((SUB, SUB), F32)
     base, more, same, other = run(
         functools.partial(left_third, 1.0 / (width * 16)),

time: 190 us -> 185 us (0.974)
  the two profiles are of different devices: /device:TPU:25 before, /device:TPU:20 now
where the time goes in v1:
time: 185 us
  waiting for transfers between devices  94.3 us (51%)
  starting transfers between devices  57.3 us (31%)
  Pallas kernels  27.7 us (15%)
  local copies, waits for them, and re-layouts  4.37 us (2%)
    ppermute x24, waiting for transfers between devices, send(): lax.ppermute(array, ('row', 'col'), [(number(p), number(to(*p))) for p in...  94.3 us
    ppermute x24, starting transfers between devices, send(): lax.ppermute(array, ('row', 'col'), [(number(p), number(to(*p))) for p in...  57.3 us
    pallas_call x10, Pallas kernels, run(): pl.pallas_call(body, out_shape=[jax.ShapeDtypeStruct(shape, dtype) for sh...  27.7 us
  transfers between devices with their start and end apart: 24, of which 14 were waited for; matrix products, arithmetic and copies ran while one was open for 0% of the time, Pallas kernels for 5%

profile of v1, /device:TPU:20, one launch (start us, length us, event | category | flops | bytes accessed | tf_op | source)
XLA Modules:
  0.0 184.5 jit_solution(9463585670962669473)
XLA Ops:
  0.7 3.0 %constant_dynamic-slice_fusion = (bf16[512,896]{1,0:T(8,128)(2,1)}, bf16[512,896]{1,0:T(8,128)(2,1)}) fusion(bf16[512,1792]{1,0:T(8,128)(2,1)} %g_ref.3, s32[]{:T(128)S(6)} %select_n.48, s32[]{:T(128)S(6)} %select_n.46), kind=kLoop, calls=%fused_computation | loop fusion | bytes 3670024 | tf_op jit(solution)/shard_map/dynamic_slice | solution.py:397
  3.7 3.3 %collective-permute-start = (bf16[512,896]{1,0:T(8,128)(2,1)}, bf16[512,896]{1,0:T(8,128)(2,1)S(1)}, u32[]{:S(2)}, u32[]{:S(2)}) collective-permute-start(bf16[512,896]{1,0:T(8,128)(2,1)} %get-tuple-element.61), channel_id=1, source_target_pairs={{0,16},{1,48},{2,18},{3,50},{4,20},{5,52},{6,22},{7,54},{8,24},{9,... | collective-permute-start | bytes 2752520 | tf_op jit(solution)/shard_map/ppermute | solution.py:26
  7.1 1.9 %shard_map.30 = (bf16[240,1408]{1,0:T(8,128)(2,1)S(1)}, bf16[240,1408]{1,0:T(8,128)(2,1)S(1)}) custom-call(s32[8]{0:T(128)S(1)} %stack.26.at_ref, bf16[512,1792]{1,0:T(8,128)(2,1)S(1)} %copy-done), custom_call_target="tpu_custom_call" | custom-call | flops 4000000000 | bytes 1835040 | tf_op jit(solution)/shard_map/pallas_call | solution.py:69
  11.1 13.8 %collective-permute-done.1.in_ref = bf16[240,1408]{1,0:T(8,128)(2,1)S(1)} collective-permute-done((bf16[240,1408]{1,0:T(8,128)(2,1)S(1)}, bf16[240,1408]{1,0:T(8,128)(2,1)S(1)}, u32[]{:S(2)}, u32[]{:S(2)}) %collective-permute-start.1) | collective-permute-done | bytes 675872 | tf_op jit(solution)/shard_map/ppermute | solution.py:26
  24.8 1.5 collective-permute-done.2.in_ref
  26.3 2.2 %collective-permute-done.near = bf16[512,896]{1,0:T(8,128)(2,1)S(1)} collective-permute-done((bf16[512,896]{1,0:T(8,128)(2,1)}, bf16[512,896]{1,0:T(8,128)(2,1)S(1)}, u32[]{:S(2)}, u32[]{:S(2)}) %collective-permute-start) | collective-permute-done | bytes 917536 | tf_op jit(solution)/shard_map/ppermute | solution.py:26
  28.5 2.5 %shard_map.31 = bf16[464,1408]{1,0:T(8,128)(2,1)S(1)} custom-call(s32[8]{0:T(128)S(1)} %stack.26.at_ref, bf16[512,1792]{1,0:T(8,128)(2,1)S(1)} %copy-done, bf16[240,1408]{1,0:T(8,128)(2,1)S(1)} %collective-permute-done.1.in_ref), custom_call_target="tpu_custom_call" | custom-call | flops 4000000000 | bytes 2510880 | tf_op jit(solution)/shard_map/pallas_call | solution.py:69
  31.0 2.6 %shard_map.32 = bf16[464,1408]{1,0:T(8,128)(2,1)S(1)} custom-call(s32[8]{0:T(128)S(1)} %stack.26.at_ref, bf16[512,1792]{1,0:T(8,128)(2,1)S(1)} %copy-done, bf16[240,1408]{1,0:T(8,128)(2,1)S(1)} %collective-permute-done.2.in_ref), custom_call_target="tpu_custom_call" | custom-call | flops 4000000000 | bytes 2510880 | tf_op jit(solution)/shard_map/pallas_call | solution.py:69
  34.2 1.5 collective-permute-start.4
  36.4 27.6 %collective-permute-done.5.in_3 = bf16[464,1408]{1,0:T(8,128)(2,1)S(1)} collective-permute-done((bf16[464,1408]{1,0:T(8,128)(2,1)S(1)}, bf16[464,1408]{1,0:T(8,128)(2,1)S(1)}, u32[]{:S(2)}, u32[]{:S(2)}) %collective-permute-start.5) | collective-permute-done | bytes 1306656 | tf_op jit(solution)/shard_map/ppermute | solution.py:26
  65.6 5.5 %shard_map.33 = (bf16[112,1920]{1,0:T(8,128)(2,1)S(1)}, bf16[112,1920]{1,0:T(8,128)(2,1)S(1)}, bf16[112,1920]{1,0:T(8,128)(2,1)S(1)}, f32[112,1920]{1,0:T(8,128)S(1)}) custom-call(s32[8]{0:T(128)S(1)} %stack.26.at_ref, bf16[512,1792]{1,0:T(8,128)(2,1)} %g_ref.3, bf16[464,1408]{1,0:T(8,128)(2,1)S(1)} %collective-permute-done.4.in_1, ...), custom_call_target="tpu_custom_call" | custom-call | flops 4000000000 | bytes 4448288 | tf_op jit(solution)/shard_map/pallas_call | solution.py:69
  71.1 5.9 %shard_map.34 = (bf16[1168,256]{1,0:T(8,128)(2,1)S(1)}, bf16[1168,256]{1,0:T(8,128)(2,1)S(1)}, bf16[1168,256]{1,0:T(8,128)(2,1)S(1)}, f32[1152,256]{1,0:T(8,128)}, f32[16,128]{1,0:T(8,128)S(1)}) custom-call(s32[8]{0:T(128)S(1)} %stack.26.at_ref, bf16[512,896]{1,0:T(8,128)(2,1)S(1)} %collective-permute-done.3.far, ...), custom_call_target="tpu_custom_call" | custom-call | flops 4000000000 | bytes 3670048 | tf_op jit(solution)/shard_map/pallas_call | solution.py:69
  79.0 5.2 %collective-permute-start.10 = (bf16[112,1920]{1,0:T(8,128)(2,1)S(1)}, bf16[112,1920]{1,0:T(8,128)(2,1)S(1)}, u32[]{:S(2)}, u32[]{:S(2)}) collective-permute-start(bf16[112,1920]{1,0:T(8,128)(2,1)S(1)} %get-tuple-element.84), channel_id=1, source_target_pairs={{0,32},{1,33},{2,34},{3,35},{4,36},{5,37},{6,38},{7,39},{8,40},{9,... | collective-permute-start | bytes 1290248 | tf_op jit(solution)/shard_map/ppermute | solution.py:26
  84.2 10.7 %collective-permute-done.10.in_2 = bf16[112,1920]{1,0:T(8,128)(2,1)S(1)} collective-permute-done((bf16[112,1920]{1,0:T(8,128)(2,1)S(1)}, bf16[112,1920]{1,0:T(8,128)(2,1)S(1)}, u32[]{:S(2)}, u32[]{:S(2)}) %collective-permute-start.10) | collective-permute-done | bytes 430112 | tf_op jit(solution)/shard_map/ppermute | solution.py:26
  94.9 1.6 collective-permute-start.11
  96.5 11.3 %collective-permute-start.12 = (bf16[112,1920]{1,0:T(8,128)(2,1)S(1)}, bf16[112,1920]{1,0:T(8,128)(2,1)S(1)}, u32[]{:S(2)}, u32[]{:S(2)}) collective-permute-start(bf16[112,1920]{1,0:T(8,128)(2,1)S(1)} %get-tuple-element.89), channel_id=1, source_target_pairs={{0,16},{1,17},{2,18},{3,19},{4,20},{5,21},{6,22},{7,23},{8,24},{9,... | collective-permute-start | bytes 1290248 | tf_op jit(solution)/shard_map/ppermute | solution.py:26
  107.8 2.4 %collective-permute-start.13 = (bf16[112,1920]{1,0:T(8,128)(2,1)S(1)}, bf16[112,1920]{1,0:T(8,128)(2,1)S(1)}, u32[]{:S(2)}, u32[]{:S(2)}) collective-permute-start(bf16[112,1920]{1,0:T(8,128)(2,1)S(1)} %get-tuple-element.90), channel_id=1, source_target_pairs={{0,48},{1,49},{2,50},{3,51},{4,52},{5,53},{6,54},{7,55},{8,56},{9,... | collective-permute-start | bytes 1290248 | tf_op jit(solution)/shard_map/ppermute | solution.py:26
  110.2 17.6 %collective-permute-done.12.in_1 = bf16[112,1920]{1,0:T(8,128)(2,1)S(1)} collective-permute-done((bf16[112,1920]{1,0:T(8,128)(2,1)S(1)}, bf16[112,1920]{1,0:T(8,128)(2,1)S(1)}, u32[]{:S(2)}, u32[]{:S(2)}) %collective-permute-start.12) | collective-permute-done | bytes 430112 | tf_op jit(solution)/shard_map/ppermute | solution.py:26
  130.3 2.7 %shard_map.35 = (bf16[400,128]{1,0:T(8,128)(2,1)S(1)}, bf16[400,128]{1,0:T(8,128)(2,1)S(1)}, bf16[400,128]{1,0:T(8,128)(2,1)S(1)}, bf16[400,128]{1,0:T(8,128)(2,...) custom-call(s32[8]{0:T(128)S(1)} %stack.26.at_ref, ...), custom_call_target="tpu_custom_call" | custom-call | flops 4000000000 | bytes 2981920 | tf_op jit(solution)/shard_map/pallas_call | solution.py:69
  133.1 6.0 %collective-permute-done.14.refs_1_ = bf16[400,128]{1,0:T(8,128)(2,1)S(1)} collective-permute-done((bf16[400,128]{1,0:T(8,128)(2,1)S(1)}, bf16[400,128]{1,0:T(8,128)(2,1)S(1)}, u32[]{:S(2)}, u32[]{:S(2)}) %collective-permute-start.14) | collective-permute-done | bytes 102432 | tf_op jit(solution)/shard_map/ppermute | solution.py:26
  139.1 2.5 %shard_map.36 = (f32[112,1408]{1,0:T(8,128)S(1)}, f32[112,384]{1,0:T(8,128)S(1)}) custom-call(s32[8]{0:T(128)S(1)} %stack.26.at_ref, f32[112,1920]{1,0:T(8,128)S(1)} %get-tuple-element.100.own_ref, bf16[112,1920]{1,0:T(8,128)(2,1)S(1)} %collective-permute-done.12.in_1, bf16[112,1920]{1,0:T(8,128)(2,1)S(1)} %collective-permute-done.13.in_3, ...), custom_call_target="tpu_custom_call" | custom-call | flops 4000000000 | bytes 2150432 | tf_op jit(solution)/shard_map/pallas_call | solution.py:69
  141.6 2.1 %collective-permute-start.21 = (f32[112,384]{1,0:T(8,128)S(1)}, f32[112,384]{1,0:T(8,128)S(1)}, u32[]{:S(2)}, u32[]{:S(2)}) collective-permute-start(f32[112,384]{1,0:T(8,128)S(1)} %get-tuple-element.107), channel_id=1, source_target_pairs={{0,64},{1,65},{2,66},{3,67},{4,68},{5,69},{6,70},{7,71},{8,72},{9,... | collective-permute-start | bytes 516104 | tf_op jit(solution)/shard_map/ppermute | solution.py:26
  143.7 1.6 collective-permute-start.15
  145.2 4.1 %collective-permute-start.17 = (bf16[400,128]{1,0:T(8,128)(2,1)S(1)}, bf16[400,128]{1,0:T(8,128)(2,1)S(1)}, u32[]{:S(2)}, u32[]{:S(2)}) collective-permute-start(bf16[400,128]{1,0:T(8,128)(2,1)S(1)} %get-tuple-element.96), channel_id=1, source_target_pairs={{0,48},{1,49},{2,50},{3,51},{4,52},{5,53},{6,54},{7,55},{8,56},{9,... | collective-permute-start | bytes 307208 | tf_op jit(solution)/shard_map/ppermute | solution.py:26
  150.0 4.4 %collective-permute-start.19 = (bf16[400,128]{1,0:T(8,128)(2,1)S(1)}, bf16[400,128]{1,0:T(8,128)(2,1)S(1)}, u32[]{:S(2)}, u32[]{:S(2)}) collective-permute-start(bf16[400,128]{1,0:T(8,128)(2,1)S(1)} %get-tuple-element.98), channel_id=1, source_target_pairs={{0,34},{1,35},{2,48},{3,49},{4,38},{5,39},{6,52},{7,53},{8,42},{9,... | collective-permute-start | bytes 307208 | tf_op jit(solution)/shard_map/ppermute | solution.py:26
  154.4 4.2 %collective-permute-start.20 = (bf16[400,128]{1,0:T(8,128)(2,1)S(1)}, bf16[400,128]{1,0:T(8,128)(2,1)S(1)}, u32[]{:S(2)}, u32[]{:S(2)}) collective-permute-start(bf16[400,128]{1,0:T(8,128)(2,1)S(1)} %get-tuple-element.99), channel_id=1, source_target_pairs={{0,32},{1,33},{2,34},{3,35},{4,36},{5,37},{6,38},{7,39},{8,40},{9,... | collective-permute-start | bytes 307208 | tf_op jit(solution)/shard_map/ppermute | solution.py:26
  158.6 1.5 shard_map.37
  160.8 5.2 %collective-permute-done.20.refs_7_ = bf16[400,128]{1,0:T(8,128)(2,1)S(1)} collective-permute-done((bf16[400,128]{1,0:T(8,128)(2,1)S(1)}, bf16[400,128]{1,0:T(8,128)(2,1)S(1)}, u32[]{:S(2)}, u32[]{:S(2)}) %collective-permute-start.20) | collective-permute-done | bytes 102432 | tf_op jit(solution)/shard_map/ppermute | solution.py:26
  166.0 1.4 shard_map.38
  167.4 4.9 %collective-permute-start.22 = (f32[128,128]{1,0:T(8,128)S(1)}, f32[128,128]{1,0:T(8,128)S(1)}, u32[]{:S(2)}, u32[]{:S(2)}) collective-permute-start(f32[128,128]{1,0:T(8,128)S(1)} %get-tuple-element.117), channel_id=1, source_target_pairs={{0,1},{1,2},{2,3},{3,0},{4,16},{5,17},{6,18},{7,19},{8,32},{9,33},... | collective-permute-start | bytes 196616 | tf_op jit(solution)/shard_map/ppermute | solution.py:26
  172.3 4.2 %collective-permute-start.23 = (f32[128,128]{1,0:T(8,128)S(1)}, f32[128,128]{1,0:T(8,128)S(1)}, u32[]{:S(2)}, u32[]{:S(2)}) collective-permute-start(f32[128,128]{1,0:T(8,128)S(1)} %get-tuple-element.118), channel_id=1, source_target_pairs={{0,0},{1,1},{2,2},{3,3},{4,18},{5,19},{6,16},{7,17},{8,34},{9,35},... | collective-permute-start | bytes 196616 | tf_op jit(solution)/shard_map/ppermute | solution.py:26
  178.0 5.3 %collective-permute-done.23.other_ref = f32[128,128]{1,0:T(8,128)S(1)} collective-permute-done((f32[128,128]{1,0:T(8,128)S(1)}, f32[128,128]{1,0:T(8,128)S(1)}, u32[]{:S(2)}, u32[]{:S(2)}) %collective-permute-start.23) | collective-permute-done | bytes 65568 | tf_op jit(solution)/shard_map/ppermute | solution.py:26
  (34 shorter events, 13.7 us)
Async XLA Ops:
  0.7 6.4 %copy-start = (bf16[512,1792]{1,0:T(8,128)(2,1)S(1)}, bf16[512,1792]{1,0:T(8,128)(2,1)}, u32[]{:S(2)}) copy-start(bf16[512,1792]{1,0:T(8,128)(2,1)} %g_ref.3) | copy-start | bytes 5505028
  3.7 24.8 %collective-permute-start = (bf16[512,896]{1,0:T(8,128)(2,1)}, bf16[512,896]{1,0:T(8,128)(2,1)S(1)}, u32[]{:S(2)}, u32[]{:S(2)}) collective-permute-start(bf16[512,896]{1,0:T(8,128)(2,1)} %get-tuple-element.61), channel_id=1, source_target_pairs={{0,16},{1,48},{2,18},{3,50},{4,20},{5,52},{6,22},{7,54},{8,24},{9,... | collective-permute-start | bytes 2752520 | tf_op jit(solution)/shard_map/ppermute | solution.py:26
  8.9 15.9 %collective-permute-start.1 = (bf16[240,1408]{1,0:T(8,128)(2,1)S(1)}, bf16[240,1408]{1,0:T(8,128)(2,1)S(1)}, u32[]{:S(2)}, u32[]{:S(2)}) collective-permute-start(bf16[240,1408]{1,0:T(8,128)(2,1)S(1)} %get-tuple-element.64), channel_id=1, source_target_pairs={{0,64},{1,65},{2,66},{3,67},{4,68},{5,69},{6,70},{7,71},{8,72},{9,... | collective-permute-start | bytes 2027528 | tf_op jit(solution)/shard_map/ppermute | solution.py:26
  10.2 16.1 %collective-permute-start.2 = (bf16[240,1408]{1,0:T(8,128)(2,1)S(1)}, bf16[240,1408]{1,0:T(8,128)(2,1)S(1)}, u32[]{:S(2)}, u32[]{:S(2)}) collective-permute-start(bf16[240,1408]{1,0:T(8,128)(2,1)S(1)} %get-tuple-element.65), channel_id=1, source_target_pairs={{0,192},{1,193},{2,194},{3,195},{4,196},{5,197},{6,198},{7,199},{8... | collective-permute-start | bytes 2027528 | tf_op jit(solution)/shard_map/ppermute | solution.py:26
  31.0 4.7 %copy-start.2 = (bf16[512,896]{1,0:T(8,128)(2,1)S(1)}, bf16[512,896]{1,0:T(8,128)(2,1)}, u32[]{:S(2)}) copy-start(bf16[512,896]{1,0:T(8,128)(2,1)} %get-tuple-element.67) | copy-start | bytes 2752516
  33.6 30.4 %collective-permute-start.5 = (bf16[464,1408]{1,0:T(8,128)(2,1)S(1)}, bf16[464,1408]{1,0:T(8,128)(2,1)S(1)}, u32[]{:S(2)}, u32[]{:S(2)}) collective-permute-start(bf16[464,1408]{1,0:T(8,128)(2,1)S(1)} %shard_map.32), channel_id=1, source_target_pairs={{0,192},{1,193},{2,194},{3,195},{4,196},{5,197},{6,198},{7,199},{8... | collective-permute-start | bytes 3919880 | tf_op jit(solution)/shard_map/ppermute | solution.py:26
  34.2 30.7 %collective-permute-start.4 = (bf16[464,1408]{1,0:T(8,128)(2,1)S(1)}, bf16[464,1408]{1,0:T(8,128)(2,1)S(1)}, u32[]{:S(2)}, u32[]{:S(2)}) collective-permute-start(bf16[464,1408]{1,0:T(8,128)(2,1)S(1)} %shard_map.31), channel_id=1, source_target_pairs={{0,64},{1,65},{2,66},{3,67},{4,68},{5,69},{6,70},{7,71},{8,72},{9,... | collective-permute-start | bytes 3919880 | tf_op jit(solution)/shard_map/ppermute | solution.py:26
  35.7 0.7 collective-permute-start.3
  64.8 6.3 %collective-permute-start.6 = (bf16[512,896]{1,0:T(8,128)(2,1)S(1)}, bf16[512,896]{1,0:T(8,128)(2,1)S(1)}, u32[]{:S(2)}, u32[]{:S(2)}) collective-permute-start(bf16[512,896]{1,0:T(8,128)(2,1)S(1)} %collective-permute-done.3.far), channel_id=1, source_target_pairs={{0,1},{1,0},{2,3},{3,2},{4,5},{5,4},{6,7},{7,6},{8,9},{9,8},{10,11... | collective-permute-start | bytes 2752520 | tf_op jit(solution)/shard_map/ppermute | solution.py:26
  65.6 5.6 %collective-permute-start.7 = (bf16[512,896]{1,0:T(8,128)(2,1)S(1)}, bf16[512,896]{1,0:T(8,128)(2,1)S(1)}, u32[]{:S(2)}, u32[]{:S(2)}) collective-permute-start(bf16[512,896]{1,0:T(8,128)(2,1)S(1)} %collective-permute-done.near), channel_id=1, source_target_pairs={{0,1},{1,0},{2,3},{3,2},{4,5},{5,4},{6,7},{7,6},{8,9},{9,8},{10,11... | collective-permute-start | bytes 2752520 | tf_op jit(solution)/shard_map/ppermute | solution.py:26
  77.0 17.9 %collective-permute-start.8 = (bf16[1168,256]{1,0:T(8,128)(2,1)S(1)}, bf16[1168,256]{1,0:T(8,128)(2,1)S(1)}, u32[]{:S(2)}, u32[]{:S(2)}) collective-permute-start(bf16[1168,256]{1,0:T(8,128)(2,1)S(1)} %get-tuple-element.81), channel_id=1, source_target_pairs={{0,4},{1,5},{2,6},{3,7},{4,8},{5,9},{6,10},{7,11},{8,12},{9,13},{1... | collective-permute-start | bytes 1794056 | tf_op jit(solution)/shard_map/ppermute | solution.py:26
  78.3 16.6 %collective-permute-start.9 = (bf16[1168,256]{1,0:T(8,128)(2,1)S(1)}, bf16[1168,256]{1,0:T(8,128)(2,1)S(1)}, u32[]{:S(2)}, u32[]{:S(2)}) collective-permute-start(bf16[1168,256]{1,0:T(8,128)(2,1)S(1)} %get-tuple-element.82), channel_id=1, source_target_pairs={{0,12},{1,13},{2,14},{3,15},{4,0},{5,1},{6,2},{7,3},{8,4},{9,5},{1... | collective-permute-start | bytes 1794056 | tf_op jit(solution)/shard_map/ppermute | solution.py:26
  79.0 15.9 %collective-permute-start.10 = (bf16[112,1920]{1,0:T(8,128)(2,1)S(1)}, bf16[112,1920]{1,0:T(8,128)(2,1)S(1)}, u32[]{:S(2)}, u32[]{:S(2)}) collective-permute-start(bf16[112,1920]{1,0:T(8,128)(2,1)S(1)} %get-tuple-element.84), channel_id=1, source_target_pairs={{0,32},{1,33},{2,34},{3,35},{4,36},{5,37},{6,38},{7,39},{8,40},{9,... | collective-permute-start | bytes 1290248 | tf_op jit(solution)/shard_map/ppermute | solution.py:26
  94.9 34.2 %collective-permute-start.11 = (bf16[1168,256]{1,0:T(8,128)(2,1)S(1)}, bf16[1168,256]{1,0:T(8,128)(2,1)S(1)}, u32[]{:S(2)}, u32[]{:S(2)}) collective-permute-start(bf16[1168,256]{1,0:T(8,128)(2,1)S(1)} %get-tuple-element.88), channel_id=1, source_target_pairs={{0,8},{1,9},{2,10},{3,11},{4,12},{5,13},{6,14},{7,15},{8,0},{9,1},... | collective-permute-start | bytes 1794056 | tf_op jit(solution)/shard_map/ppermute | solution.py:26
  96.5 31.3 %collective-permute-start.12 = (bf16[112,1920]{1,0:T(8,128)(2,1)S(1)}, bf16[112,1920]{1,0:T(8,128)(2,1)S(1)}, u32[]{:S(2)}, u32[]{:S(2)}) collective-permute-start(bf16[112,1920]{1,0:T(8,128)(2,1)S(1)} %get-tuple-element.89), channel_id=1, source_target_pairs={{0,16},{1,17},{2,18},{3,19},{4,20},{5,21},{6,22},{7,23},{8,24},{9,... | collective-permute-start | bytes 1290248 | tf_op jit(solution)/shard_map/ppermute | solution.py:26
  107.8 21.2 %collective-permute-start.13 = (bf16[112,1920]{1,0:T(8,128)(2,1)S(1)}, bf16[112,1920]{1,0:T(8,128)(2,1)S(1)}, u32[]{:S(2)}, u32[]{:S(2)}) collective-permute-start(bf16[112,1920]{1,0:T(8,128)(2,1)S(1)} %get-tuple-element.90), channel_id=1, source_target_pairs={{0,48},{1,49},{2,50},{3,51},{4,52},{5,53},{6,54},{7,55},{8,56},{9,... | collective-permute-start | bytes 1290248 | tf_op jit(solution)/shard_map/ppermute | solution.py:26
  129.0 1.3 copy-start.1
  133.0 6.1 %collective-permute-start.14 = (bf16[400,128]{1,0:T(8,128)(2,1)S(1)}, bf16[400,128]{1,0:T(8,128)(2,1)S(1)}, u32[]{:S(2)}, u32[]{:S(2)}) collective-permute-start(bf16[400,128]{1,0:T(8,128)(2,1)S(1)} %get-tuple-element.93), channel_id=1, source_target_pairs={{0,2},{1,3},{2,16},{3,17},{4,6},{5,7},{6,20},{7,21},{8,10},{9,11},... | collective-permute-start | bytes 307208 | tf_op jit(solution)/shard_map/ppermute | solution.py:26
  141.6 12.9 %collective-permute-start.21 = (f32[112,384]{1,0:T(8,128)S(1)}, f32[112,384]{1,0:T(8,128)S(1)}, u32[]{:S(2)}, u32[]{:S(2)}) collective-permute-start(f32[112,384]{1,0:T(8,128)S(1)} %get-tuple-element.107), channel_id=1, source_target_pairs={{0,64},{1,65},{2,66},{3,67},{4,68},{5,69},{6,70},{7,71},{8,72},{9,... | collective-permute-start | bytes 516104 | tf_op jit(solution)/shard_map/ppermute | solution.py:26
  143.7 6.3 %collective-permute-start.15 = (bf16[400,128]{1,0:T(8,128)(2,1)S(1)}, bf16[400,128]{1,0:T(8,128)(2,1)S(1)}, u32[]{:S(2)}, u32[]{:S(2)}) collective-permute-start(bf16[400,128]{1,0:T(8,128)(2,1)S(1)} %get-tuple-element.94), channel_id=1, source_target_pairs={{0,50},{1,51},{2,0},{3,1},{4,54},{5,55},{6,4},{7,5},{8,58},{9,59},... | collective-permute-start | bytes 307208 | tf_op jit(solution)/shard_map/ppermute | solution.py:26
  145.2 14.9 %collective-permute-start.16 = (bf16[400,128]{1,0:T(8,128)(2,1)S(1)}, bf16[400,128]{1,0:T(8,128)(2,1)S(1)}, u32[]{:S(2)}, u32[]{:S(2)}) collective-permute-start(bf16[400,128]{1,0:T(8,128)(2,1)S(1)} %get-tuple-element.95), channel_id=1, source_target_pairs={{0,16},{1,17},{2,18},{3,19},{4,20},{5,21},{6,22},{7,23},{8,24},{9,... | collective-permute-start | bytes 307208 | tf_op jit(solution)/shard_map/ppermute | solution.py:26
  145.2 14.9 %collective-permute-start.17 = (bf16[400,128]{1,0:T(8,128)(2,1)S(1)}, bf16[400,128]{1,0:T(8,128)(2,1)S(1)}, u32[]{:S(2)}, u32[]{:S(2)}) collective-permute-start(bf16[400,128]{1,0:T(8,128)(2,1)S(1)} %get-tuple-element.96), channel_id=1, source_target_pairs={{0,48},{1,49},{2,50},{3,51},{4,52},{5,53},{6,54},{7,55},{8,56},{9,... | collective-permute-start | bytes 307208 | tf_op jit(solution)/shard_map/ppermute | solution.py:26
  149.4 11.4 %collective-permute-start.18 = (bf16[400,128]{1,0:T(8,128)(2,1)S(1)}, bf16[400,128]{1,0:T(8,128)(2,1)S(1)}, u32[]{:S(2)}, u32[]{:S(2)}) collective-permute-start(bf16[400,128]{1,0:T(8,128)(2,1)S(1)} %get-tuple-element.97), channel_id=1, source_target_pairs={{0,18},{1,19},{2,32},{3,33},{4,22},{5,23},{6,36},{7,37},{8,26},{9,... | collective-permute-start | bytes 307208 | tf_op jit(solution)/shard_map/ppermute | solution.py:26
  150.0 10.7 %collective-permute-start.19 = (bf16[400,128]{1,0:T(8,128)(2,1)S(1)}, bf16[400,128]{1,0:T(8,128)(2,1)S(1)}, u32[]{:S(2)}, u32[]{:S(2)}) collective-permute-start(bf16[400,128]{1,0:T(8,128)(2,1)S(1)} %get-tuple-element.98), channel_id=1, source_target_pairs={{0,34},{1,35},{2,48},{3,49},{4,38},{5,39},{6,52},{7,53},{8,42},{9,... | collective-permute-start | bytes 307208 | tf_op jit(solution)/shard_map/ppermute | solution.py:26
  154.4 11.6 %collective-permute-start.20 = (bf16[400,128]{1,0:T(8,128)(2,1)S(1)}, bf16[400,128]{1,0:T(8,128)(2,1)S(1)}, u32[]{:S(2)}, u32[]{:S(2)}) collective-permute-start(bf16[400,128]{1,0:T(8,128)(2,1)S(1)} %get-tuple-element.99), channel_id=1, source_target_pairs={{0,32},{1,33},{2,34},{3,35},{4,36},{5,37},{6,38},{7,39},{8,40},{9,... | collective-permute-start | bytes 307208 | tf_op jit(solution)/shard_map/ppermute | solution.py:26
  167.4 10.5 %collective-permute-start.22 = (f32[128,128]{1,0:T(8,128)S(1)}, f32[128,128]{1,0:T(8,128)S(1)}, u32[]{:S(2)}, u32[]{:S(2)}) collective-permute-start(f32[128,128]{1,0:T(8,128)S(1)} %get-tuple-element.117), channel_id=1, source_target_pairs={{0,1},{1,2},{2,3},{3,0},{4,16},{5,17},{6,18},{7,19},{8,32},{9,33},... | collective-permute-start | bytes 196616 | tf_op jit(solution)/shard_map/ppermute | solution.py:26
  172.3 11.0 %collective-permute-start.23 = (f32[128,128]{1,0:T(8,128)S(1)}, f32[128,128]{1,0:T(8,128)S(1)}, u32[]{:S(2)}, u32[]{:S(2)}) collective-permute-start(f32[128,128]{1,0:T(8,128)S(1)} %get-tuple-element.118), channel_id=1, source_target_pairs={{0,0},{1,1},{2,2},{3,3},{4,18},{5,19},{6,16},{7,17},{8,34},{9,35},... | collective-permute-start | bytes 196616 | tf_op jit(solution)/shard_map/ppermute | solution.py:26

commit v2 on v0

--- a/solution.py
+++ b/solution.py
@@ -14,7 +14,6 @@
 PLACES = list(itertools.product(*(range(n) for n in SIZES)))
 STEPS = (1, 3, 2)
 Z_STEPS = (1, 7, 2, 6, 3, 5, 4)
-FLOPS = 4_000_000_000
 
 
 def number(place):
@@ -64,7 +63,7 @@
     )
 
 
-def run(body, outs, scratch, flops, *args):
+def run(body, outs, scratch, *args):
     smem, vmem = pl.BlockSpec(memory_space=pltpu.SMEM), pl.BlockSpec(memory_space=pltpu.VMEM)
     return pl.pallas_call(
         body,
@@ -72,9 +71,7 @@
         in_specs=[smem] + [vmem] * (len(args) - 1),
         out_specs=[vmem] * len(outs),
         scratch_shapes=[pltpu.VMEM(shape, dtype) for shape, dtype in scratch],
-        cost_estimate=pl.CostEstimate(
-            flops=flops, bytes_accessed=sum(a.size * a.dtype.itemsize for a in args), transcendentals=0
-        ),
+        cost_estimate=pl.CostEstimate(flops=1000, bytes_accessed=1000, transcendentals=0),
         compiler_params=pltpu.CompilerParams(vmem_limit_bytes=48 * 1024 * 1024),
     )(*args)
 
@@ -397,36 +394,37 @@
     cut = lambda parity: lax.dynamic_slice_in_dim(gradient, parity * half, half, 1)
     near, far, gradient = barrier((cut((zh + 1) % 2), cut(zh % 2), gradient))
     near = send(near, lambda x, zh, y, zl, core: (x, 2 * core + (zh + 1) % 2, y, zl, zh // 2))
-    far = send(far, lambda x, zh, y, zl, core: (x, 2 * core + zh % 2, y, zl, zh // 2))
 
     window = [((rows, WINDOW), BF16), ((512, 512), BF16), ((512, 128), F32)]
     half_part, whole_part = ((HALF_ROWS + 16, WINDOW), BF16), ((BLOCK + 16, WINDOW), BF16)
     over_x = lambda s, v: send(v, lambda x, zh, y, zl, core: (x + s, zh, y, zl, core))
-    far_1, far_3 = run(right_far, [half_part] * 2, window, FLOPS, at, gradient)
+    far_1, far_3 = run(right_far, [half_part] * 2, window, at, gradient)
     far_1, far_3 = over_x(1, far_1), over_x(3, far_3)
+    near, far, far_1, far_3 = barrier((near, far, far_1, far_3))
+    far = send(far, lambda x, zh, y, zl, core: (x, 2 * core + zh % 2, y, zl, zh // 2))
     add = lambda s, v: run(
-        functools.partial(right_near, s), [whole_part], window + [((BLOCK, 256), F32)], FLOPS, at, gradient, v
+        functools.partial(right_near, s), [whole_part], window + [((BLOCK, 256), F32)], at, gradient, v
     )[0]
     code_1, code_3 = add(1, far_1), add(3, far_3)
     right_1, right_3 = over_x(1, code_1), over_x(3, code_3)
-    near, far, _ = barrier((near, far, (code_1, code_3)))
 
     swap = lambda x, zh, y, zl, core: (x, zh, y, zl, 1 - core)
     far_2, near_2 = send(far, swap), send(near, swap)
+
+    far, near, far_2, near_2, right_1, right_3 = barrier((far, near, far_2, near_2, right_1, right_3))
     packed = (ROWS + 16, 256)
     left_1, left_3, left_2, left_own, norms = run(
         left_first,
         [(packed, BF16)] * 3 + [((ROWS, 256), F32), ((16, SUB), F32)],
         [((2048, half), BF16), ((256, half), BF16), ((2048, SUB), F32), ((16, SUB), F32)],
-        FLOPS,
         at,
         far,
         near,
         far_2,
         near_2,
     )
-    right_1, right_3, _ = barrier((right_1, right_3, left_1))
     over_y = lambda s, v: send(v, lambda x, zh, y, zl, core: (x, zh, y + s, zl, core))
+    right_1, right_3, _ = barrier((right_1, right_3, left_2))
     left_1, left_3, left_2 = over_y(1, left_1), over_y(3, left_3), over_y(2, left_2)
 
     piece = (CHUNK, WIDTH + 128)
@@ -434,26 +432,19 @@
         right_second,
         [(piece, BF16)] * 3 + [(piece, F32)],
         window + [((512, WINDOW), F32), ((640, 512), F32)],
-        FLOPS,
         at,
         gradient,
         right_1,
         right_3,
     )
     over_z = lambda s, v: send(v, lambda x, zh, y, zl, core: (x, zh + s, y, zl, core))
-    right_2, right_1 = over_z(2, code_2), over_z(1, code_1)
-    code_3, _ = barrier((code_3, left_3))
-    right_3 = over_z(3, code_3)
-    left_1, left_3, left_2, right_1, right_3, right_2 = barrier(
-        (left_1, left_3, left_2, right_1, right_3, right_2)
-    )
+    right_1, right_3, right_2 = over_z(1, code_1), over_z(3, code_3), over_z(2, code_2)
 
     piece = (400, SUB)
     codes = run(
         left_second,
         [(piece, BF16)] * 7 + [(piece, F32)],
         [((ROWS, 256), F32), ((4, 16, SUB), F32)] + [((16, SUB), F32)] * 3,
-        FLOPS,
         at,
         left_own,
         norms,
@@ -461,35 +452,34 @@
         left_3,
         left_2,
     )
+    arrived = [send(code, along_z(s)) for s, code in zip(Z_STEPS, codes)]
     right_1, right_3, _ = barrier((right_1, right_3, codes))
-    arrived = [send(code, along_z(s)) for s, code in zip(Z_STEPS, codes)]
 
     right_base, image = run(
         functools.partial(right_third, 1.0 / (rows * 16)),
         [((CHUNK, WINDOW), F32), ((CHUNK, IMAGE), F32)],
         [((1024, 128), F32), ((11, 128), F32)],
-        FLOPS,
         at,
         right_own,
         right_1,
         right_3,
         right_2,
     )
+    arrived, image = barrier((arrived, image))
     image = over_x(1, image)
-    right_gram = run(right_last, [((CHUNK, width), F32)], [], FLOPS, at, right_base, image)[0]
+    right_gram = run(right_last, [((CHUNK, width), F32)], [], at, right_base, image)[0]
 
     square = ((SUB, SUB), F32)
     base, more, same, other = run(
         functools.partial(left_third, 1.0 / (width * 16)),
         [((256, SUB), F32), square, square, square],
         [((384, SUB), F32)],
-        FLOPS,
         at,
         codes[7],
         *arrived,
     )
     same, other = send(same, mirror(0)), send(other, mirror(1))
-    left_gram = run(left_last, [((512, SUB), F32)], [], FLOPS, at, base, more, same, other)[0]
+    left_gram = run(left_last, [((512, SUB), F32)], [], at, base, more, same, other)[0]
     return (left_gram, right_gram)
 
 

time: 190 us -> 166 us (0.87)
  the two profiles are of different devices: /device:TPU:25 before, /device:TPU:54 now
where the time goes in v2:
time: 166 us
  starting transfers between devices  80.2 us (48%)
  waiting for transfers between devices  54.4 us (33%)
  Pallas kernels  27.7 us (17%)
  local copies, waits for them, and re-layouts  3.1 us (2%)
    ppermute x24, starting transfers between devices, send(): lax.ppermute(array, ('row', 'col'), [(number(p), number(to(*p))) for p in...  80.2 us
    ppermute x24, waiting for transfers between devices, send(): lax.ppermute(array, ('row', 'col'), [(number(p), number(to(*p))) for p in...  54.4 us
    pallas_call x10, Pallas kernels, run(): pl.pallas_call(body, out_shape=[jax.ShapeDtypeStruct(shape, dtype) for sh...  27.7 us
  transfers between devices with their start and end apart: 24, of which 11 were waited for; matrix products, arithmetic and copies ran while one was open for 0% of the time, Pallas kernels for 12%

profile of v2, /device:TPU:54, one launch (start us, length us, event | category | flops | bytes accessed | tf_op | source)
XLA Modules:
  0.0 166.3 jit_solution(17614803528950371479)
XLA Ops:
  0.7 3.0 %constant_dynamic-slice_fusion = (bf16[512,896]{1,0:T(8,128)(2,1)}, bf16[512,896]{1,0:T(8,128)(2,1)}) fusion(bf16[512,1792]{1,0:T(8,128)(2,1)} %g_ref.3, s32[]{:T(128)S(6)} %select_n.48, s32[]{:T(128)S(6)} %select_n.46), kind=kLoop, calls=%fused_computation | loop fusion | bytes 3670024 | tf_op jit(solution)/shard_map/dynamic_slice | solution.py:394
  3.7 3.3 %collective-permute-start = (bf16[512,896]{1,0:T(8,128)(2,1)}, bf16[512,896]{1,0:T(8,128)(2,1)S(1)}, u32[]{:S(2)}, u32[]{:S(2)}) collective-permute-start(bf16[512,896]{1,0:T(8,128)(2,1)} %get-tuple-element.52), channel_id=1, source_target_pairs={{0,16},{1,48},{2,18},{3,50},{4,20},{5,52},{6,22},{7,54},{8,24},{9,... | collective-permute-start | bytes 2752520 | tf_op jit(solution)/shard_map/ppermute | solution.py:25
  7.1 1.9 %shard_map.30 = (bf16[240,1408]{1,0:T(8,128)(2,1)S(1)}, bf16[240,1408]{1,0:T(8,128)(2,1)S(1)}) custom-call(s32[8]{0:T(128)S(1)} %stack.26.at_ref, bf16[512,1792]{1,0:T(8,128)(2,1)S(1)} %copy-done), custom_call_target="tpu_custom_call" | custom-call | flops 1000 | bytes 1000 | tf_op jit(solution)/shard_map/pallas_call | solution.py:68
  9.5 1.5 collective-permute-start.2
  11.1 14.7 %collective-permute-done.1.in_ref = bf16[240,1408]{1,0:T(8,128)(2,1)S(1)} collective-permute-done((bf16[240,1408]{1,0:T(8,128)(2,1)S(1)}, bf16[240,1408]{1,0:T(8,128)(2,1)S(1)}, u32[]{:S(2)}, u32[]{:S(2)}) %collective-permute-start.1) | collective-permute-done | bytes 675872 | tf_op jit(solution)/shard_map/ppermute | solution.py:25
  25.8 2.0 %collective-permute-done.2.in_ref = bf16[240,1408]{1,0:T(8,128)(2,1)S(1)} collective-permute-done((bf16[240,1408]{1,0:T(8,128)(2,1)S(1)}, bf16[240,1408]{1,0:T(8,128)(2,1)S(1)}, u32[]{:S(2)}, u32[]{:S(2)}) %collective-permute-start.2) | collective-permute-done | bytes 675872 | tf_op jit(solution)/shard_map/ppermute | solution.py:25
  28.5 2.6 %shard_map.32 = bf16[464,1408]{1,0:T(8,128)(2,1)S(1)} custom-call(s32[8]{0:T(128)S(1)} %stack.26.at_ref, bf16[512,1792]{1,0:T(8,128)(2,1)S(1)} %copy-done, bf16[240,1408]{1,0:T(8,128)(2,1)S(1)} %collective-permute-done.2.in_ref), custom_call_target="tpu_custom_call" | custom-call | flops 1000 | bytes 1000 | tf_op jit(solution)/shard_map/pallas_call | solution.py:68
  31.8 2.5 %shard_map.31 = bf16[464,1408]{1,0:T(8,128)(2,1)S(1)} custom-call(s32[8]{0:T(128)S(1)} %stack.26.at_ref, bf16[512,1792]{1,0:T(8,128)(2,1)S(1)} %copy-done, bf16[240,1408]{1,0:T(8,128)(2,1)S(1)} %collective-permute-done.1.in_ref), custom_call_target="tpu_custom_call" | custom-call | flops 1000 | bytes 1000 | tf_op jit(solution)/shard_map/pallas_call | solution.py:68
  34.3 2.7 %collective-permute-start.6 = (bf16[464,1408]{1,0:T(8,128)(2,1)S(1)}, bf16[464,1408]{1,0:T(8,128)(2,1)S(1)}, u32[]{:S(2)}, u32[]{:S(2)}) collective-permute-start(bf16[464,1408]{1,0:T(8,128)(2,1)S(1)} %shard_map.31), channel_id=1, source_target_pairs={{0,64},{1,65},{2,66},{3,67},{4,68},{5,69},{6,70},{7,71},{8,72},{9,... | collective-permute-start | bytes 3919880 | tf_op jit(solution)/shard_map/ppermute | solution.py:25
  37.0 6.5 %collective-permute-start.5 = (bf16[512,896]{1,0:T(8,128)(2,1)S(1)}, bf16[512,896]{1,0:T(8,128)(2,1)S(1)}, u32[]{:S(2)}, u32[]{:S(2)}) collective-permute-start(bf16[512,896]{1,0:T(8,128)(2,1)S(1)} %collective-permute-done.near), channel_id=1, source_target_pairs={{0,1},{1,0},{2,3},{3,2},{4,5},{5,4},{6,7},{7,6},{8,9},{9,8},{10,11... | collective-permute-start | bytes 2752520 | tf_op jit(solution)/shard_map/ppermute | solution.py:25
  43.4 14.2 %collective-permute-start.4 = (bf16[512,896]{1,0:T(8,128)(2,1)S(1)}, bf16[512,896]{1,0:T(8,128)(2,1)S(1)}, u32[]{:S(2)}, u32[]{:S(2)}) collective-permute-start(bf16[512,896]{1,0:T(8,128)(2,1)S(1)} %collective-permute-done.3.far), channel_id=1, source_target_pairs={{0,1},{1,0},{2,3},{3,2},{4,5},{5,4},{6,7},{7,6},{8,9},{9,8},{10,11... | collective-permute-start | bytes 2752520 | tf_op jit(solution)/shard_map/ppermute | solution.py:25
  57.8 2.4 %collective-permute-done.6.in_1 = bf16[464,1408]{1,0:T(8,128)(2,1)S(1)} collective-permute-done((bf16[464,1408]{1,0:T(8,128)(2,1)S(1)}, bf16[464,1408]{1,0:T(8,128)(2,1)S(1)}, u32[]{:S(2)}, u32[]{:S(2)}) %collective-permute-start.6) | collective-permute-done | bytes 1306656 | tf_op jit(solution)/shard_map/ppermute | solution.py:25
  60.2 5.9 %shard_map.33 = (bf16[1168,256]{1,0:T(8,128)(2,1)S(1)}, bf16[1168,256]{1,0:T(8,128)(2,1)S(1)}, bf16[1168,256]{1,0:T(8,128)(2,1)S(1)}, f32[1152,256]{1,0:T(8,128)}, f32[16,128]{1,0:T(8,128)S(1)}) custom-call(s32[8]{0:T(128)S(1)} %stack.26.at_ref, bf16[512,896]{1,0:T(8,128)(2,1)S(1)} %collective-permute-done.3.far, ...), custom_call_target="tpu_custom_call" | custom-call | flops 1000 | bytes 1000 | tf_op jit(solution)/shard_map/pallas_call | solution.py:68
  68.1 1.6 collective-permute-start.10
  69.6 5.5 %shard_map.35 = (bf16[112,1920]{1,0:T(8,128)(2,1)S(1)}, bf16[112,1920]{1,0:T(8,128)(2,1)S(1)}, bf16[112,1920]{1,0:T(8,128)(2,1)S(1)}, f32[112,1920]{1,0:T(8,128)S(1)}) custom-call(s32[8]{0:T(128)S(1)} %stack.26.at_ref, bf16[512,1792]{1,0:T(8,128)(2,1)} %g_ref.3, bf16[464,1408]{1,0:T(8,128)(2,1)S(1)} %collective-permute-done.6.in_1, ...), custom_call_target="tpu_custom_call" | custom-call | flops 1000 | bytes 1000 | tf_op jit(solution)/shard_map/pallas_call | solution.py:68
  75.2 4.7 %collective-permute-start.18 = (bf16[112,1920]{1,0:T(8,128)(2,1)S(1)}, bf16[112,1920]{1,0:T(8,128)(2,1)S(1)}, u32[]{:S(2)}, u32[]{:S(2)}) collective-permute-start(bf16[112,1920]{1,0:T(8,128)(2,1)S(1)} %get-tuple-element.83), channel_id=1, source_target_pairs={{0,16},{1,17},{2,18},{3,19},{4,20},{5,21},{6,22},{7,23},{8,24},{9,... | collective-permute-start | bytes 1290248 | tf_op jit(solution)/shard_map/ppermute | solution.py:25
  79.9 4.8 %collective-permute-start.19 = (bf16[112,1920]{1,0:T(8,128)(2,1)S(1)}, bf16[112,1920]{1,0:T(8,128)(2,1)S(1)}, u32[]{:S(2)}, u32[]{:S(2)}) collective-permute-start(bf16[112,1920]{1,0:T(8,128)(2,1)S(1)} %get-tuple-element.84), channel_id=1, source_target_pairs={{0,48},{1,49},{2,50},{3,51},{4,52},{5,53},{6,54},{7,55},{8,56},{9,... | collective-permute-start | bytes 1290248 | tf_op jit(solution)/shard_map/ppermute | solution.py:25
  84.7 14.0 %collective-permute-start.20 = (bf16[112,1920]{1,0:T(8,128)(2,1)S(1)}, bf16[112,1920]{1,0:T(8,128)(2,1)S(1)}, u32[]{:S(2)}, u32[]{:S(2)}) collective-permute-start(bf16[112,1920]{1,0:T(8,128)(2,1)S(1)} %get-tuple-element.87), channel_id=1, source_target_pairs={{0,32},{1,33},{2,34},{3,35},{4,36},{5,37},{6,38},{7,39},{8,40},{9,... | collective-permute-start | bytes 1290248 | tf_op jit(solution)/shard_map/ppermute | solution.py:25
  98.7 2.7 %shard_map.34 = (bf16[400,128]{1,0:T(8,128)(2,1)S(1)}, bf16[400,128]{1,0:T(8,128)(2,1)S(1)}, bf16[400,128]{1,0:T(8,128)(2,1)S(1)}, bf16[400,128]{1,0:T(8,128)(2,...) custom-call(s32[8]{0:T(128)S(1)} %stack.26.at_ref, ...), custom_call_target="tpu_custom_call" | custom-call | flops 1000 | bytes 1000 | tf_op jit(solution)/shard_map/pallas_call | solution.py:68
  101.3 2.5 %collective-permute-start.11 = (bf16[400,128]{1,0:T(8,128)(2,1)S(1)}, bf16[400,128]{1,0:T(8,128)(2,1)S(1)}, u32[]{:S(2)}, u32[]{:S(2)}) collective-permute-start(bf16[400,128]{1,0:T(8,128)(2,1)S(1)} %get-tuple-element.71), channel_id=1, source_target_pairs={{0,2},{1,3},{2,16},{3,17},{4,6},{5,7},{6,20},{7,21},{8,10},{9,11},... | collective-permute-start | bytes 307208 | tf_op jit(solution)/shard_map/ppermute | solution.py:25
  104.0 17.3 %collective-permute-done.18.in_1 = bf16[112,1920]{1,0:T(8,128)(2,1)S(1)} collective-permute-done((bf16[112,1920]{1,0:T(8,128)(2,1)S(1)}, bf16[112,1920]{1,0:T(8,128)(2,1)S(1)}, u32[]{:S(2)}, u32[]{:S(2)}) %collective-permute-start.18) | collective-permute-done | bytes 430112 | tf_op jit(solution)/shard_map/ppermute | solution.py:25
  121.3 4.1 %collective-permute-start.14 = (bf16[400,128]{1,0:T(8,128)(2,1)S(1)}, bf16[400,128]{1,0:T(8,128)(2,1)S(1)}, u32[]{:S(2)}, u32[]{:S(2)}) collective-permute-start(bf16[400,128]{1,0:T(8,128)(2,1)S(1)} %get-tuple-element.74), channel_id=1, source_target_pairs={{0,48},{1,49},{2,50},{3,51},{4,52},{5,53},{6,54},{7,55},{8,56},{9,... | collective-permute-start | bytes 307208 | tf_op jit(solution)/shard_map/ppermute | solution.py:25
  125.6 5.0 %collective-permute-start.16 = (bf16[400,128]{1,0:T(8,128)(2,1)S(1)}, bf16[400,128]{1,0:T(8,128)(2,1)S(1)}, u32[]{:S(2)}, u32[]{:S(2)}) collective-permute-start(bf16[400,128]{1,0:T(8,128)(2,1)S(1)} %get-tuple-element.76), channel_id=1, source_target_pairs={{0,34},{1,35},{2,48},{3,49},{4,38},{5,39},{6,52},{7,53},{8,42},{9,... | collective-permute-start | bytes 307208 | tf_op jit(solution)/shard_map/ppermute | solution.py:25
  131.0 2.5 %shard_map.36 = (f32[112,1408]{1,0:T(8,128)S(1)}, f32[112,384]{1,0:T(8,128)S(1)}) custom-call(s32[8]{0:T(128)S(1)} %stack.26.at_ref, f32[112,1920]{1,0:T(8,128)S(1)} %get-tuple-element.82.own_ref, bf16[112,1920]{1,0:T(8,128)(2,1)S(1)} %collective-permute-done.18.in_1, bf16[112,1920]{1,0:T(8,128)(2,1)S(1)} %collective-permute-done.19.in_3, ...), custom_call_target="tpu_custom_call" | custom-call | flops 1000 | bytes 1000 | tf_op jit(solution)/shard_map/pallas_call | solution.py:68
  133.5 2.5 %collective-permute-done.15.refs_5_ = bf16[400,128]{1,0:T(8,128)(2,1)S(1)} collective-permute-done((bf16[400,128]{1,0:T(8,128)(2,1)S(1)}, bf16[400,128]{1,0:T(8,128)(2,1)S(1)}, u32[]{:S(2)}, u32[]{:S(2)}) %collective-permute-start.15) | collective-permute-done | bytes 102432 | tf_op jit(solution)/shard_map/ppermute | solution.py:25
  136.0 1.8 %collective-permute-done.16.refs_6_ = bf16[400,128]{1,0:T(8,128)(2,1)S(1)} collective-permute-done((bf16[400,128]{1,0:T(8,128)(2,1)S(1)}, bf16[400,128]{1,0:T(8,128)(2,1)S(1)}, u32[]{:S(2)}, u32[]{:S(2)}) %collective-permute-start.16) | collective-permute-done | bytes 102432 | tf_op jit(solution)/shard_map/ppermute | solution.py:25
  137.8 4.2 %collective-permute-done.17.refs_7_ = bf16[400,128]{1,0:T(8,128)(2,1)S(1)} collective-permute-done((bf16[400,128]{1,0:T(8,128)(2,1)S(1)}, bf16[400,128]{1,0:T(8,128)(2,1)S(1)}, u32[]{:S(2)}, u32[]{:S(2)}) %collective-permute-start.17) | collective-permute-done | bytes 102432 | tf_op jit(solution)/shard_map/ppermute | solution.py:25
  142.0 2.2 %collective-permute-start.23 = (f32[112,384]{1,0:T(8,128)S(1)}, f32[112,384]{1,0:T(8,128)S(1)}, u32[]{:S(2)}, u32[]{:S(2)}) collective-permute-start(f32[112,384]{1,0:T(8,128)S(1)} %get-tuple-element.101), channel_id=1, source_target_pairs={{0,64},{1,65},{2,66},{3,67},{4,68},{5,69},{6,70},{7,71},{8,72},{9,... | collective-permute-start | bytes 516104 | tf_op jit(solution)/shard_map/ppermute | solution.py:25
  145.7 6.8 %collective-permute-start.21 = (f32[128,128]{1,0:T(8,128)S(1)}, f32[128,128]{1,0:T(8,128)S(1)}, u32[]{:S(2)}, u32[]{:S(2)}) collective-permute-start(f32[128,128]{1,0:T(8,128)S(1)} %get-tuple-element.98), channel_id=1, source_target_pairs={{0,1},{1,2},{2,3},{3,0},{4,16},{5,17},{6,18},{7,19},{8,32},{9,33},... | collective-permute-start | bytes 196616 | tf_op jit(solution)/shard_map/ppermute | solution.py:25
  152.5 1.9 %collective-permute-start.22 = (f32[128,128]{1,0:T(8,128)S(1)}, f32[128,128]{1,0:T(8,128)S(1)}, u32[]{:S(2)}, u32[]{:S(2)}) collective-permute-start(f32[128,128]{1,0:T(8,128)S(1)} %get-tuple-element.99), channel_id=1, source_target_pairs={{0,0},{1,1},{2,2},{3,3},{4,18},{5,19},{6,16},{7,17},{8,34},{9,35},... | collective-permute-start | bytes 196616 | tf_op jit(solution)/shard_map/ppermute | solution.py:25
  155.8 7.7 %collective-permute-done.22.other_ref = f32[128,128]{1,0:T(8,128)S(1)} collective-permute-done((f32[128,128]{1,0:T(8,128)S(1)}, f32[128,128]{1,0:T(8,128)S(1)}, u32[]{:S(2)}, u32[]{:S(2)}) %collective-permute-start.22) | collective-permute-done | bytes 65568 | tf_op jit(solution)/shard_map/ppermute | solution.py:25
  164.7 1.5 shard_map.39
  (34 shorter events, 9.0 us)
Async XLA Ops:
  0.7 6.4 %copy-start = (bf16[512,1792]{1,0:T(8,128)(2,1)S(1)}, bf16[512,1792]{1,0:T(8,128)(2,1)}, u32[]{:S(2)}) copy-start(bf16[512,1792]{1,0:T(8,128)(2,1)} %g_ref.3) | copy-start | bytes 5505028
  3.7 24.1 %collective-permute-start = (bf16[512,896]{1,0:T(8,128)(2,1)}, bf16[512,896]{1,0:T(8,128)(2,1)S(1)}, u32[]{:S(2)}, u32[]{:S(2)}) collective-permute-start(bf16[512,896]{1,0:T(8,128)(2,1)} %get-tuple-element.52), channel_id=1, source_target_pairs={{0,16},{1,48},{2,18},{3,50},{4,20},{5,52},{6,22},{7,54},{8,24},{9,... | collective-permute-start | bytes 2752520 | tf_op jit(solution)/shard_map/ppermute | solution.py:25
  7.1 20.7 %copy-start.2 = (bf16[512,896]{1,0:T(8,128)(2,1)S(1)}, bf16[512,896]{1,0:T(8,128)(2,1)}, u32[]{:S(2)}) copy-start(bf16[512,896]{1,0:T(8,128)(2,1)} %get-tuple-element.57) | copy-start | bytes 2752516
  9.0 16.8 %collective-permute-start.1 = (bf16[240,1408]{1,0:T(8,128)(2,1)S(1)}, bf16[240,1408]{1,0:T(8,128)(2,1)S(1)}, u32[]{:S(2)}, u32[]{:S(2)}) collective-permute-start(bf16[240,1408]{1,0:T(8,128)(2,1)S(1)} %get-tuple-element.55), channel_id=1, source_target_pairs={{0,64},{1,65},{2,66},{3,67},{4,68},{5,69},{6,70},{7,71},{8,72},{9,... | collective-permute-start | bytes 2027528 | tf_op jit(solution)/shard_map/ppermute | solution.py:25
  9.5 18.3 %collective-permute-start.2 = (bf16[240,1408]{1,0:T(8,128)(2,1)S(1)}, bf16[240,1408]{1,0:T(8,128)(2,1)S(1)}, u32[]{:S(2)}, u32[]{:S(2)}) collective-permute-start(bf16[240,1408]{1,0:T(8,128)(2,1)S(1)} %get-tuple-element.56), channel_id=1, source_target_pairs={{0,192},{1,193},{2,194},{3,195},{4,196},{5,197},{6,198},{7,199},{8... | collective-permute-start | bytes 2027528 | tf_op jit(solution)/shard_map/ppermute | solution.py:25
  27.8 15.7 %collective-permute-start.3 = (bf16[512,896]{1,0:T(8,128)(2,1)S(1)}, bf16[512,896]{1,0:T(8,128)(2,1)S(1)}, u32[]{:S(2)}, u32[]{:S(2)}) collective-permute-start(bf16[512,896]{1,0:T(8,128)(2,1)S(1)} %copy-done.2), channel_id=1, source_target_pairs={{0,0},{1,32},{2,2},{3,34},{4,4},{5,36},{6,6},{7,38},{8,8},{9,40},{... | collective-permute-start | bytes 2752520 | tf_op jit(solution)/shard_map/ppermute | solution.py:25
  31.1 26.7 %collective-permute-start.7 = (bf16[464,1408]{1,0:T(8,128)(2,1)S(1)}, bf16[464,1408]{1,0:T(8,128)(2,1)S(1)}, u32[]{:S(2)}, u32[]{:S(2)}) collective-permute-start(bf16[464,1408]{1,0:T(8,128)(2,1)S(1)} %shard_map.32), channel_id=1, source_target_pairs={{0,192},{1,193},{2,194},{3,195},{4,196},{5,197},{6,198},{7,199},{8... | collective-permute-start | bytes 3919880 | tf_op jit(solution)/shard_map/ppermute | solution.py:25
  34.3 25.9 %collective-permute-start.6 = (bf16[464,1408]{1,0:T(8,128)(2,1)S(1)}, bf16[464,1408]{1,0:T(8,128)(2,1)S(1)}, u32[]{:S(2)}, u32[]{:S(2)}) collective-permute-start(bf16[464,1408]{1,0:T(8,128)(2,1)S(1)} %shard_map.31), channel_id=1, source_target_pairs={{0,64},{1,65},{2,66},{3,67},{4,68},{5,69},{6,70},{7,71},{8,72},{9,... | collective-permute-start | bytes 3919880 | tf_op jit(solution)/shard_map/ppermute | solution.py:25
  37.0 20.6 %collective-permute-start.5 = (bf16[512,896]{1,0:T(8,128)(2,1)S(1)}, bf16[512,896]{1,0:T(8,128)(2,1)S(1)}, u32[]{:S(2)}, u32[]{:S(2)}) collective-permute-start(bf16[512,896]{1,0:T(8,128)(2,1)S(1)} %collective-permute-done.near), channel_id=1, source_target_pairs={{0,1},{1,0},{2,3},{3,2},{4,5},{5,4},{6,7},{7,6},{8,9},{9,8},{10,11... | collective-permute-start | bytes 2752520 | tf_op jit(solution)/shard_map/ppermute | solution.py:25
  43.4 16.7 %collective-permute-start.4 = (bf16[512,896]{1,0:T(8,128)(2,1)S(1)}, bf16[512,896]{1,0:T(8,128)(2,1)S(1)}, u32[]{:S(2)}, u32[]{:S(2)}) collective-permute-start(bf16[512,896]{1,0:T(8,128)(2,1)S(1)} %collective-permute-done.3.far), channel_id=1, source_target_pairs={{0,1},{1,0},{2,3},{3,2},{4,5},{5,4},{6,7},{7,6},{8,9},{9,8},{10,11... | collective-permute-start | bytes 2752520 | tf_op jit(solution)/shard_map/ppermute | solution.py:25
  66.0 18.6 %collective-permute-start.8 = (bf16[1168,256]{1,0:T(8,128)(2,1)S(1)}, bf16[1168,256]{1,0:T(8,128)(2,1)S(1)}, u32[]{:S(2)}, u32[]{:S(2)}) collective-permute-start(bf16[1168,256]{1,0:T(8,128)(2,1)S(1)} %get-tuple-element.67), channel_id=1, source_target_pairs={{0,4},{1,5},{2,6},{3,7},{4,8},{5,9},{6,10},{7,11},{8,12},{9,13},{1... | collective-permute-start | bytes 1794056 | tf_op jit(solution)/shard_map/ppermute | solution.py:25
  67.3 31.3 %collective-permute-start.9 = (bf16[1168,256]{1,0:T(8,128)(2,1)S(1)}, bf16[1168,256]{1,0:T(8,128)(2,1)S(1)}, u32[]{:S(2)}, u32[]{:S(2)}) collective-permute-start(bf16[1168,256]{1,0:T(8,128)(2,1)S(1)} %get-tuple-element.68), channel_id=1, source_target_pairs={{0,12},{1,13},{2,14},{3,15},{4,0},{5,1},{6,2},{7,3},{8,4},{9,5},{1... | collective-permute-start | bytes 1794056 | tf_op jit(solution)/shard_map/ppermute | solution.py:25
  68.1 30.6 %copy-start.1 = (f32[1152,256]{1,0:T(8,128)S(1)}, f32[1152,256]{1,0:T(8,128)}, u32[]{:S(2)}) copy-start(f32[1152,256]{1,0:T(8,128)} %get-tuple-element.65.own_ref) | copy-start | bytes 3538948
  68.1 30.6 %collective-permute-start.10 = (bf16[1168,256]{1,0:T(8,128)(2,1)S(1)}, bf16[1168,256]{1,0:T(8,128)(2,1)S(1)}, u32[]{:S(2)}, u32[]{:S(2)}) collective-permute-start(bf16[1168,256]{1,0:T(8,128)(2,1)S(1)} %get-tuple-element.69), channel_id=1, source_target_pairs={{0,8},{1,9},{2,10},{3,11},{4,12},{5,13},{6,14},{7,15},{8,0},{9,1},... | collective-permute-start | bytes 1794056 | tf_op jit(solution)/shard_map/ppermute | solution.py:25
  75.2 46.1 %collective-permute-start.18 = (bf16[112,1920]{1,0:T(8,128)(2,1)S(1)}, bf16[112,1920]{1,0:T(8,128)(2,1)S(1)}, u32[]{:S(2)}, u32[]{:S(2)}) collective-permute-start(bf16[112,1920]{1,0:T(8,128)(2,1)S(1)} %get-tuple-element.83), channel_id=1, source_target_pairs={{0,16},{1,17},{2,18},{3,19},{4,20},{5,21},{6,22},{7,23},{8,24},{9,... | collective-permute-start | bytes 1290248 | tf_op jit(solution)/shard_map/ppermute | solution.py:25
  79.9 41.4 %collective-permute-start.19 = (bf16[112,1920]{1,0:T(8,128)(2,1)S(1)}, bf16[112,1920]{1,0:T(8,128)(2,1)S(1)}, u32[]{:S(2)}, u32[]{:S(2)}) collective-permute-start(bf16[112,1920]{1,0:T(8,128)(2,1)S(1)} %get-tuple-element.84), channel_id=1, source_target_pairs={{0,48},{1,49},{2,50},{3,51},{4,52},{5,53},{6,54},{7,55},{8,56},{9,... | collective-permute-start | bytes 1290248 | tf_op jit(solution)/shard_map/ppermute | solution.py:25
  84.7 40.9 %collective-permute-start.20 = (bf16[112,1920]{1,0:T(8,128)(2,1)S(1)}, bf16[112,1920]{1,0:T(8,128)(2,1)S(1)}, u32[]{:S(2)}, u32[]{:S(2)}) collective-permute-start(bf16[112,1920]{1,0:T(8,128)(2,1)S(1)} %get-tuple-element.87), channel_id=1, source_target_pairs={{0,32},{1,33},{2,34},{3,35},{4,36},{5,37},{6,38},{7,39},{8,40},{9,... | collective-permute-start | bytes 1290248 | tf_op jit(solution)/shard_map/ppermute | solution.py:25
  101.3 24.3 %collective-permute-start.11 = (bf16[400,128]{1,0:T(8,128)(2,1)S(1)}, bf16[400,128]{1,0:T(8,128)(2,1)S(1)}, u32[]{:S(2)}, u32[]{:S(2)}) collective-permute-start(bf16[400,128]{1,0:T(8,128)(2,1)S(1)} %get-tuple-element.71), channel_id=1, source_target_pairs={{0,2},{1,3},{2,16},{3,17},{4,6},{5,7},{6,20},{7,21},{8,10},{9,11},... | collective-permute-start | bytes 307208 | tf_op jit(solution)/shard_map/ppermute | solution.py:25
  103.9 26.8 %collective-permute-start.12 = (bf16[400,128]{1,0:T(8,128)(2,1)S(1)}, bf16[400,128]{1,0:T(8,128)(2,1)S(1)}, u32[]{:S(2)}, u32[]{:S(2)}) collective-permute-start(bf16[400,128]{1,0:T(8,128)(2,1)S(1)} %get-tuple-element.72), channel_id=1, source_target_pairs={{0,50},{1,51},{2,0},{3,1},{4,54},{5,55},{6,4},{7,5},{8,58},{9,59},... | collective-permute-start | bytes 307208 | tf_op jit(solution)/shard_map/ppermute | solution.py:25
  121.3 12.2 %collective-permute-start.13 = (bf16[400,128]{1,0:T(8,128)(2,1)S(1)}, bf16[400,128]{1,0:T(8,128)(2,1)S(1)}, u32[]{:S(2)}, u32[]{:S(2)}) collective-permute-start(bf16[400,128]{1,0:T(8,128)(2,1)S(1)} %get-tuple-element.73), channel_id=1, source_target_pairs={{0,16},{1,17},{2,18},{3,19},{4,20},{5,21},{6,22},{7,23},{8,24},{9,... | collective-permute-start | bytes 307208 | tf_op jit(solution)/shard_map/ppermute | solution.py:25
  121.3 12.2 %collective-permute-start.14 = (bf16[400,128]{1,0:T(8,128)(2,1)S(1)}, bf16[400,128]{1,0:T(8,128)(2,1)S(1)}, u32[]{:S(2)}, u32[]{:S(2)}) collective-permute-start(bf16[400,128]{1,0:T(8,128)(2,1)S(1)} %get-tuple-element.74), channel_id=1, source_target_pairs={{0,48},{1,49},{2,50},{3,51},{4,52},{5,53},{6,54},{7,55},{8,56},{9,... | collective-permute-start | bytes 307208 | tf_op jit(solution)/shard_map/ppermute | solution.py:25
  125.6 10.4 %collective-permute-start.15 = (bf16[400,128]{1,0:T(8,128)(2,1)S(1)}, bf16[400,128]{1,0:T(8,128)(2,1)S(1)}, u32[]{:S(2)}, u32[]{:S(2)}) collective-permute-start(bf16[400,128]{1,0:T(8,128)(2,1)S(1)} %get-tuple-element.75), channel_id=1, source_target_pairs={{0,18},{1,19},{2,32},{3,33},{4,22},{5,23},{6,36},{7,37},{8,26},{9,... | collective-permute-start | bytes 307208 | tf_op jit(solution)/shard_map/ppermute | solution.py:25
  125.6 12.2 %collective-permute-start.16 = (bf16[400,128]{1,0:T(8,128)(2,1)S(1)}, bf16[400,128]{1,0:T(8,128)(2,1)S(1)}, u32[]{:S(2)}, u32[]{:S(2)}) collective-permute-start(bf16[400,128]{1,0:T(8,128)(2,1)S(1)} %get-tuple-element.76), channel_id=1, source_target_pairs={{0,34},{1,35},{2,48},{3,49},{4,38},{5,39},{6,52},{7,53},{8,42},{9,... | collective-permute-start | bytes 307208 | tf_op jit(solution)/shard_map/ppermute | solution.py:25
  130.7 11.4 %collective-permute-start.17 = (bf16[400,128]{1,0:T(8,128)(2,1)S(1)}, bf16[400,128]{1,0:T(8,128)(2,1)S(1)}, u32[]{:S(2)}, u32[]{:S(2)}) collective-permute-start(bf16[400,128]{1,0:T(8,128)(2,1)S(1)} %get-tuple-element.77), channel_id=1, source_target_pairs={{0,32},{1,33},{2,34},{3,35},{4,36},{5,37},{6,38},{7,39},{8,40},{9,... | collective-permute-start | bytes 307208 | tf_op jit(solution)/shard_map/ppermute | solution.py:25
  142.0 22.7 %collective-permute-start.23 = (f32[112,384]{1,0:T(8,128)S(1)}, f32[112,384]{1,0:T(8,128)S(1)}, u32[]{:S(2)}, u32[]{:S(2)}) collective-permute-start(f32[112,384]{1,0:T(8,128)S(1)} %get-tuple-element.101), channel_id=1, source_target_pairs={{0,64},{1,65},{2,66},{3,67},{4,68},{5,69},{6,70},{7,71},{8,72},{9,... | collective-permute-start | bytes 516104 | tf_op jit(solution)/shard_map/ppermute | solution.py:25
  145.7 10.1 %collective-permute-start.21 = (f32[128,128]{1,0:T(8,128)S(1)}, f32[128,128]{1,0:T(8,128)S(1)}, u32[]{:S(2)}, u32[]{:S(2)}) collective-permute-start(f32[128,128]{1,0:T(8,128)S(1)} %get-tuple-element.98), channel_id=1, source_target_pairs={{0,1},{1,2},{2,3},{3,0},{4,16},{5,17},{6,18},{7,19},{8,32},{9,33},... | collective-permute-start | bytes 196616 | tf_op jit(solution)/shard_map/ppermute | solution.py:25
  152.5 11.0 %collective-permute-start.22 = (f32[128,128]{1,0:T(8,128)S(1)}, f32[128,128]{1,0:T(8,128)S(1)}, u32[]{:S(2)}, u32[]{:S(2)}) collective-permute-start(f32[128,128]{1,0:T(8,128)S(1)} %get-tuple-element.99), channel_id=1, source_target_pairs={{0,0},{1,1},{2,2},{3,3},{4,18},{5,19},{6,16},{7,17},{8,34},{9,35},... | collective-permute-start | bytes 196616 | tf_op jit(solution)/shard_map/ppermute | solution.py:25

commit v3 on v1

--- a/solution.py
+++ b/solution.py
@@ -14,7 +14,6 @@
 PLACES = list(itertools.product(*(range(n) for n in SIZES)))
 STEPS = (1, 3, 2)
 Z_STEPS = (1, 7, 2, 6, 3, 5, 4)
-FLOPS = 4_000_000_000
 
 
 def number(place):
@@ -64,7 +63,7 @@
     )
 
 
-def run(body, outs, scratch, flops, *args):
+def run(body, outs, scratch, *args):
     smem, vmem = pl.BlockSpec(memory_space=pltpu.SMEM), pl.BlockSpec(memory_space=pltpu.VMEM)
     return pl.pallas_call(
         body,
@@ -72,9 +71,7 @@
         in_specs=[smem] + [vmem] * (len(args) - 1),
         out_specs=[vmem] * len(outs),
         scratch_shapes=[pltpu.VMEM(shape, dtype) for shape, dtype in scratch],
-        cost_estimate=pl.CostEstimate(
-            flops=flops, bytes_accessed=sum(a.size * a.dtype.itemsize for a in args), transcendentals=0
-        ),
+        cost_estimate=pl.CostEstimate(flops=1000, bytes_accessed=1000, transcendentals=0),
         compiler_params=pltpu.CompilerParams(vmem_limit_bytes=48 * 1024 * 1024),
     )(*args)
 
@@ -401,16 +398,15 @@
     window = [((rows, WINDOW), BF16), ((512, 512), BF16), ((512, 128), F32)]
     half_part, whole_part = ((HALF_ROWS + 16, WINDOW), BF16), ((BLOCK + 16, WINDOW), BF16)
     over_x = lambda s, v: send(v, lambda x, zh, y, zl, core: (x + s, zh, y, zl, core))
-    far_1, far_3 = run(right_far, [half_part] * 2, window, FLOPS, at, gradient)
+    far_1, far_3 = run(right_far, [half_part] * 2, window, at, gradient)
     far_1, far_3 = over_x(1, far_1), over_x(3, far_3)
     near, far, far_1, far_3 = barrier((near, far, far_1, far_3))
     far = send(far, lambda x, zh, y, zl, core: (x, 2 * core + zh % 2, y, zl, zh // 2))
     add = lambda s, v: run(
-        functools.partial(right_near, s), [whole_part], window + [((BLOCK, 256), F32)], FLOPS, at, gradient, v
+        functools.partial(right_near, s), [whole_part], window + [((BLOCK, 256), F32)], at, gradient, v
     )[0]
     code_1, code_3 = add(1, far_1), add(3, far_3)
     right_1, right_3 = over_x(1, code_1), over_x(3, code_3)
-    near, far, right_1, right_3 = barrier((near, far, right_1, right_3))
 
     swap = lambda x, zh, y, zl, core: (x, zh, y, zl, 1 - core)
     far_2, near_2 = send(far, swap), send(near, swap)
@@ -420,14 +416,13 @@
         right_second,
         [(piece, BF16)] * 3 + [(piece, F32)],
         window + [((512, WINDOW), F32), ((640, 512), F32)],
-        FLOPS,
         at,
         gradient,
         right_1,
         right_3,
     )
     over_z = lambda s, v: send(v, lambda x, zh, y, zl, core: (x, zh + s, y, zl, core))
-    right_2 = over_z(2, code_2)
+    right_1, right_3 = over_z(1, code_1), over_z(3, code_3)
 
     far, near, far_2, near_2, _ = barrier((far, near, far_2, near_2, code_1))
     packed = (ROWS + 16, 256)
@@ -435,7 +430,6 @@
         left_first,
         [(packed, BF16)] * 3 + [((ROWS, 256), F32), ((16, SUB), F32)],
         [((2048, half), BF16), ((256, half), BF16), ((2048, SUB), F32), ((16, SUB), F32)],
-        FLOPS,
         at,
         far,
         near,
@@ -444,16 +438,15 @@
     )
     over_y = lambda s, v: send(v, lambda x, zh, y, zl, core: (x, zh, y + s, zl, core))
     left_1, left_3 = over_y(1, left_1), over_y(3, left_3)
-    left_1, left_3, left_2, right_2, code_1, code_3 = barrier((left_1, left_3, left_2, right_2, code_1, code_3))
-    left_2, right_1, right_3 = over_y(2, left_2), over_z(1, code_1), over_z(3, code_3)
     left_2, right_1, right_3 = barrier((left_2, right_1, right_3))
+    left_1, left_3, code_2, right_1, right_3 = barrier((left_1, left_3, code_2, right_1, right_3))
+    left_2, right_2 = over_y(2, left_2), over_z(2, code_2)
 
     piece = (400, SUB)
     codes = run(
         left_second,
         [(piece, BF16)] * 7 + [(piece, F32)],
         [((ROWS, 256), F32), ((4, 16, SUB), F32)] + [((16, SUB), F32)] * 3,
-        FLOPS,
         at,
         left_own,
         norms,
@@ -462,35 +455,33 @@
         left_2,
     )
     arrived = [send(code, along_z(s)) for s, code in zip(Z_STEPS, codes)]
-    right_1, right_3, _ = barrier((right_1, right_3, arrived[0]))
+    right_1, right_3, _ = barrier((right_1, right_3, codes))
 
     right_base, image = run(
         functools.partial(right_third, 1.0 / (rows * 16)),
         [((CHUNK, WINDOW), F32), ((CHUNK, IMAGE), F32)],
         [((1024, 128), F32), ((11, 128), F32)],
-        FLOPS,
         at,
         right_own,
         right_1,
         right_3,
         right_2,
     )
+    arrived, image = barrier((arrived, image))
     image = over_x(1, image)
-    right_gram = run(right_last, [((CHUNK, width), F32)], [], FLOPS, at, right_base, image)[0]
-
-    arrived, right_gram = barrier((arrived, right_gram))
+    right_gram = run(right_last, [((CHUNK, width), F32)], [], at, right_base, image)[0]
+
     square = ((SUB, SUB), F32)
     base, more, same, other = run(
         functools.partial(left_third, 1.0 / (width * 16)),
         [((256, SUB), F32), square, square, square],
         [((384, SUB), F32)],
-        FLOPS,
         at,
         codes[7],
         *arrived,
     )
     same, other = send(same, mirror(0)), send(other, mirror(1))
-    left_gram = run(left_last, [((512, SUB), F32)], [], FLOPS, at, base, more, same, other)[0]
+    left_gram = run(left_last, [((512, SUB), F32)], [], at, base, more, same, other)[0]
     return (left_gram, right_gram)
 
 

time: 185 us -> 170 us (0.919)
  the two profiles are of different devices: /device:TPU:20 before, /device:TPU:25 now
where the time goes in v3:
time: 170 us
  waiting for transfers between devices  84.5 us (50%)
  starting transfers between devices  52.4 us (31%)
  Pallas kernels  27.7 us (16%)
  local copies, waits for them, and re-layouts  4.37 us (3%)
    ppermute x24, waiting for transfers between devices, send(): lax.ppermute(array, ('row', 'col'), [(number(p), number(to(*p))) for p in...  84.5 us
    ppermute x24, starting transfers between devices, send(): lax.ppermute(array, ('row', 'col'), [(number(p), number(to(*p))) for p in...  52.4 us
    pallas_call x10, Pallas kernels, run(): pl.pallas_call(body, out_shape=[jax.ShapeDtypeStruct(shape, dtype) for sh...  27.7 us
  transfers between devices with their start and end apart: 24, of which 16 were waited for; matrix products, arithmetic and copies ran while one was open for 0% of the time, Pallas kernels for 15%

profile of v3, /device:TPU:25, one launch (start us, length us, event | category | flops | bytes accessed | tf_op | source)
XLA Modules:
  0.0 169.8 jit_solution(704098095558547907)
XLA Ops:
  0.7 3.0 %constant_dynamic-slice_fusion = (bf16[512,896]{1,0:T(8,128)(2,1)}, bf16[512,896]{1,0:T(8,128)(2,1)}) fusion(bf16[512,1792]{1,0:T(8,128)(2,1)} %g_ref.3, s32[]{:T(128)S(6)} %select_n.48, s32[]{:T(128)S(6)} %select_n.46), kind=kLoop, calls=%fused_computation | loop fusion | bytes 3670024 | tf_op jit(solution)/shard_map/dynamic_slice | solution.py:394
  3.7 6.6 %collective-permute-start = (bf16[512,896]{1,0:T(8,128)(2,1)}, bf16[512,896]{1,0:T(8,128)(2,1)S(1)}, u32[]{:S(2)}, u32[]{:S(2)}) collective-permute-start(bf16[512,896]{1,0:T(8,128)(2,1)} %get-tuple-element.56), channel_id=1, source_target_pairs={{0,16},{1,48},{2,18},{3,50},{4,20},{5,52},{6,22},{7,54},{8,24},{9,... | collective-permute-start | bytes 2752520 | tf_op jit(solution)/shard_map/ppermute | solution.py:25
  10.4 1.9 %shard_map.30 = (bf16[240,1408]{1,0:T(8,128)(2,1)S(1)}, bf16[240,1408]{1,0:T(8,128)(2,1)S(1)}) custom-call(s32[8]{0:T(128)S(1)} %stack.26.at_ref, bf16[512,1792]{1,0:T(8,128)(2,1)S(1)} %copy-done), custom_call_target="tpu_custom_call" | custom-call | flops 1000 | bytes 1000 | tf_op jit(solution)/shard_map/pallas_call | solution.py:68
  13.6 1.5 collective-permute-start.2
  15.0 13.4 %collective-permute-done.1.in_ref = bf16[240,1408]{1,0:T(8,128)(2,1)S(1)} collective-permute-done((bf16[240,1408]{1,0:T(8,128)(2,1)S(1)}, bf16[240,1408]{1,0:T(8,128)(2,1)S(1)}, u32[]{:S(2)}, u32[]{:S(2)}) %collective-permute-start.1) | collective-permute-done | bytes 675872 | tf_op jit(solution)/shard_map/ppermute | solution.py:25
  28.7 2.1 %collective-permute-done.near = bf16[512,896]{1,0:T(8,128)(2,1)S(1)} collective-permute-done((bf16[512,896]{1,0:T(8,128)(2,1)}, bf16[512,896]{1,0:T(8,128)(2,1)S(1)}, u32[]{:S(2)}, u32[]{:S(2)}) %collective-permute-start) | collective-permute-done | bytes 917536 | tf_op jit(solution)/shard_map/ppermute | solution.py:25
  30.8 7.1 %collective-permute-start.3 = (bf16[512,896]{1,0:T(8,128)(2,1)S(1)}, bf16[512,896]{1,0:T(8,128)(2,1)S(1)}, u32[]{:S(2)}, u32[]{:S(2)}) collective-permute-start(bf16[512,896]{1,0:T(8,128)(2,1)S(1)} %copy-done.2), channel_id=1, source_target_pairs={{0,0},{1,32},{2,2},{3,34},{4,4},{5,36},{6,6},{7,38},{8,8},{9,40},{... | collective-permute-start | bytes 2752520 | tf_op jit(solution)/shard_map/ppermute | solution.py:25
  38.0 2.6 %shard_map.32 = bf16[464,1408]{1,0:T(8,128)(2,1)S(1)} custom-call(s32[8]{0:T(128)S(1)} %stack.26.at_ref, bf16[512,1792]{1,0:T(8,128)(2,1)S(1)} %copy-done, bf16[240,1408]{1,0:T(8,128)(2,1)S(1)} %collective-permute-done.2.in_ref), custom_call_target="tpu_custom_call" | custom-call | flops 1000 | bytes 1000 | tf_op jit(solution)/shard_map/pallas_call | solution.py:68
  40.5 2.5 %collective-permute-start.7 = (bf16[464,1408]{1,0:T(8,128)(2,1)S(1)}, bf16[464,1408]{1,0:T(8,128)(2,1)S(1)}, u32[]{:S(2)}, u32[]{:S(2)}) collective-permute-start(bf16[464,1408]{1,0:T(8,128)(2,1)S(1)} %shard_map.32), channel_id=1, source_target_pairs={{0,192},{1,193},{2,194},{3,195},{4,196},{5,197},{6,198},{7,199},{8... | collective-permute-start | bytes 3919880 | tf_op jit(solution)/shard_map/ppermute | solution.py:25
  43.1 2.5 %shard_map.31 = bf16[464,1408]{1,0:T(8,128)(2,1)S(1)} custom-call(s32[8]{0:T(128)S(1)} %stack.26.at_ref, bf16[512,1792]{1,0:T(8,128)(2,1)S(1)} %copy-done, bf16[240,1408]{1,0:T(8,128)(2,1)S(1)} %collective-permute-done.1.in_ref), custom_call_target="tpu_custom_call" | custom-call | flops 1000 | bytes 1000 | tf_op jit(solution)/shard_map/pallas_call | solution.py:68
  45.8 6.1 %collective-permute-done.3.far = bf16[512,896]{1,0:T(8,128)(2,1)S(1)} collective-permute-done((bf16[512,896]{1,0:T(8,128)(2,1)S(1)}, bf16[512,896]{1,0:T(8,128)(2,1)S(1)}, u32[]{:S(2)}, u32[]{:S(2)}) %collective-permute-start.3) | collective-permute-done | bytes 917536 | tf_op jit(solution)/shard_map/ppermute | solution.py:25
  51.8 12.2 %collective-permute-done.7.in_3 = bf16[464,1408]{1,0:T(8,128)(2,1)S(1)} collective-permute-done((bf16[464,1408]{1,0:T(8,128)(2,1)S(1)}, bf16[464,1408]{1,0:T(8,128)(2,1)S(1)}, u32[]{:S(2)}, u32[]{:S(2)}) %collective-permute-start.7) | collective-permute-done | bytes 1306656 | tf_op jit(solution)/shard_map/ppermute | solution.py:25
  64.0 6.0 %collective-permute-done.6.in_1 = bf16[464,1408]{1,0:T(8,128)(2,1)S(1)} collective-permute-done((bf16[464,1408]{1,0:T(8,128)(2,1)S(1)}, bf16[464,1408]{1,0:T(8,128)(2,1)S(1)}, u32[]{:S(2)}, u32[]{:S(2)}) %collective-permute-start.6) | collective-permute-done | bytes 1306656 | tf_op jit(solution)/shard_map/ppermute | solution.py:25
  70.0 5.5 %shard_map.33 = (bf16[112,1920]{1,0:T(8,128)(2,1)S(1)}, bf16[112,1920]{1,0:T(8,128)(2,1)S(1)}, bf16[112,1920]{1,0:T(8,128)(2,1)S(1)}, f32[112,1920]{1,0:T(8,128)S(1)}) custom-call(s32[8]{0:T(128)S(1)} %stack.26.at_ref, bf16[512,1792]{1,0:T(8,128)(2,1)} %g_ref.3, bf16[464,1408]{1,0:T(8,128)(2,1)S(1)} %collective-permute-done.6.in_1, ...), custom_call_target="tpu_custom_call" | custom-call | flops 1000 | bytes 1000 | tf_op jit(solution)/shard_map/pallas_call | solution.py:68
  75.6 2.4 %collective-permute-start.10 = (bf16[112,1920]{1,0:T(8,128)(2,1)S(1)}, bf16[112,1920]{1,0:T(8,128)(2,1)S(1)}, u32[]{:S(2)}, u32[]{:S(2)}) collective-permute-start(bf16[112,1920]{1,0:T(8,128)(2,1)S(1)} %get-tuple-element.65), channel_id=1, source_target_pairs={{0,16},{1,17},{2,18},{3,19},{4,20},{5,21},{6,22},{7,23},{8,24},{9,... | collective-permute-start | bytes 1290248 | tf_op jit(solution)/shard_map/ppermute | solution.py:25
  77.9 5.9 %shard_map.34 = (bf16[1168,256]{1,0:T(8,128)(2,1)S(1)}, bf16[1168,256]{1,0:T(8,128)(2,1)S(1)}, bf16[1168,256]{1,0:T(8,128)(2,1)S(1)}, f32[1152,256]{1,0:T(8,128)}, f32[16,128]{1,0:T(8,128)S(1)}) custom-call(s32[8]{0:T(128)S(1)} %stack.26.at_ref, bf16[512,896]{1,0:T(8,128)(2,1)S(1)} %collective-permute-done.3.far, ...), custom_call_target="tpu_custom_call" | custom-call | flops 1000 | bytes 1000 | tf_op jit(solution)/shard_map/pallas_call | solution.py:68
  83.8 1.5 collective-permute-start.9
  85.3 8.0 %collective-permute-done.11.in_3 = bf16[112,1920]{1,0:T(8,128)(2,1)S(1)} collective-permute-done((bf16[112,1920]{1,0:T(8,128)(2,1)S(1)}, bf16[112,1920]{1,0:T(8,128)(2,1)S(1)}, u32[]{:S(2)}, u32[]{:S(2)}) %collective-permute-start.11) | collective-permute-done | bytes 430112 | tf_op jit(solution)/shard_map/ppermute | solution.py:25
  94.2 4.6 %collective-permute-done.8.in_1 = bf16[1168,256]{1,0:T(8,128)(2,1)S(1)} collective-permute-done((bf16[1168,256]{1,0:T(8,128)(2,1)S(1)}, bf16[1168,256]{1,0:T(8,128)(2,1)S(1)}, u32[]{:S(2)}, u32[]{:S(2)}) %collective-permute-start.8) | collective-permute-done | bytes 598048 | tf_op jit(solution)/shard_map/ppermute | solution.py:25
  100.1 9.3 %collective-permute-done.12.in_2 = bf16[1168,256]{1,0:T(8,128)(2,1)S(1)} collective-permute-done((bf16[1168,256]{1,0:T(8,128)(2,1)S(1)}, bf16[1168,256]{1,0:T(8,128)(2,1)S(1)}, u32[]{:S(2)}, u32[]{:S(2)}) %collective-permute-start.12) | collective-permute-done | bytes 598048 | tf_op jit(solution)/shard_map/ppermute | solution.py:25
  110.7 2.7 %shard_map.35 = (bf16[400,128]{1,0:T(8,128)(2,1)S(1)}, bf16[400,128]{1,0:T(8,128)(2,1)S(1)}, bf16[400,128]{1,0:T(8,128)(2,1)S(1)}, bf16[400,128]{1,0:T(8,128)(2,...) custom-call(s32[8]{0:T(128)S(1)} %stack.26.at_ref, ...), custom_call_target="tpu_custom_call" | custom-call | flops 1000 | bytes 1000 | tf_op jit(solution)/shard_map/pallas_call | solution.py:68
  113.3 4.5 %collective-permute-start.13 = (bf16[400,128]{1,0:T(8,128)(2,1)S(1)}, bf16[400,128]{1,0:T(8,128)(2,1)S(1)}, u32[]{:S(2)}, u32[]{:S(2)}) collective-permute-start(bf16[400,128]{1,0:T(8,128)(2,1)S(1)} %get-tuple-element.83), channel_id=1, source_target_pairs={{0,2},{1,3},{2,16},{3,17},{4,6},{5,7},{6,20},{7,21},{8,10},{9,11},... | collective-permute-start | bytes 307208 | tf_op jit(solution)/shard_map/ppermute | solution.py:25
  118.4 2.7 %collective-permute-start.15 = (bf16[400,128]{1,0:T(8,128)(2,1)S(1)}, bf16[400,128]{1,0:T(8,128)(2,1)S(1)}, u32[]{:S(2)}, u32[]{:S(2)}) collective-permute-start(bf16[400,128]{1,0:T(8,128)(2,1)S(1)} %get-tuple-element.85), channel_id=1, source_target_pairs={{0,16},{1,17},{2,18},{3,19},{4,20},{5,21},{6,22},{7,23},{8,24},{9,... | collective-permute-start | bytes 307208 | tf_op jit(solution)/shard_map/ppermute | solution.py:25
  121.9 9.7 %collective-permute-done.13.refs_1_ = bf16[400,128]{1,0:T(8,128)(2,1)S(1)} collective-permute-done((bf16[400,128]{1,0:T(8,128)(2,1)S(1)}, bf16[400,128]{1,0:T(8,128)(2,1)S(1)}, u32[]{:S(2)}, u32[]{:S(2)}) %collective-permute-start.13) | collective-permute-done | bytes 102432 | tf_op jit(solution)/shard_map/ppermute | solution.py:25
  131.6 4.5 %collective-permute-start.18 = (bf16[400,128]{1,0:T(8,128)(2,1)S(1)}, bf16[400,128]{1,0:T(8,128)(2,1)S(1)}, u32[]{:S(2)}, u32[]{:S(2)}) collective-permute-start(bf16[400,128]{1,0:T(8,128)(2,1)S(1)} %get-tuple-element.88), channel_id=1, source_target_pairs={{0,34},{1,35},{2,48},{3,49},{4,38},{5,39},{6,52},{7,53},{8,42},{9,... | collective-permute-start | bytes 307208 | tf_op jit(solution)/shard_map/ppermute | solution.py:25
  136.1 2.5 %shard_map.36 = (f32[112,1408]{1,0:T(8,128)S(1)}, f32[112,384]{1,0:T(8,128)S(1)}) custom-call(s32[8]{0:T(128)S(1)} %stack.26.at_ref, f32[112,1920]{1,0:T(8,128)S(1)} %get-tuple-element.90.own_ref, bf16[112,1920]{1,0:T(8,128)(2,1)S(1)} %collective-permute-done.10.in_1, bf16[112,1920]{1,0:T(8,128)(2,1)S(1)} %collective-permute-done.11.in_3, ...), custom_call_target="tpu_custom_call" | custom-call | flops 1000 | bytes 1000 | tf_op jit(solution)/shard_map/pallas_call | solution.py:68
  139.3 5.3 %collective-permute-done.19.refs_7_ = bf16[400,128]{1,0:T(8,128)(2,1)S(1)} collective-permute-done((bf16[400,128]{1,0:T(8,128)(2,1)S(1)}, bf16[400,128]{1,0:T(8,128)(2,1)S(1)}, u32[]{:S(2)}, u32[]{:S(2)}) %collective-permute-start.19) | collective-permute-done | bytes 102432 | tf_op jit(solution)/shard_map/ppermute | solution.py:25
  144.5 6.6 %collective-permute-start.23 = (f32[112,384]{1,0:T(8,128)S(1)}, f32[112,384]{1,0:T(8,128)S(1)}, u32[]{:S(2)}, u32[]{:S(2)}) collective-permute-start(f32[112,384]{1,0:T(8,128)S(1)} %get-tuple-element.109), channel_id=1, source_target_pairs={{0,64},{1,65},{2,66},{3,67},{4,68},{5,69},{6,70},{7,71},{8,72},{9,... | collective-permute-start | bytes 516104 | tf_op jit(solution)/shard_map/ppermute | solution.py:25
  152.7 8.6 %collective-permute-start.22 = (f32[128,128]{1,0:T(8,128)S(1)}, f32[128,128]{1,0:T(8,128)S(1)}, u32[]{:S(2)}, u32[]{:S(2)}) collective-permute-start(f32[128,128]{1,0:T(8,128)S(1)} %get-tuple-element.107), channel_id=1, source_target_pairs={{0,0},{1,1},{2,2},{3,3},{4,18},{5,19},{6,16},{7,17},{8,34},{9,35},... | collective-permute-start | bytes 196616 | tf_op jit(solution)/shard_map/ppermute | solution.py:25
  161.3 1.6 collective-permute-done.21.same_ref
  162.9 4.1 %collective-permute-done.22.other_ref = f32[128,128]{1,0:T(8,128)S(1)} collective-permute-done((f32[128,128]{1,0:T(8,128)S(1)}, f32[128,128]{1,0:T(8,128)S(1)}, u32[]{:S(2)}, u32[]{:S(2)}) %collective-permute-start.22) | collective-permute-done | bytes 65568 | tf_op jit(solution)/shard_map/ppermute | solution.py:25
  168.3 1.5 shard_map.39
  (34 shorter events, 10.3 us)
Async XLA Ops:
  0.7 9.7 %copy-start = (bf16[512,1792]{1,0:T(8,128)(2,1)S(1)}, bf16[512,1792]{1,0:T(8,128)(2,1)}, u32[]{:S(2)}) copy-start(bf16[512,1792]{1,0:T(8,128)(2,1)} %g_ref.3) | copy-start | bytes 5505028
  3.7 27.1 %collective-permute-start = (bf16[512,896]{1,0:T(8,128)(2,1)}, bf16[512,896]{1,0:T(8,128)(2,1)S(1)}, u32[]{:S(2)}, u32[]{:S(2)}) collective-permute-start(bf16[512,896]{1,0:T(8,128)(2,1)} %get-tuple-element.56), channel_id=1, source_target_pairs={{0,16},{1,48},{2,18},{3,50},{4,20},{5,52},{6,22},{7,54},{8,24},{9,... | collective-permute-start | bytes 2752520 | tf_op jit(solution)/shard_map/ppermute | solution.py:25
  10.4 20.4 %copy-start.2 = (bf16[512,896]{1,0:T(8,128)(2,1)S(1)}, bf16[512,896]{1,0:T(8,128)(2,1)}, u32[]{:S(2)}) copy-start(bf16[512,896]{1,0:T(8,128)(2,1)} %get-tuple-element.61) | copy-start | bytes 2752516
  12.3 16.1 %collective-permute-start.1 = (bf16[240,1408]{1,0:T(8,128)(2,1)S(1)}, bf16[240,1408]{1,0:T(8,128)(2,1)S(1)}, u32[]{:S(2)}, u32[]{:S(2)}) collective-permute-start(bf16[240,1408]{1,0:T(8,128)(2,1)S(1)} %get-tuple-element.59), channel_id=1, source_target_pairs={{0,64},{1,65},{2,66},{3,67},{4,68},{5,69},{6,70},{7,71},{8,72},{9,... | collective-permute-start | bytes 2027528 | tf_op jit(solution)/shard_map/ppermute | solution.py:25
  13.6 15.2 %collective-permute-start.2 = (bf16[240,1408]{1,0:T(8,128)(2,1)S(1)}, bf16[240,1408]{1,0:T(8,128)(2,1)S(1)}, u32[]{:S(2)}, u32[]{:S(2)}) collective-permute-start(bf16[240,1408]{1,0:T(8,128)(2,1)S(1)} %get-tuple-element.60), channel_id=1, source_target_pairs={{0,192},{1,193},{2,194},{3,195},{4,196},{5,197},{6,198},{7,199},{8... | collective-permute-start | bytes 2027528 | tf_op jit(solution)/shard_map/ppermute | solution.py:25
  30.8 21.0 %collective-permute-start.3 = (bf16[512,896]{1,0:T(8,128)(2,1)S(1)}, bf16[512,896]{1,0:T(8,128)(2,1)S(1)}, u32[]{:S(2)}, u32[]{:S(2)}) collective-permute-start(bf16[512,896]{1,0:T(8,128)(2,1)S(1)} %copy-done.2), channel_id=1, source_target_pairs={{0,0},{1,32},{2,2},{3,34},{4,4},{5,36},{6,6},{7,38},{8,8},{9,40},{... | collective-permute-start | bytes 2752520 | tf_op jit(solution)/shard_map/ppermute | solution.py:25
  40.5 23.4 %collective-permute-start.7 = (bf16[464,1408]{1,0:T(8,128)(2,1)S(1)}, bf16[464,1408]{1,0:T(8,128)(2,1)S(1)}, u32[]{:S(2)}, u32[]{:S(2)}) collective-permute-start(bf16[464,1408]{1,0:T(8,128)(2,1)S(1)} %shard_map.32), channel_id=1, source_target_pairs={{0,192},{1,193},{2,194},{3,195},{4,196},{5,197},{6,198},{7,199},{8... | collective-permute-start | bytes 3919880 | tf_op jit(solution)/shard_map/ppermute | solution.py:25
  45.6 24.4 %collective-permute-start.6 = (bf16[464,1408]{1,0:T(8,128)(2,1)S(1)}, bf16[464,1408]{1,0:T(8,128)(2,1)S(1)}, u32[]{:S(2)}, u32[]{:S(2)}) collective-permute-start(bf16[464,1408]{1,0:T(8,128)(2,1)S(1)} %shard_map.31), channel_id=1, source_target_pairs={{0,64},{1,65},{2,66},{3,67},{4,68},{5,69},{6,70},{7,71},{8,72},{9,... | collective-permute-start | bytes 3919880 | tf_op jit(solution)/shard_map/ppermute | solution.py:25
  45.7 32.3 %collective-permute-start.5 = (bf16[512,896]{1,0:T(8,128)(2,1)S(1)}, bf16[512,896]{1,0:T(8,128)(2,1)S(1)}, u32[]{:S(2)}, u32[]{:S(2)}) collective-permute-start(bf16[512,896]{1,0:T(8,128)(2,1)S(1)} %collective-permute-done.near), channel_id=1, source_target_pairs={{0,1},{1,0},{2,3},{3,2},{4,5},{5,4},{6,7},{7,6},{8,9},{9,8},{10,11... | collective-permute-start | bytes 2752520 | tf_op jit(solution)/shard_map/ppermute | solution.py:25
  51.8 26.1 %collective-permute-start.4 = (bf16[512,896]{1,0:T(8,128)(2,1)S(1)}, bf16[512,896]{1,0:T(8,128)(2,1)S(1)}, u32[]{:S(2)}, u32[]{:S(2)}) collective-permute-start(bf16[512,896]{1,0:T(8,128)(2,1)S(1)} %collective-permute-done.3.far), channel_id=1, source_target_pairs={{0,1},{1,0},{2,3},{3,2},{4,5},{5,4},{6,7},{7,6},{8,9},{9,8},{10,11... | collective-permute-start | bytes 2752520 | tf_op jit(solution)/shard_map/ppermute | solution.py:25
  75.5 17.8 %collective-permute-start.11 = (bf16[112,1920]{1,0:T(8,128)(2,1)S(1)}, bf16[112,1920]{1,0:T(8,128)(2,1)S(1)}, u32[]{:S(2)}, u32[]{:S(2)}) collective-permute-start(bf16[112,1920]{1,0:T(8,128)(2,1)S(1)} %get-tuple-element.76), channel_id=1, source_target_pairs={{0,48},{1,49},{2,50},{3,51},{4,52},{5,53},{6,54},{7,55},{8,56},{9,... | collective-permute-start | bytes 1290248 | tf_op jit(solution)/shard_map/ppermute | solution.py:25
  75.6 17.7 %collective-permute-start.10 = (bf16[112,1920]{1,0:T(8,128)(2,1)S(1)}, bf16[112,1920]{1,0:T(8,128)(2,1)S(1)}, u32[]{:S(2)}, u32[]{:S(2)}) collective-permute-start(bf16[112,1920]{1,0:T(8,128)(2,1)S(1)} %get-tuple-element.65), channel_id=1, source_target_pairs={{0,16},{1,17},{2,18},{3,19},{4,20},{5,21},{6,22},{7,23},{8,24},{9,... | collective-permute-start | bytes 1290248 | tf_op jit(solution)/shard_map/ppermute | solution.py:25
  83.8 15.1 %collective-permute-start.8 = (bf16[1168,256]{1,0:T(8,128)(2,1)S(1)}, bf16[1168,256]{1,0:T(8,128)(2,1)S(1)}, u32[]{:S(2)}, u32[]{:S(2)}) collective-permute-start(bf16[1168,256]{1,0:T(8,128)(2,1)S(1)} %get-tuple-element.72), channel_id=1, source_target_pairs={{0,4},{1,5},{2,6},{3,7},{4,8},{5,9},{6,10},{7,11},{8,12},{9,13},{1... | collective-permute-start | bytes 1794056 | tf_op jit(solution)/shard_map/ppermute | solution.py:25
  83.8 16.3 %collective-permute-start.9 = (bf16[1168,256]{1,0:T(8,128)(2,1)S(1)}, bf16[1168,256]{1,0:T(8,128)(2,1)S(1)}, u32[]{:S(2)}, u32[]{:S(2)}) collective-permute-start(bf16[1168,256]{1,0:T(8,128)(2,1)S(1)} %get-tuple-element.73), channel_id=1, source_target_pairs={{0,12},{1,13},{2,14},{3,15},{4,0},{5,1},{6,2},{7,3},{8,4},{9,5},{1... | collective-permute-start | bytes 1794056 | tf_op jit(solution)/shard_map/ppermute | solution.py:25
  93.3 16.1 %collective-permute-start.12 = (bf16[1168,256]{1,0:T(8,128)(2,1)S(1)}, bf16[1168,256]{1,0:T(8,128)(2,1)S(1)}, u32[]{:S(2)}, u32[]{:S(2)}) collective-permute-start(bf16[1168,256]{1,0:T(8,128)(2,1)S(1)} %get-tuple-element.81), channel_id=1, source_target_pairs={{0,8},{1,9},{2,10},{3,11},{4,12},{5,13},{6,14},{7,15},{8,0},{9,1},... | collective-permute-start | bytes 1794056 | tf_op jit(solution)/shard_map/ppermute | solution.py:25
  100.1 36.0 %collective-permute-start.20 = (bf16[112,1920]{1,0:T(8,128)(2,1)S(1)}, bf16[112,1920]{1,0:T(8,128)(2,1)S(1)}, u32[]{:S(2)}, u32[]{:S(2)}) collective-permute-start(bf16[112,1920]{1,0:T(8,128)(2,1)S(1)} %get-tuple-element.95), channel_id=1, source_target_pairs={{0,32},{1,33},{2,34},{3,35},{4,36},{5,37},{6,38},{7,39},{8,40},{9,... | collective-permute-start | bytes 1290248 | tf_op jit(solution)/shard_map/ppermute | solution.py:25
  109.4 1.3 copy-start.1
  113.3 18.2 %collective-permute-start.13 = (bf16[400,128]{1,0:T(8,128)(2,1)S(1)}, bf16[400,128]{1,0:T(8,128)(2,1)S(1)}, u32[]{:S(2)}, u32[]{:S(2)}) collective-permute-start(bf16[400,128]{1,0:T(8,128)(2,1)S(1)} %get-tuple-element.83), channel_id=1, source_target_pairs={{0,2},{1,3},{2,16},{3,17},{4,6},{5,7},{6,20},{7,21},{8,10},{9,11},... | collective-permute-start | bytes 307208 | tf_op jit(solution)/shard_map/ppermute | solution.py:25
  117.8 13.8 %collective-permute-start.14 = (bf16[400,128]{1,0:T(8,128)(2,1)S(1)}, bf16[400,128]{1,0:T(8,128)(2,1)S(1)}, u32[]{:S(2)}, u32[]{:S(2)}) collective-permute-start(bf16[400,128]{1,0:T(8,128)(2,1)S(1)} %get-tuple-element.84), channel_id=1, source_target_pairs={{0,50},{1,51},{2,0},{3,1},{4,54},{5,55},{6,4},{7,5},{8,58},{9,59},... | collective-permute-start | bytes 307208 | tf_op jit(solution)/shard_map/ppermute | solution.py:25
  118.4 20.2 %collective-permute-start.15 = (bf16[400,128]{1,0:T(8,128)(2,1)S(1)}, bf16[400,128]{1,0:T(8,128)(2,1)S(1)}, u32[]{:S(2)}, u32[]{:S(2)}) collective-permute-start(bf16[400,128]{1,0:T(8,128)(2,1)S(1)} %get-tuple-element.85), channel_id=1, source_target_pairs={{0,16},{1,17},{2,18},{3,19},{4,20},{5,21},{6,22},{7,23},{8,24},{9,... | collective-permute-start | bytes 307208 | tf_op jit(solution)/shard_map/ppermute | solution.py:25
  121.0 17.6 %collective-permute-start.16 = (bf16[400,128]{1,0:T(8,128)(2,1)S(1)}, bf16[400,128]{1,0:T(8,128)(2,1)S(1)}, u32[]{:S(2)}, u32[]{:S(2)}) collective-permute-start(bf16[400,128]{1,0:T(8,128)(2,1)S(1)} %get-tuple-element.86), channel_id=1, source_target_pairs={{0,48},{1,49},{2,50},{3,51},{4,52},{5,53},{6,54},{7,55},{8,56},{9,... | collective-permute-start | bytes 307208 | tf_op jit(solution)/shard_map/ppermute | solution.py:25
  131.6 7.3 %collective-permute-start.17 = (bf16[400,128]{1,0:T(8,128)(2,1)S(1)}, bf16[400,128]{1,0:T(8,128)(2,1)S(1)}, u32[]{:S(2)}, u32[]{:S(2)}) collective-permute-start(bf16[400,128]{1,0:T(8,128)(2,1)S(1)} %get-tuple-element.87), channel_id=1, source_target_pairs={{0,18},{1,19},{2,32},{3,33},{4,22},{5,23},{6,36},{7,37},{8,26},{9,... | collective-permute-start | bytes 307208 | tf_op jit(solution)/shard_map/ppermute | solution.py:25
  131.6 7.7 %collective-permute-start.18 = (bf16[400,128]{1,0:T(8,128)(2,1)S(1)}, bf16[400,128]{1,0:T(8,128)(2,1)S(1)}, u32[]{:S(2)}, u32[]{:S(2)}) collective-permute-start(bf16[400,128]{1,0:T(8,128)(2,1)S(1)} %get-tuple-element.88), channel_id=1, source_target_pairs={{0,34},{1,35},{2,48},{3,49},{4,38},{5,39},{6,52},{7,53},{8,42},{9,... | collective-permute-start | bytes 307208 | tf_op jit(solution)/shard_map/ppermute | solution.py:25
  136.1 8.5 %collective-permute-start.19 = (bf16[400,128]{1,0:T(8,128)(2,1)S(1)}, bf16[400,128]{1,0:T(8,128)(2,1)S(1)}, u32[]{:S(2)}, u32[]{:S(2)}) collective-permute-start(bf16[400,128]{1,0:T(8,128)(2,1)S(1)} %get-tuple-element.89), channel_id=1, source_target_pairs={{0,32},{1,33},{2,34},{3,35},{4,36},{5,37},{6,38},{7,39},{8,40},{9,... | collective-permute-start | bytes 307208 | tf_op jit(solution)/shard_map/ppermute | solution.py:25
  144.5 23.8 %collective-permute-start.23 = (f32[112,384]{1,0:T(8,128)S(1)}, f32[112,384]{1,0:T(8,128)S(1)}, u32[]{:S(2)}, u32[]{:S(2)}) collective-permute-start(f32[112,384]{1,0:T(8,128)S(1)} %get-tuple-element.109), channel_id=1, source_target_pairs={{0,64},{1,65},{2,66},{3,67},{4,68},{5,69},{6,70},{7,71},{8,72},{9,... | collective-permute-start | bytes 516104 | tf_op jit(solution)/shard_map/ppermute | solution.py:25
  152.6 10.3 %collective-permute-start.21 = (f32[128,128]{1,0:T(8,128)S(1)}, f32[128,128]{1,0:T(8,128)S(1)}, u32[]{:S(2)}, u32[]{:S(2)}) collective-permute-start(f32[128,128]{1,0:T(8,128)S(1)} %get-tuple-element.106), channel_id=1, source_target_pairs={{0,1},{1,2},{2,3},{3,0},{4,16},{5,17},{6,18},{7,19},{8,32},{9,33},... | collective-permute-start | bytes 196616 | tf_op jit(solution)/shard_map/ppermute | solution.py:25
  152.7 14.4 %collective-permute-start.22 = (f32[128,128]{1,0:T(8,128)S(1)}, f32[128,128]{1,0:T(8,128)S(1)}, u32[]{:S(2)}, u32[]{:S(2)}) collective-permute-start(f32[128,128]{1,0:T(8,128)S(1)} %get-tuple-element.107), channel_id=1, source_target_pairs={{0,0},{1,1},{2,2},{3,3},{4,18},{5,19},{6,16},{7,17},{8,34},{9,35},... | collective-permute-start | bytes 196616 | tf_op jit(solution)/shard_map/ppermute | solution.py:25

commit v4 on v3

--- a/solution.py
+++ b/solution.py
@@ -13,7 +13,7 @@
 SIZES = (4, 4, 4, 2, 2)
 PLACES = list(itertools.product(*(range(n) for n in SIZES)))
 STEPS = (1, 3, 2)
-Z_STEPS = (1, 7, 2, 6, 3, 5, 4)
+Z_STEPS = (4, 3, 5, 2, 6, 1, 7)
 
 
 def number(place):
@@ -163,10 +163,17 @@
         out_ref[:BLOCK, lanes] = raised(part[...], wide(rows, lanes), cols[:, lanes]).astype(BF16)
 
 
-def right_second(at_ref, g_ref, in_1, in_3, out_1, out_3, out_2, own_ref, w_ref, l_ref, r_ref, e_ref, t_ref):
+def right_product(at_ref, g_ref, out_ref, norm_ref, w_ref, l_ref, r_ref):
+    d = at_ref[0]
+    fill_window(g_ref, w_ref, l_ref, d)
+    norm_ref[...] = jnp.broadcast_to(column_norms(w_ref), (8, WINDOW))
+    for lanes in PARTS:
+        out_ref[:, lanes] = product(l_ref, w_ref, lanes, d)
+
+
+def right_second(at_ref, p_ref, norm_ref, in_1, in_3, out_1, out_3, out_2, own_ref, r_ref, e_ref, t_ref):
     d, zh = at_ref[0], at_ref[1]
-    fill_window(g_ref, w_ref, l_ref, d)
-    squares, theirs = jnp.square(column_norms(w_ref)), []
+    squares, theirs = jnp.square(norm_ref[0:1, :]), []
     for ref in (in_1, in_3):
         tail = ref[BLOCK:, :].astype(F32)
         norms = tail[0:1] + tail[1:2]
@@ -179,7 +186,7 @@
     e_ref[:64, :] = jnp.zeros((64, WINDOW), F32)
     e_ref[BLOCK:, :] = jnp.zeros((64, WINDOW), F32)
     for lanes in PARTS:
-        part = product(l_ref, w_ref, lanes, d)
+        part = p_ref[:, lanes]
         for ref, their_cols, their_rows in theirs:
             part += root(ref[:BLOCK, lanes].astype(F32), wide(their_rows, lanes), their_cols[:, lanes])
         e_ref[pl.ds(begin, BLOCK), lanes] = raised(part, wide(rows, lanes), cols[:, lanes])
@@ -400,14 +407,20 @@
     over_x = lambda s, v: send(v, lambda x, zh, y, zl, core: (x + s, zh, y, zl, core))
     far_1, far_3 = run(right_far, [half_part] * 2, window, at, gradient)
     far_1, far_3 = over_x(1, far_1), over_x(3, far_3)
-    near, far, far_1, far_3 = barrier((near, far, far_1, far_3))
-    far = send(far, lambda x, zh, y, zl, core: (x, 2 * core + zh % 2, y, zl, zh // 2))
     add = lambda s, v: run(
         functools.partial(right_near, s), [whole_part], window + [((BLOCK, 256), F32)], at, gradient, v
     )[0]
     code_1, code_3 = add(1, far_1), add(3, far_3)
     right_1, right_3 = over_x(1, code_1), over_x(3, code_3)
-
+    near, far, _ = barrier((near, far, code_3))
+    far = send(far, lambda x, zh, y, zl, core: (x, 2 * core + zh % 2, y, zl, zh // 2))
+
+    gradient, _ = barrier((gradient, (code_1, code_3)))
+    product_own, norms_own = run(
+        right_product, [((BLOCK, WINDOW), F32), ((8, WINDOW), F32)], window, at, gradient
+    )
+
+    near, far, product_own = barrier((near, far, product_own))
     swap = lambda x, zh, y, zl, core: (x, zh, y, zl, 1 - core)
     far_2, near_2 = send(far, swap), send(near, swap)
 
@@ -415,9 +428,10 @@
     code_1, code_3, code_2, right_own = run(
         right_second,
         [(piece, BF16)] * 3 + [(piece, F32)],
-        window + [((512, WINDOW), F32), ((640, 512), F32)],
+        [((512, 128), F32), ((512, WINDOW), F32), ((640, 512), F32)],
         at,
-        gradient,
+        product_own,
+        norms_own,
         right_1,
         right_3,
     )

time: 170 us -> 164 us (0.965)
  the two profiles are of different devices: /device:TPU:25 before, /device:TPU:60 now
where the time goes in v4:
time: 164 us
  starting transfers between devices  64.7 us (39%)
  waiting for transfers between devices  62.5 us (38%)
  Pallas kernels  29.9 us (18%)
  local copies, waits for them, and re-layouts  5.84 us (4%)
    ppermute x24, starting transfers between devices, send(): lax.ppermute(array, ('row', 'col'), [(number(p), number(to(*p))) for p in...  64.7 us
    ppermute x24, waiting for transfers between devices, send(): lax.ppermute(array, ('row', 'col'), [(number(p), number(to(*p))) for p in...  62.5 us
    pallas_call x11, Pallas kernels, run(): pl.pallas_call(body, out_shape=[jax.ShapeDtypeStruct(shape, dtype) for sh...  29.9 us
  transfers between devices with their start and end apart: 24, of which 14 were waited for; matrix products, arithmetic and copies ran while one was open for 0% of the time, Pallas kernels for 17%

profile of v4, /device:TPU:60, one launch (start us, length us, event | category | flops | bytes accessed | tf_op | source)
XLA Modules:
  0.0 163.8 jit_solution(9115876051345072075)
XLA Ops:
  0.7 3.0 %constant_dynamic-slice_fusion = (bf16[512,896]{1,0:T(8,128)(2,1)}, bf16[512,896]{1,0:T(8,128)(2,1)}) fusion(bf16[512,1792]{1,0:T(8,128)(2,1)} %g_ref.3, s32[]{:T(128)S(6)} %select_n.48, s32[]{:T(128)S(6)} %select_n.46), kind=kLoop, calls=%fused_computation | loop fusion | bytes 3670024 | tf_op jit(solution)/shard_map/dynamic_slice | solution.py:401
  3.7 3.3 %collective-permute-start = (bf16[512,896]{1,0:T(8,128)(2,1)}, bf16[512,896]{1,0:T(8,128)(2,1)S(1)}, u32[]{:S(2)}, u32[]{:S(2)}) collective-permute-start(bf16[512,896]{1,0:T(8,128)(2,1)} %get-tuple-element.60), channel_id=1, source_target_pairs={{0,16},{1,48},{2,18},{3,50},{4,20},{5,52},{6,22},{7,54},{8,24},{9,... | collective-permute-start | bytes 2752520 | tf_op jit(solution)/shard_map/ppermute | solution.py:25
  7.0 1.9 %shard_map.30 = (bf16[240,1408]{1,0:T(8,128)(2,1)S(1)}, bf16[240,1408]{1,0:T(8,128)(2,1)S(1)}) custom-call(s32[8]{0:T(128)S(1)} %stack.26.at_ref, bf16[512,1792]{1,0:T(8,128)(2,1)S(1)} %copy-done), custom_call_target="tpu_custom_call" | custom-call | flops 1000 | bytes 1000 | tf_op jit(solution)/shard_map/pallas_call | solution.py:68
  11.0 14.7 %collective-permute-done.1.in_ref = bf16[240,1408]{1,0:T(8,128)(2,1)S(1)} collective-permute-done((bf16[240,1408]{1,0:T(8,128)(2,1)S(1)}, bf16[240,1408]{1,0:T(8,128)(2,1)S(1)}, u32[]{:S(2)}, u32[]{:S(2)}) %collective-permute-start.1) | collective-permute-done | bytes 675872 | tf_op jit(solution)/shard_map/ppermute | solution.py:25
  25.7 2.6 %shard_map.31 = bf16[464,1408]{1,0:T(8,128)(2,1)S(1)} custom-call(s32[8]{0:T(128)S(1)} %stack.26.at_ref, bf16[512,1792]{1,0:T(8,128)(2,1)S(1)} %copy-done, bf16[240,1408]{1,0:T(8,128)(2,1)S(1)} %collective-permute-done.1.in_ref), custom_call_target="tpu_custom_call" | custom-call | flops 1000 | bytes 1000 | tf_op jit(solution)/shard_map/pallas_call | solution.py:68
  29.1 2.5 %shard_map.32 = bf16[464,1408]{1,0:T(8,128)(2,1)S(1)} custom-call(s32[8]{0:T(128)S(1)} %stack.26.at_ref, bf16[512,1792]{1,0:T(8,128)(2,1)S(1)} %copy-done, bf16[240,1408]{1,0:T(8,128)(2,1)S(1)} %collective-permute-done.3.in_ref), custom_call_target="tpu_custom_call" | custom-call | flops 1000 | bytes 1000 | tf_op jit(solution)/shard_map/pallas_call | solution.py:68
  31.6 2.5 %collective-permute-start.6 = (bf16[464,1408]{1,0:T(8,128)(2,1)S(1)}, bf16[464,1408]{1,0:T(8,128)(2,1)S(1)}, u32[]{:S(2)}, u32[]{:S(2)}) collective-permute-start(bf16[464,1408]{1,0:T(8,128)(2,1)S(1)} %shard_map.32), channel_id=1, source_target_pairs={{0,64},{1,65},{2,66},{3,67},{4,68},{5,69},{6,70},{7,71},{8,72},{9,... | collective-permute-start | bytes 3919880 | tf_op jit(solution)/shard_map/ppermute | solution.py:25
  34.1 1.6 shard_map.33
  35.7 1.5 copy-done.1
  37.2 20.5 %collective-permute-start.4 = (bf16[512,896]{1,0:T(8,128)(2,1)S(1)}, bf16[512,896]{1,0:T(8,128)(2,1)S(1)}, u32[]{:S(2)}, u32[]{:S(2)}) collective-permute-start(bf16[512,896]{1,0:T(8,128)(2,1)S(1)} %collective-permute-done.2.far), channel_id=1, source_target_pairs={{0,1},{1,0},{2,3},{3,2},{4,5},{5,4},{6,7},{7,6},{8,9},{9,8},{10,11... | collective-permute-start | bytes 2752520 | tf_op jit(solution)/shard_map/ppermute | solution.py:25
  58.5 2.8 %collective-permute-done.7.in_3 = bf16[464,1408]{1,0:T(8,128)(2,1)S(1)} collective-permute-done((bf16[464,1408]{1,0:T(8,128)(2,1)S(1)}, bf16[464,1408]{1,0:T(8,128)(2,1)S(1)}, u32[]{:S(2)}, u32[]{:S(2)}) %collective-permute-start.7) | collective-permute-done | bytes 1306656 | tf_op jit(solution)/shard_map/ppermute | solution.py:25
  61.2 6.1 %shard_map.34 = (bf16[112,1920]{1,0:T(8,128)(2,1)S(1)}, bf16[112,1920]{1,0:T(8,128)(2,1)S(1)}, bf16[112,1920]{1,0:T(8,128)(2,1)S(1)}, f32[112,1920]{1,0:T(8,128)S(1)}) custom-call(s32[8]{0:T(128)S(1)} %stack.26.at_ref, f32[448,1408]{1,0:T(8,128)} %copy-done.1, f32[8,1408]{1,0:T(8,128)S(1)} %get-tuple-element.72.norm_ref, ...), custom_call_target="tpu_custom_call" | custom-call | flops 1000 | bytes 1000 | tf_op jit(solution)/shard_map/pallas_call | solution.py:68
  67.3 6.8 %collective-permute-start.11 = (bf16[112,1920]{1,0:T(8,128)(2,1)S(1)}, bf16[112,1920]{1,0:T(8,128)(2,1)S(1)}, u32[]{:S(2)}, u32[]{:S(2)}) collective-permute-start(bf16[112,1920]{1,0:T(8,128)(2,1)S(1)} %get-tuple-element.84), channel_id=1, source_target_pairs={{0,48},{1,49},{2,50},{3,51},{4,52},{5,53},{6,54},{7,55},{8,56},{9,... | collective-permute-start | bytes 1290248 | tf_op jit(solution)/shard_map/ppermute | solution.py:25
  74.1 5.9 %shard_map.35 = (bf16[1168,256]{1,0:T(8,128)(2,1)S(1)}, bf16[1168,256]{1,0:T(8,128)(2,1)S(1)}, bf16[1168,256]{1,0:T(8,128)(2,1)S(1)}, f32[1152,256]{1,0:T(8,128)}, f32[16,128]{1,0:T(8,128)S(1)}) custom-call(s32[8]{0:T(128)S(1)} %stack.26.at_ref, bf16[512,896]{1,0:T(8,128)(2,1)S(1)} %collective-permute-done.2.far, ...), custom_call_target="tpu_custom_call" | custom-call | flops 1000 | bytes 1000 | tf_op jit(solution)/shard_map/pallas_call | solution.py:68
  80.2 1.8 %collective-permute-start.9 = (bf16[1168,256]{1,0:T(8,128)(2,1)S(1)}, bf16[1168,256]{1,0:T(8,128)(2,1)S(1)}, u32[]{:S(2)}, u32[]{:S(2)}) collective-permute-start(bf16[1168,256]{1,0:T(8,128)(2,1)S(1)} %get-tuple-element.81), channel_id=1, source_target_pairs={{0,12},{1,13},{2,14},{3,15},{4,0},{5,1},{6,2},{7,3},{8,4},{9,5},{1... | collective-permute-start | bytes 1794056 | tf_op jit(solution)/shard_map/ppermute | solution.py:25
  82.0 7.2 %collective-permute-done.11.in_3 = bf16[112,1920]{1,0:T(8,128)(2,1)S(1)} collective-permute-done((bf16[112,1920]{1,0:T(8,128)(2,1)S(1)}, bf16[112,1920]{1,0:T(8,128)(2,1)S(1)}, u32[]{:S(2)}, u32[]{:S(2)}) %collective-permute-start.11) | collective-permute-done | bytes 430112 | tf_op jit(solution)/shard_map/ppermute | solution.py:25
  89.2 3.9 %collective-permute-done.10.in_1 = bf16[112,1920]{1,0:T(8,128)(2,1)S(1)} collective-permute-done((bf16[112,1920]{1,0:T(8,128)(2,1)S(1)}, bf16[112,1920]{1,0:T(8,128)(2,1)S(1)}, u32[]{:S(2)}, u32[]{:S(2)}) %collective-permute-start.10) | collective-permute-done | bytes 430112 | tf_op jit(solution)/shard_map/ppermute | solution.py:25
  96.5 2.2 %collective-permute-start.20 = (bf16[112,1920]{1,0:T(8,128)(2,1)S(1)}, bf16[112,1920]{1,0:T(8,128)(2,1)S(1)}, u32[]{:S(2)}, u32[]{:S(2)}) collective-permute-start(bf16[112,1920]{1,0:T(8,128)(2,1)S(1)} %get-tuple-element.103), channel_id=1, source_target_pairs={{0,32},{1,33},{2,34},{3,35},{4,36},{5,37},{6,38},{7,39},{8,40},{9,... | collective-permute-start | bytes 1290248 | tf_op jit(solution)/shard_map/ppermute | solution.py:25
  98.7 11.2 %collective-permute-done.12.in_2 = bf16[1168,256]{1,0:T(8,128)(2,1)S(1)} collective-permute-done((bf16[1168,256]{1,0:T(8,128)(2,1)S(1)}, bf16[1168,256]{1,0:T(8,128)(2,1)S(1)}, u32[]{:S(2)}, u32[]{:S(2)}) %collective-permute-start.12) | collective-permute-done | bytes 598048 | tf_op jit(solution)/shard_map/ppermute | solution.py:25
  111.2 2.7 %shard_map.36 = (bf16[400,128]{1,0:T(8,128)(2,1)S(1)}, bf16[400,128]{1,0:T(8,128)(2,1)S(1)}, bf16[400,128]{1,0:T(8,128)(2,1)S(1)}, bf16[400,128]{1,0:T(8,128)(2,...) custom-call(s32[8]{0:T(128)S(1)} %stack.26.at_ref, ...), custom_call_target="tpu_custom_call" | custom-call | flops 1000 | bytes 1000 | tf_op jit(solution)/shard_map/pallas_call | solution.py:68
  113.8 3.3 %collective-permute-start.13 = (bf16[400,128]{1,0:T(8,128)(2,1)S(1)}, bf16[400,128]{1,0:T(8,128)(2,1)S(1)}, u32[]{:S(2)}, u32[]{:S(2)}) collective-permute-start(bf16[400,128]{1,0:T(8,128)(2,1)S(1)} %get-tuple-element.91), channel_id=1, source_target_pairs={{0,32},{1,33},{2,34},{3,35},{4,36},{5,37},{6,38},{7,39},{8,40},{9,... | collective-permute-start | bytes 307208 | tf_op jit(solution)/shard_map/ppermute | solution.py:25
  118.4 3.8 %collective-permute-start.15 = (bf16[400,128]{1,0:T(8,128)(2,1)S(1)}, bf16[400,128]{1,0:T(8,128)(2,1)S(1)}, u32[]{:S(2)}, u32[]{:S(2)}) collective-permute-start(bf16[400,128]{1,0:T(8,128)(2,1)S(1)} %get-tuple-element.93), channel_id=1, source_target_pairs={{0,34},{1,35},{2,48},{3,49},{4,38},{5,39},{6,52},{7,53},{8,42},{9,... | collective-permute-start | bytes 307208 | tf_op jit(solution)/shard_map/ppermute | solution.py:25
  122.2 8.0 %collective-permute-done.13.refs_1_ = bf16[400,128]{1,0:T(8,128)(2,1)S(1)} collective-permute-done((bf16[400,128]{1,0:T(8,128)(2,1)S(1)}, bf16[400,128]{1,0:T(8,128)(2,1)S(1)}, u32[]{:S(2)}, u32[]{:S(2)}) %collective-permute-start.13) | collective-permute-done | bytes 102432 | tf_op jit(solution)/shard_map/ppermute | solution.py:25
  130.2 1.7 %collective-permute-done.14.refs_2_ = bf16[400,128]{1,0:T(8,128)(2,1)S(1)} collective-permute-done((bf16[400,128]{1,0:T(8,128)(2,1)S(1)}, bf16[400,128]{1,0:T(8,128)(2,1)S(1)}, u32[]{:S(2)}, u32[]{:S(2)}) %collective-permute-start.14) | collective-permute-done | bytes 102432 | tf_op jit(solution)/shard_map/ppermute | solution.py:25
  131.9 4.4 %collective-permute-start.18 = (bf16[400,128]{1,0:T(8,128)(2,1)S(1)}, bf16[400,128]{1,0:T(8,128)(2,1)S(1)}, u32[]{:S(2)}, u32[]{:S(2)}) collective-permute-start(bf16[400,128]{1,0:T(8,128)(2,1)S(1)} %get-tuple-element.96), channel_id=1, source_target_pairs={{0,2},{1,3},{2,16},{3,17},{4,6},{5,7},{6,20},{7,21},{8,10},{9,11},... | collective-permute-start | bytes 307208 | tf_op jit(solution)/shard_map/ppermute | solution.py:25
  137.2 2.5 %shard_map.37 = (f32[112,1408]{1,0:T(8,128)S(1)}, f32[112,384]{1,0:T(8,128)S(1)}) custom-call(s32[8]{0:T(128)S(1)} %stack.26.at_ref, f32[112,1920]{1,0:T(8,128)S(1)} %get-tuple-element.98.own_ref, bf16[112,1920]{1,0:T(8,128)(2,1)S(1)} %collective-permute-done.10.in_1, bf16[112,1920]{1,0:T(8,128)(2,1)S(1)} %collective-permute-done.11.in_3, ...), custom_call_target="tpu_custom_call" | custom-call | flops 1000 | bytes 1000 | tf_op jit(solution)/shard_map/pallas_call | solution.py:68
  141.0 2.8 %collective-permute-start.23 = (f32[112,384]{1,0:T(8,128)S(1)}, f32[112,384]{1,0:T(8,128)S(1)}, u32[]{:S(2)}, u32[]{:S(2)}) collective-permute-start(f32[112,384]{1,0:T(8,128)S(1)} %get-tuple-element.117), channel_id=1, source_target_pairs={{0,64},{1,65},{2,66},{3,67},{4,68},{5,69},{6,70},{7,71},{8,72},{9,... | collective-permute-start | bytes 516104 | tf_op jit(solution)/shard_map/ppermute | solution.py:25
  145.2 5.1 %collective-permute-start.21 = (f32[128,128]{1,0:T(8,128)S(1)}, f32[128,128]{1,0:T(8,128)S(1)}, u32[]{:S(2)}, u32[]{:S(2)}) collective-permute-start(f32[128,128]{1,0:T(8,128)S(1)} %get-tuple-element.114), channel_id=1, source_target_pairs={{0,1},{1,2},{2,3},{3,0},{4,16},{5,17},{6,18},{7,19},{8,32},{9,33},... | collective-permute-start | bytes 196616 | tf_op jit(solution)/shard_map/ppermute | solution.py:25
  150.4 1.9 %collective-permute-start.22 = (f32[128,128]{1,0:T(8,128)S(1)}, f32[128,128]{1,0:T(8,128)S(1)}, u32[]{:S(2)}, u32[]{:S(2)}) collective-permute-start(f32[128,128]{1,0:T(8,128)S(1)} %get-tuple-element.115), channel_id=1, source_target_pairs={{0,0},{1,1},{2,2},{3,3},{4,18},{5,19},{6,16},{7,17},{8,34},{9,35},... | collective-permute-start | bytes 196616 | tf_op jit(solution)/shard_map/ppermute | solution.py:25
  152.3 1.8 %collective-permute-done.21.same_ref = f32[128,128]{1,0:T(8,128)S(1)} collective-permute-done((f32[128,128]{1,0:T(8,128)S(1)}, f32[128,128]{1,0:T(8,128)S(1)}, u32[]{:S(2)}, u32[]{:S(2)}) %collective-permute-start.21) | collective-permute-done | bytes 65568 | tf_op jit(solution)/shard_map/ppermute | solution.py:25
  154.0 7.0 %collective-permute-done.22.other_ref = f32[128,128]{1,0:T(8,128)S(1)} collective-permute-done((f32[128,128]{1,0:T(8,128)S(1)}, f32[128,128]{1,0:T(8,128)S(1)}, u32[]{:S(2)}, u32[]{:S(2)}) %collective-permute-start.22) | collective-permute-done | bytes 65568 | tf_op jit(solution)/shard_map/ppermute | solution.py:25
  162.3 1.5 shard_map.40
  (37 shorter events, 14.6 us)
Async XLA Ops:
  0.7 6.4 %copy-start = (bf16[512,1792]{1,0:T(8,128)(2,1)S(1)}, bf16[512,1792]{1,0:T(8,128)(2,1)}, u32[]{:S(2)}) copy-start(bf16[512,1792]{1,0:T(8,128)(2,1)} %g_ref.3) | copy-start | bytes 5505028
  3.7 24.6 %collective-permute-start = (bf16[512,896]{1,0:T(8,128)(2,1)}, bf16[512,896]{1,0:T(8,128)(2,1)S(1)}, u32[]{:S(2)}, u32[]{:S(2)}) collective-permute-start(bf16[512,896]{1,0:T(8,128)(2,1)} %get-tuple-element.60), channel_id=1, source_target_pairs={{0,16},{1,48},{2,18},{3,50},{4,20},{5,52},{6,22},{7,54},{8,24},{9,... | collective-permute-start | bytes 2752520 | tf_op jit(solution)/shard_map/ppermute | solution.py:25
  8.9 16.8 %collective-permute-start.1 = (bf16[240,1408]{1,0:T(8,128)(2,1)S(1)}, bf16[240,1408]{1,0:T(8,128)(2,1)S(1)}, u32[]{:S(2)}, u32[]{:S(2)}) collective-permute-start(bf16[240,1408]{1,0:T(8,128)(2,1)S(1)} %get-tuple-element.63), channel_id=1, source_target_pairs={{0,192},{1,193},{2,194},{3,195},{4,196},{5,197},{6,198},{7,199},{8... | collective-permute-start | bytes 2027528 | tf_op jit(solution)/shard_map/ppermute | solution.py:25
  9.6 18.8 %copy-start.3 = (bf16[512,896]{1,0:T(8,128)(2,1)S(1)}, bf16[512,896]{1,0:T(8,128)(2,1)}, u32[]{:S(2)}) copy-start(bf16[512,896]{1,0:T(8,128)(2,1)} %get-tuple-element.65) | copy-start | bytes 2752516
  9.6 19.5 %collective-permute-start.3 = (bf16[240,1408]{1,0:T(8,128)(2,1)S(1)}, bf16[240,1408]{1,0:T(8,128)(2,1)S(1)}, u32[]{:S(2)}, u32[]{:S(2)}) collective-permute-start(bf16[240,1408]{1,0:T(8,128)(2,1)S(1)} %get-tuple-element.66), channel_id=1, source_target_pairs={{0,64},{1,65},{2,66},{3,67},{4,68},{5,69},{6,70},{7,71},{8,72},{9,... | collective-permute-start | bytes 2027528 | tf_op jit(solution)/shard_map/ppermute | solution.py:25
  28.3 8.8 %collective-permute-start.2 = (bf16[512,896]{1,0:T(8,128)(2,1)S(1)}, bf16[512,896]{1,0:T(8,128)(2,1)S(1)}, u32[]{:S(2)}, u32[]{:S(2)}) collective-permute-start(bf16[512,896]{1,0:T(8,128)(2,1)S(1)} %copy-done.3), channel_id=1, source_target_pairs={{0,0},{1,32},{2,2},{3,34},{4,4},{5,36},{6,6},{7,38},{8,8},{9,40},{... | collective-permute-start | bytes 2752520 | tf_op jit(solution)/shard_map/ppermute | solution.py:25
  31.6 26.9 %collective-permute-start.6 = (bf16[464,1408]{1,0:T(8,128)(2,1)S(1)}, bf16[464,1408]{1,0:T(8,128)(2,1)S(1)}, u32[]{:S(2)}, u32[]{:S(2)}) collective-permute-start(bf16[464,1408]{1,0:T(8,128)(2,1)S(1)} %shard_map.32), channel_id=1, source_target_pairs={{0,64},{1,65},{2,66},{3,67},{4,68},{5,69},{6,70},{7,71},{8,72},{9,... | collective-permute-start | bytes 3919880 | tf_op jit(solution)/shard_map/ppermute | solution.py:25
  34.1 27.2 %collective-permute-start.7 = (bf16[464,1408]{1,0:T(8,128)(2,1)S(1)}, bf16[464,1408]{1,0:T(8,128)(2,1)S(1)}, u32[]{:S(2)}, u32[]{:S(2)}) collective-permute-start(bf16[464,1408]{1,0:T(8,128)(2,1)S(1)} %shard_map.31), channel_id=1, source_target_pairs={{0,192},{1,193},{2,194},{3,195},{4,196},{5,197},{6,198},{7,199},{8... | collective-permute-start | bytes 3919880 | tf_op jit(solution)/shard_map/ppermute | solution.py:25
  35.7 1.5 copy-start.1
  37.2 37.0 %collective-permute-start.4 = (bf16[512,896]{1,0:T(8,128)(2,1)S(1)}, bf16[512,896]{1,0:T(8,128)(2,1)S(1)}, u32[]{:S(2)}, u32[]{:S(2)}) collective-permute-start(bf16[512,896]{1,0:T(8,128)(2,1)S(1)} %collective-permute-done.2.far), channel_id=1, source_target_pairs={{0,1},{1,0},{2,3},{3,2},{4,5},{5,4},{6,7},{7,6},{8,9},{9,8},{10,11... | collective-permute-start | bytes 2752520 | tf_op jit(solution)/shard_map/ppermute | solution.py:25
  57.7 16.5 %collective-permute-start.5 = (bf16[512,896]{1,0:T(8,128)(2,1)S(1)}, bf16[512,896]{1,0:T(8,128)(2,1)S(1)}, u32[]{:S(2)}, u32[]{:S(2)}) collective-permute-start(bf16[512,896]{1,0:T(8,128)(2,1)S(1)} %collective-permute-done.near), channel_id=1, source_target_pairs={{0,1},{1,0},{2,3},{3,2},{4,5},{5,4},{6,7},{7,6},{8,9},{9,8},{10,11... | collective-permute-start | bytes 2752520 | tf_op jit(solution)/shard_map/ppermute | solution.py:25
  67.3 21.9 %collective-permute-start.11 = (bf16[112,1920]{1,0:T(8,128)(2,1)S(1)}, bf16[112,1920]{1,0:T(8,128)(2,1)S(1)}, u32[]{:S(2)}, u32[]{:S(2)}) collective-permute-start(bf16[112,1920]{1,0:T(8,128)(2,1)S(1)} %get-tuple-element.84), channel_id=1, source_target_pairs={{0,48},{1,49},{2,50},{3,51},{4,52},{5,53},{6,54},{7,55},{8,56},{9,... | collective-permute-start | bytes 1290248 | tf_op jit(solution)/shard_map/ppermute | solution.py:25
  74.1 19.0 %collective-permute-start.10 = (bf16[112,1920]{1,0:T(8,128)(2,1)S(1)}, bf16[112,1920]{1,0:T(8,128)(2,1)S(1)}, u32[]{:S(2)}, u32[]{:S(2)}) collective-permute-start(bf16[112,1920]{1,0:T(8,128)(2,1)S(1)} %get-tuple-element.73), channel_id=1, source_target_pairs={{0,16},{1,17},{2,18},{3,19},{4,20},{5,21},{6,22},{7,23},{8,24},{9,... | collective-permute-start | bytes 1290248 | tf_op jit(solution)/shard_map/ppermute | solution.py:25
  80.0 15.8 %collective-permute-start.8 = (bf16[1168,256]{1,0:T(8,128)(2,1)S(1)}, bf16[1168,256]{1,0:T(8,128)(2,1)S(1)}, u32[]{:S(2)}, u32[]{:S(2)}) collective-permute-start(bf16[1168,256]{1,0:T(8,128)(2,1)S(1)} %get-tuple-element.80), channel_id=1, source_target_pairs={{0,4},{1,5},{2,6},{3,7},{4,8},{5,9},{6,10},{7,11},{8,12},{9,13},{1... | collective-permute-start | bytes 1794056 | tf_op jit(solution)/shard_map/ppermute | solution.py:25
  80.2 16.3 %collective-permute-start.9 = (bf16[1168,256]{1,0:T(8,128)(2,1)S(1)}, bf16[1168,256]{1,0:T(8,128)(2,1)S(1)}, u32[]{:S(2)}, u32[]{:S(2)}) collective-permute-start(bf16[1168,256]{1,0:T(8,128)(2,1)S(1)} %get-tuple-element.81), channel_id=1, source_target_pairs={{0,12},{1,13},{2,14},{3,15},{4,0},{5,1},{6,2},{7,3},{8,4},{9,5},{1... | collective-permute-start | bytes 1794056 | tf_op jit(solution)/shard_map/ppermute | solution.py:25
  93.1 16.7 %collective-permute-start.12 = (bf16[1168,256]{1,0:T(8,128)(2,1)S(1)}, bf16[1168,256]{1,0:T(8,128)(2,1)S(1)}, u32[]{:S(2)}, u32[]{:S(2)}) collective-permute-start(bf16[1168,256]{1,0:T(8,128)(2,1)S(1)} %get-tuple-element.89), channel_id=1, source_target_pairs={{0,8},{1,9},{2,10},{3,11},{4,12},{5,13},{6,14},{7,15},{8,0},{9,1},... | collective-permute-start | bytes 1794056 | tf_op jit(solution)/shard_map/ppermute | solution.py:25
  96.5 39.9 %collective-permute-start.20 = (bf16[112,1920]{1,0:T(8,128)(2,1)S(1)}, bf16[112,1920]{1,0:T(8,128)(2,1)S(1)}, u32[]{:S(2)}, u32[]{:S(2)}) collective-permute-start(bf16[112,1920]{1,0:T(8,128)(2,1)S(1)} %get-tuple-element.103), channel_id=1, source_target_pairs={{0,32},{1,33},{2,34},{3,35},{4,36},{5,37},{6,38},{7,39},{8,40},{9,... | collective-permute-start | bytes 1290248 | tf_op jit(solution)/shard_map/ppermute | solution.py:25
  109.9 1.3 copy-start.2
  113.8 16.4 %collective-permute-start.13 = (bf16[400,128]{1,0:T(8,128)(2,1)S(1)}, bf16[400,128]{1,0:T(8,128)(2,1)S(1)}, u32[]{:S(2)}, u32[]{:S(2)}) collective-permute-start(bf16[400,128]{1,0:T(8,128)(2,1)S(1)} %get-tuple-element.91), channel_id=1, source_target_pairs={{0,32},{1,33},{2,34},{3,35},{4,36},{5,37},{6,38},{7,39},{8,40},{9,... | collective-permute-start | bytes 307208 | tf_op jit(solution)/shard_map/ppermute | solution.py:25
  117.2 14.8 %collective-permute-start.14 = (bf16[400,128]{1,0:T(8,128)(2,1)S(1)}, bf16[400,128]{1,0:T(8,128)(2,1)S(1)}, u32[]{:S(2)}, u32[]{:S(2)}) collective-permute-start(bf16[400,128]{1,0:T(8,128)(2,1)S(1)} %get-tuple-element.92), channel_id=1, source_target_pairs={{0,18},{1,19},{2,32},{3,33},{4,22},{5,23},{6,36},{7,37},{8,26},{9,... | collective-permute-start | bytes 307208 | tf_op jit(solution)/shard_map/ppermute | solution.py:25
  118.4 21.3 %collective-permute-start.15 = (bf16[400,128]{1,0:T(8,128)(2,1)S(1)}, bf16[400,128]{1,0:T(8,128)(2,1)S(1)}, u32[]{:S(2)}, u32[]{:S(2)}) collective-permute-start(bf16[400,128]{1,0:T(8,128)(2,1)S(1)} %get-tuple-element.93), channel_id=1, source_target_pairs={{0,34},{1,35},{2,48},{3,49},{4,38},{5,39},{6,52},{7,53},{8,42},{9,... | collective-permute-start | bytes 307208 | tf_op jit(solution)/shard_map/ppermute | solution.py:25
  122.2 17.5 %collective-permute-start.16 = (bf16[400,128]{1,0:T(8,128)(2,1)S(1)}, bf16[400,128]{1,0:T(8,128)(2,1)S(1)}, u32[]{:S(2)}, u32[]{:S(2)}) collective-permute-start(bf16[400,128]{1,0:T(8,128)(2,1)S(1)} %get-tuple-element.94), channel_id=1, source_target_pairs={{0,16},{1,17},{2,18},{3,19},{4,20},{5,21},{6,22},{7,23},{8,24},{9,... | collective-permute-start | bytes 307208 | tf_op jit(solution)/shard_map/ppermute | solution.py:25
  130.2 9.5 %collective-permute-start.17 = (bf16[400,128]{1,0:T(8,128)(2,1)S(1)}, bf16[400,128]{1,0:T(8,128)(2,1)S(1)}, u32[]{:S(2)}, u32[]{:S(2)}) collective-permute-start(bf16[400,128]{1,0:T(8,128)(2,1)S(1)} %get-tuple-element.95), channel_id=1, source_target_pairs={{0,48},{1,49},{2,50},{3,51},{4,52},{5,53},{6,54},{7,55},{8,56},{9,... | collective-permute-start | bytes 307208 | tf_op jit(solution)/shard_map/ppermute | solution.py:25
  131.9 7.9 %collective-permute-start.18 = (bf16[400,128]{1,0:T(8,128)(2,1)S(1)}, bf16[400,128]{1,0:T(8,128)(2,1)S(1)}, u32[]{:S(2)}, u32[]{:S(2)}) collective-permute-start(bf16[400,128]{1,0:T(8,128)(2,1)S(1)} %get-tuple-element.96), channel_id=1, source_target_pairs={{0,2},{1,3},{2,16},{3,17},{4,6},{5,7},{6,20},{7,21},{8,10},{9,11},... | collective-permute-start | bytes 307208 | tf_op jit(solution)/shard_map/ppermute | solution.py:25
  136.4 4.7 %collective-permute-start.19 = (bf16[400,128]{1,0:T(8,128)(2,1)S(1)}, bf16[400,128]{1,0:T(8,128)(2,1)S(1)}, u32[]{:S(2)}, u32[]{:S(2)}) collective-permute-start(bf16[400,128]{1,0:T(8,128)(2,1)S(1)} %get-tuple-element.97), channel_id=1, source_target_pairs={{0,50},{1,51},{2,0},{3,1},{4,54},{5,55},{6,4},{7,5},{8,58},{9,59},... | collective-permute-start | bytes 307208 | tf_op jit(solution)/shard_map/ppermute | solution.py:25
  141.0 21.3 %collective-permute-start.23 = (f32[112,384]{1,0:T(8,128)S(1)}, f32[112,384]{1,0:T(8,128)S(1)}, u32[]{:S(2)}, u32[]{:S(2)}) collective-permute-start(f32[112,384]{1,0:T(8,128)S(1)} %get-tuple-element.117), channel_id=1, source_target_pairs={{0,64},{1,65},{2,66},{3,67},{4,68},{5,69},{6,70},{7,71},{8,72},{9,... | collective-permute-start | bytes 516104 | tf_op jit(solution)/shard_map/ppermute | solution.py:25
  145.2 8.8 %collective-permute-start.21 = (f32[128,128]{1,0:T(8,128)S(1)}, f32[128,128]{1,0:T(8,128)S(1)}, u32[]{:S(2)}, u32[]{:S(2)}) collective-permute-start(f32[128,128]{1,0:T(8,128)S(1)} %get-tuple-element.114), channel_id=1, source_target_pairs={{0,1},{1,2},{2,3},{3,0},{4,16},{5,17},{6,18},{7,19},{8,32},{9,33},... | collective-permute-start | bytes 196616 | tf_op jit(solution)/shard_map/ppermute | solution.py:25
  150.4 10.7 %collective-permute-start.22 = (f32[128,128]{1,0:T(8,128)S(1)}, f32[128,128]{1,0:T(8,128)S(1)}, u32[]{:S(2)}, u32[]{:S(2)}) collective-permute-start(f32[128,128]{1,0:T(8,128)S(1)} %get-tuple-element.115), channel_id=1, source_target_pairs={{0,0},{1,1},{2,2},{3,3},{4,18},{5,19},{6,16},{7,17},{8,34},{9,35},... | collective-permute-start | bytes 196616 | tf_op jit(solution)/shard_map/ppermute | solution.py:25

commit v5 on v4

--- a/solution.py
+++ b/solution.py
@@ -372,6 +372,11 @@
     )
 
 
+def last(at_ref, *refs):
+    left_last(at_ref, *refs[:4], refs[6])
+    right_last(at_ref, *refs[4:6], refs[7])
+
+
 def mirror(step):
     def to(x, zh, y, zl, core):
         if zh != y:
@@ -399,7 +404,7 @@
     half = width // 2
 
     cut = lambda parity: lax.dynamic_slice_in_dim(gradient, parity * half, half, 1)
-    near, far, gradient = barrier((cut((zh + 1) % 2), cut(zh % 2), gradient))
+    near, gradient = barrier((cut((zh + 1) % 2), gradient))
     near = send(near, lambda x, zh, y, zl, core: (x, 2 * core + (zh + 1) % 2, y, zl, zh // 2))
 
     window = [((rows, WINDOW), BF16), ((512, 512), BF16), ((512, 128), F32)]
@@ -412,7 +417,7 @@
     )[0]
     code_1, code_3 = add(1, far_1), add(3, far_3)
     right_1, right_3 = over_x(1, code_1), over_x(3, code_3)
-    near, far, _ = barrier((near, far, code_3))
+    near, far, _ = barrier((near, cut(zh % 2), code_3))
     far = send(far, lambda x, zh, y, zl, core: (x, 2 * core + zh % 2, y, zl, zh // 2))
 
     gradient, _ = barrier((gradient, (code_1, code_3)))
@@ -483,7 +488,6 @@
     )
     arrived, image = barrier((arrived, image))
     image = over_x(1, image)
-    right_gram = run(right_last, [((CHUNK, width), F32)], [], at, right_base, image)[0]
 
     square = ((SUB, SUB), F32)
     base, more, same, other = run(
@@ -495,7 +499,9 @@
         *arrived,
     )
     same, other = send(same, mirror(0)), send(other, mirror(1))
-    left_gram = run(left_last, [((512, SUB), F32)], [], at, base, more, same, other)[0]
+    left_gram, right_gram = run(
+        last, [((512, SUB), F32), ((CHUNK, width), F32)], [], at, base, more, same, other, right_base, image
+    )
     return (left_gram, right_gram)
 
 

time: 164 us -> 162 us (0.988)
  the two profiles are of different devices: /device:TPU:60 before, /device:TPU:25 now
where the time goes in v5:
time: 162 us; the launch traced here: 161 us
  waiting for transfers between devices  67.6 us (42%)
  starting transfers between devices  57.3 us (35%)
  Pallas kernels  30.5 us (19%)
  local copies, waits for them, and re-layouts  5.23 us (3%)
    ppermute x24, waiting for transfers between devices, send(): lax.ppermute(array, ('row', 'col'), [(number(p), number(to(*p))) for p in...  67.6 us
    ppermute x24, starting transfers between devices, send(): lax.ppermute(array, ('row', 'col'), [(number(p), number(to(*p))) for p in...  57.3 us
    pallas_call x10, Pallas kernels, run(): pl.pallas_call(body, out_shape=[jax.ShapeDtypeStruct(shape, dtype) for sh...  30.5 us
  transfers between devices with their start and end apart: 24, of which 11 were waited for; matrix products, arithmetic and copies ran while one was open for 0% of the time, Pallas kernels for 18%

profile of v5, /device:TPU:25, one launch (start us, length us, event | category | flops | bytes accessed | tf_op | source)
XLA Modules:
  0.0 161.4 jit_solution(3488817574607398272)
XLA Ops:
  0.7 2.3 %constant_dynamic-slice_fusion.1 = bf16[512,896]{1,0:T(8,128)(2,1)} fusion(bf16[512,1792]{1,0:T(8,128)(2,1)} %g_ref.3, s32[]{:T(128)S(6)} %select_n.46), kind=kLoop, calls=%fused_computation.1 | loop fusion | bytes 1835012 | tf_op jit(solution)/shard_map/dynamic_slice | solution.py:406
  3.0 6.6 %collective-permute-start = (bf16[512,896]{1,0:T(8,128)(2,1)}, bf16[512,896]{1,0:T(8,128)(2,1)S(1)}, u32[]{:S(2)}, u32[]{:S(2)}) collective-permute-start(bf16[512,896]{1,0:T(8,128)(2,1)} %constant_dynamic-slice_fusion.1), channel_id=1, source_target_pairs={{0,16},{1,48},{2,18},{3,50},{4,20},{5,52},{6,22},{7,54},{8,24},{9,... | collective-permute-start | bytes 2752520 | tf_op jit(solution)/shard_map/ppermute | solution.py:25
  9.7 3.0 %shard_map.30 = (bf16[240,1408]{1,0:T(8,128)(2,1)}, bf16[240,1408]{1,0:T(8,128)(2,1)}) custom-call(s32[8]{0:T(128)S(1)} %stack.26.at_ref, bf16[512,1792]{1,0:T(8,128)(2,1)S(1)} %copy-done), custom_call_target="tpu_custom_call" | custom-call | flops 1000 | bytes 1000 | tf_op jit(solution)/shard_map/pallas_call | solution.py:68
  12.7 2.5 %collective-permute-start.1 = (bf16[240,1408]{1,0:T(8,128)(2,1)}, bf16[240,1408]{1,0:T(8,128)(2,1)}, u32[]{:S(2)}, u32[]{:S(2)}) collective-permute-start(bf16[240,1408]{1,0:T(8,128)(2,1)} %get-tuple-element.61), channel_id=1, source_target_pairs={{0,192},{1,193},{2,194},{3,195},{4,196},{5,197},{6,198},{7,199},{8... | collective-permute-start | bytes 2027528 | tf_op jit(solution)/shard_map/ppermute | solution.py:25
  15.3 13.1 %collective-permute-done.1.in_ref = bf16[240,1408]{1,0:T(8,128)(2,1)} collective-permute-done((bf16[240,1408]{1,0:T(8,128)(2,1)}, bf16[240,1408]{1,0:T(8,128)(2,1)}, u32[]{:S(2)}, u32[]{:S(2)}) %collective-permute-start.1) | collective-permute-done | bytes 675872 | tf_op jit(solution)/shard_map/ppermute | solution.py:25
  28.3 3.1 %shard_map.31 = bf16[464,1408]{1,0:T(8,128)(2,1)S(1)} custom-call(s32[8]{0:T(128)S(1)} %stack.26.at_ref, bf16[512,1792]{1,0:T(8,128)(2,1)S(1)} %copy-done, bf16[240,1408]{1,0:T(8,128)(2,1)} %collective-permute-done.1.in_ref), custom_call_target="tpu_custom_call" | custom-call | flops 1000 | bytes 1000 | tf_op jit(solution)/shard_map/pallas_call | solution.py:68
  31.5 5.8 %collective-permute-start.2 = (bf16[512,896]{1,0:T(8,128)(2,1)S(1)}, bf16[512,896]{1,0:T(8,128)(2,1)S(1)}, u32[]{:S(2)}, u32[]{:S(2)}) collective-permute-start(bf16[512,896]{1,0:T(8,128)(2,1)S(1)} %constant_dynamic-slice_fusion), channel_id=1, source_target_pairs={{0,0},{1,32},{2,2},{3,34},{4,4},{5,36},{6,6},{7,38},{8,8},{9,40},{... | collective-permute-start | bytes 2752520 | tf_op jit(solution)/shard_map/ppermute | solution.py:25
  37.3 2.5 %shard_map.32 = bf16[464,1408]{1,0:T(8,128)(2,1)S(1)} custom-call(s32[8]{0:T(128)S(1)} %stack.26.at_ref, bf16[512,1792]{1,0:T(8,128)(2,1)S(1)} %copy-done, bf16[240,1408]{1,0:T(8,128)(2,1)S(1)} %collective-permute-done.3.in_ref), custom_call_target="tpu_custom_call" | custom-call | flops 1000 | bytes 1000 | tf_op jit(solution)/shard_map/pallas_call | solution.py:68
  41.0 2.3 %collective-permute-start.7 = (bf16[464,1408]{1,0:T(8,128)(2,1)S(1)}, bf16[464,1408]{1,0:T(8,128)(2,1)S(1)}, u32[]{:S(2)}, u32[]{:S(2)}) collective-permute-start(bf16[464,1408]{1,0:T(8,128)(2,1)S(1)} %shard_map.31), channel_id=1, source_target_pairs={{0,192},{1,193},{2,194},{3,195},{4,196},{5,197},{6,198},{7,199},{8... | collective-permute-start | bytes 3919880 | tf_op jit(solution)/shard_map/ppermute | solution.py:25
  46.4 13.6 %collective-permute-done.2.far = bf16[512,896]{1,0:T(8,128)(2,1)S(1)} collective-permute-done((bf16[512,896]{1,0:T(8,128)(2,1)S(1)}, bf16[512,896]{1,0:T(8,128)(2,1)S(1)}, u32[]{:S(2)}, u32[]{:S(2)}) %collective-permute-start.2) | collective-permute-done | bytes 917536 | tf_op jit(solution)/shard_map/ppermute | solution.py:25
  60.5 4.9 %collective-permute-done.6.in_1 = bf16[464,1408]{1,0:T(8,128)(2,1)S(1)} collective-permute-done((bf16[464,1408]{1,0:T(8,128)(2,1)S(1)}, bf16[464,1408]{1,0:T(8,128)(2,1)S(1)}, u32[]{:S(2)}, u32[]{:S(2)}) %collective-permute-start.6) | collective-permute-done | bytes 1306656 | tf_op jit(solution)/shard_map/ppermute | solution.py:25
  65.5 6.1 %shard_map.34 = (bf16[112,1920]{1,0:T(8,128)(2,1)S(1)}, bf16[112,1920]{1,0:T(8,128)(2,1)S(1)}, bf16[112,1920]{1,0:T(8,128)(2,1)S(1)}, f32[112,1920]{1,0:T(8,128)S(1)}) custom-call(s32[8]{0:T(128)S(1)} %stack.26.at_ref, f32[448,1408]{1,0:T(8,128)} %copy-done.1, f32[8,1408]{1,0:T(8,128)S(1)} %get-tuple-element.70.norm_ref, ...), custom_call_target="tpu_custom_call" | custom-call | flops 1000 | bytes 1000 | tf_op jit(solution)/shard_map/pallas_call | solution.py:68
  71.6 2.4 %collective-permute-start.11 = (bf16[112,1920]{1,0:T(8,128)(2,1)S(1)}, bf16[112,1920]{1,0:T(8,128)(2,1)S(1)}, u32[]{:S(2)}, u32[]{:S(2)}) collective-permute-start(bf16[112,1920]{1,0:T(8,128)(2,1)S(1)} %get-tuple-element.82), channel_id=1, source_target_pairs={{0,48},{1,49},{2,50},{3,51},{4,52},{5,53},{6,54},{7,55},{8,56},{9,... | collective-permute-start | bytes 1290248 | tf_op jit(solution)/shard_map/ppermute | solution.py:25
  74.0 5.9 %shard_map.35 = (bf16[1168,256]{1,0:T(8,128)(2,1)S(1)}, bf16[1168,256]{1,0:T(8,128)(2,1)S(1)}, bf16[1168,256]{1,0:T(8,128)(2,1)S(1)}, f32[1152,256]{1,0:T(8,128)}, f32[16,128]{1,0:T(8,128)S(1)}) custom-call(s32[8]{0:T(128)S(1)} %stack.26.at_ref, bf16[512,896]{1,0:T(8,128)(2,1)S(1)} %collective-permute-done.2.far, ...), custom_call_target="tpu_custom_call" | custom-call | flops 1000 | bytes 1000 | tf_op jit(solution)/shard_map/pallas_call | solution.py:68
  81.4 2.4 %collective-permute-done.11.in_3 = bf16[112,1920]{1,0:T(8,128)(2,1)S(1)} collective-permute-done((bf16[112,1920]{1,0:T(8,128)(2,1)S(1)}, bf16[112,1920]{1,0:T(8,128)(2,1)S(1)}, u32[]{:S(2)}, u32[]{:S(2)}) %collective-permute-start.11) | collective-permute-done | bytes 430112 | tf_op jit(solution)/shard_map/ppermute | solution.py:25
  83.8 1.9 %collective-permute-done.10.in_1 = bf16[112,1920]{1,0:T(8,128)(2,1)S(1)} collective-permute-done((bf16[112,1920]{1,0:T(8,128)(2,1)S(1)}, bf16[112,1920]{1,0:T(8,128)(2,1)S(1)}, u32[]{:S(2)}, u32[]{:S(2)}) %collective-permute-start.10) | collective-permute-done | bytes 430112 | tf_op jit(solution)/shard_map/ppermute | solution.py:25
  86.7 5.3 %collective-permute-done.8.in_1 = bf16[1168,256]{1,0:T(8,128)(2,1)S(1)} collective-permute-done((bf16[1168,256]{1,0:T(8,128)(2,1)S(1)}, bf16[1168,256]{1,0:T(8,128)(2,1)S(1)}, u32[]{:S(2)}, u32[]{:S(2)}) %collective-permute-start.8) | collective-permute-done | bytes 598048 | tf_op jit(solution)/shard_map/ppermute | solution.py:25
  93.2 2.6 %collective-permute-start.20 = (bf16[112,1920]{1,0:T(8,128)(2,1)S(1)}, bf16[112,1920]{1,0:T(8,128)(2,1)S(1)}, u32[]{:S(2)}, u32[]{:S(2)}) collective-permute-start(bf16[112,1920]{1,0:T(8,128)(2,1)S(1)} %get-tuple-element.101), channel_id=1, source_target_pairs={{0,32},{1,33},{2,34},{3,35},{4,36},{5,37},{6,38},{7,39},{8,40},{9,... | collective-permute-start | bytes 1290248 | tf_op jit(solution)/shard_map/ppermute | solution.py:25
  95.8 7.7 %collective-permute-done.12.in_2 = bf16[1168,256]{1,0:T(8,128)(2,1)S(1)} collective-permute-done((bf16[1168,256]{1,0:T(8,128)(2,1)S(1)}, bf16[1168,256]{1,0:T(8,128)(2,1)S(1)}, u32[]{:S(2)}, u32[]{:S(2)}) %collective-permute-start.12) | collective-permute-done | bytes 598048 | tf_op jit(solution)/shard_map/ppermute | solution.py:25
  104.7 2.7 %shard_map.36 = (bf16[400,128]{1,0:T(8,128)(2,1)S(1)}, bf16[400,128]{1,0:T(8,128)(2,1)S(1)}, bf16[400,128]{1,0:T(8,128)(2,1)S(1)}, bf16[400,128]{1,0:T(8,128)(2,...) custom-call(s32[8]{0:T(128)S(1)} %stack.26.at_ref, ...), custom_call_target="tpu_custom_call" | custom-call | flops 1000 | bytes 1000 | tf_op jit(solution)/shard_map/pallas_call | solution.py:68
  107.4 6.4 %collective-permute-start.13 = (bf16[400,128]{1,0:T(8,128)(2,1)S(1)}, bf16[400,128]{1,0:T(8,128)(2,1)S(1)}, u32[]{:S(2)}, u32[]{:S(2)}) collective-permute-start(bf16[400,128]{1,0:T(8,128)(2,1)S(1)} %get-tuple-element.89), channel_id=1, source_target_pairs={{0,32},{1,33},{2,34},{3,35},{4,36},{5,37},{6,38},{7,39},{8,40},{9,... | collective-permute-start | bytes 307208 | tf_op jit(solution)/shard_map/ppermute | solution.py:25
  113.8 4.9 %collective-permute-start.14 = (bf16[400,128]{1,0:T(8,128)(2,1)S(1)}, bf16[400,128]{1,0:T(8,128)(2,1)S(1)}, u32[]{:S(2)}, u32[]{:S(2)}) collective-permute-start(bf16[400,128]{1,0:T(8,128)(2,1)S(1)} %get-tuple-element.90), channel_id=1, source_target_pairs={{0,18},{1,19},{2,32},{3,33},{4,22},{5,23},{6,36},{7,37},{8,26},{9,... | collective-permute-start | bytes 307208 | tf_op jit(solution)/shard_map/ppermute | solution.py:25
  118.8 2.5 %collective-permute-start.16 = (bf16[400,128]{1,0:T(8,128)(2,1)S(1)}, bf16[400,128]{1,0:T(8,128)(2,1)S(1)}, u32[]{:S(2)}, u32[]{:S(2)}) collective-permute-start(bf16[400,128]{1,0:T(8,128)(2,1)S(1)} %get-tuple-element.92), channel_id=1, source_target_pairs={{0,16},{1,17},{2,18},{3,19},{4,20},{5,21},{6,22},{7,23},{8,24},{9,... | collective-permute-start | bytes 307208 | tf_op jit(solution)/shard_map/ppermute | solution.py:25
  121.2 5.7 %collective-permute-start.17 = (bf16[400,128]{1,0:T(8,128)(2,1)S(1)}, bf16[400,128]{1,0:T(8,128)(2,1)S(1)}, u32[]{:S(2)}, u32[]{:S(2)}) collective-permute-start(bf16[400,128]{1,0:T(8,128)(2,1)S(1)} %get-tuple-element.93), channel_id=1, source_target_pairs={{0,48},{1,49},{2,50},{3,51},{4,52},{5,53},{6,54},{7,55},{8,56},{9,... | collective-permute-start | bytes 307208 | tf_op jit(solution)/shard_map/ppermute | solution.py:25
  126.9 9.5 %collective-permute-done.14.refs_2_ = bf16[400,128]{1,0:T(8,128)(2,1)S(1)} collective-permute-done((bf16[400,128]{1,0:T(8,128)(2,1)S(1)}, bf16[400,128]{1,0:T(8,128)(2,1)S(1)}, u32[]{:S(2)}, u32[]{:S(2)}) %collective-permute-start.14) | collective-permute-done | bytes 102432 | tf_op jit(solution)/shard_map/ppermute | solution.py:25
  136.4 2.7 %collective-permute-start.19 = (bf16[400,128]{1,0:T(8,128)(2,1)S(1)}, bf16[400,128]{1,0:T(8,128)(2,1)S(1)}, u32[]{:S(2)}, u32[]{:S(2)}) collective-permute-start(bf16[400,128]{1,0:T(8,128)(2,1)S(1)} %get-tuple-element.95), channel_id=1, source_target_pairs={{0,50},{1,51},{2,0},{3,1},{4,54},{5,55},{6,4},{7,5},{8,58},{9,59},... | collective-permute-start | bytes 307208 | tf_op jit(solution)/shard_map/ppermute | solution.py:25
  139.1 2.5 %shard_map.37 = (f32[112,1408]{1,0:T(8,128)S(1)}, f32[112,384]{1,0:T(8,128)S(1)}) custom-call(s32[8]{0:T(128)S(1)} %stack.26.at_ref, f32[112,1920]{1,0:T(8,128)S(1)} %get-tuple-element.96.own_ref, bf16[112,1920]{1,0:T(8,128)(2,1)S(1)} %collective-permute-done.10.in_1, bf16[112,1920]{1,0:T(8,128)(2,1)S(1)} %collective-permute-done.11.in_3, ...), custom_call_target="tpu_custom_call" | custom-call | flops 1000 | bytes 1000 | tf_op jit(solution)/shard_map/pallas_call | solution.py:68
  141.6 2.2 %collective-permute-start.23 = (f32[112,384]{1,0:T(8,128)S(1)}, f32[112,384]{1,0:T(8,128)S(1)}, u32[]{:S(2)}, u32[]{:S(2)}) collective-permute-start(f32[112,384]{1,0:T(8,128)S(1)} %get-tuple-element.115), channel_id=1, source_target_pairs={{0,64},{1,65},{2,66},{3,67},{4,68},{5,69},{6,70},{7,71},{8,72},{9,... | collective-permute-start | bytes 516104 | tf_op jit(solution)/shard_map/ppermute | solution.py:25
  145.3 6.5 %collective-permute-start.22 = (f32[128,128]{1,0:T(8,128)S(1)}, f32[128,128]{1,0:T(8,128)S(1)}, u32[]{:S(2)}, u32[]{:S(2)}) collective-permute-start(f32[128,128]{1,0:T(8,128)S(1)} %get-tuple-element.113), channel_id=1, source_target_pairs={{0,0},{1,1},{2,2},{3,3},{4,18},{5,19},{6,16},{7,17},{8,34},{9,35},... | collective-permute-start | bytes 196616 | tf_op jit(solution)/shard_map/ppermute | solution.py:25
  151.9 3.6 %collective-permute-done.21.refs_2_ = f32[128,128]{1,0:T(8,128)S(1)} collective-permute-done((f32[128,128]{1,0:T(8,128)S(1)}, f32[128,128]{1,0:T(8,128)S(1)}, u32[]{:S(2)}, u32[]{:S(2)}) %collective-permute-start.21) | collective-permute-done | bytes 65568 | tf_op jit(solution)/shard_map/ppermute | solution.py:25
  155.5 4.3 %collective-permute-done.22.refs_3_ = f32[128,128]{1,0:T(8,128)S(1)} collective-permute-done((f32[128,128]{1,0:T(8,128)S(1)}, f32[128,128]{1,0:T(8,128)S(1)}, u32[]{:S(2)}, u32[]{:S(2)}) %collective-permute-start.22) | collective-permute-done | bytes 65568 | tf_op jit(solution)/shard_map/ppermute | solution.py:25
  159.8 1.6 %shard_map.39 = (f32[512,128]{1,0:T(8,128)}, f32[112,1792]{1,0:T(8,128)}) custom-call(s32[8]{0:T(128)S(1)} %stack.26.at_ref, f32[256,128]{1,0:T(8,128)S(1)} %get-tuple-element.110.refs_0_, f32[128,128]{1,0:T(8,128)S(1)} %get-tuple-element.111.refs_1_, f32[128,128]{1,0:T(8,128)S(1)} %collective-permute-done.21.refs_2_, ...), custom_call_target="tpu_custom_call" | custom-call | flops 1000 | bytes 1000 | tf_op jit(solution)/shard_map/pallas_call | solution.py:68
  (35 shorter events, 11.6 us)
Async XLA Ops:
  0.6 9.0 %copy-start = (bf16[512,1792]{1,0:T(8,128)(2,1)S(1)}, bf16[512,1792]{1,0:T(8,128)(2,1)}, u32[]{:S(2)}) copy-start(bf16[512,1792]{1,0:T(8,128)(2,1)} %g_ref.3) | copy-start | bytes 5505028
  3.0 28.5 %collective-permute-start = (bf16[512,896]{1,0:T(8,128)(2,1)}, bf16[512,896]{1,0:T(8,128)(2,1)S(1)}, u32[]{:S(2)}, u32[]{:S(2)}) collective-permute-start(bf16[512,896]{1,0:T(8,128)(2,1)} %constant_dynamic-slice_fusion.1), channel_id=1, source_target_pairs={{0,16},{1,48},{2,18},{3,50},{4,20},{5,52},{6,22},{7,54},{8,24},{9,... | collective-permute-start | bytes 2752520 | tf_op jit(solution)/shard_map/ppermute | solution.py:25
  12.7 15.6 %collective-permute-start.1 = (bf16[240,1408]{1,0:T(8,128)(2,1)}, bf16[240,1408]{1,0:T(8,128)(2,1)}, u32[]{:S(2)}, u32[]{:S(2)}) collective-permute-start(bf16[240,1408]{1,0:T(8,128)(2,1)} %get-tuple-element.61), channel_id=1, source_target_pairs={{0,192},{1,193},{2,194},{3,195},{4,196},{5,197},{6,198},{7,199},{8... | collective-permute-start | bytes 2027528 | tf_op jit(solution)/shard_map/ppermute | solution.py:25
  15.2 22.1 %collective-permute-start.3 = (bf16[240,1408]{1,0:T(8,128)(2,1)}, bf16[240,1408]{1,0:T(8,128)(2,1)S(1)}, u32[]{:S(2)}, u32[]{:S(2)}) collective-permute-start(bf16[240,1408]{1,0:T(8,128)(2,1)} %get-tuple-element.64), channel_id=1, source_target_pairs={{0,64},{1,65},{2,66},{3,67},{4,68},{5,69},{6,70},{7,71},{8,72},{9,... | collective-permute-start | bytes 2027528 | tf_op jit(solution)/shard_map/ppermute | solution.py:25
  31.5 28.6 %collective-permute-start.2 = (bf16[512,896]{1,0:T(8,128)(2,1)S(1)}, bf16[512,896]{1,0:T(8,128)(2,1)S(1)}, u32[]{:S(2)}, u32[]{:S(2)}) collective-permute-start(bf16[512,896]{1,0:T(8,128)(2,1)S(1)} %constant_dynamic-slice_fusion), channel_id=1, source_target_pairs={{0,0},{1,32},{2,2},{3,34},{4,4},{5,36},{6,6},{7,38},{8,8},{9,40},{... | collective-permute-start | bytes 2752520 | tf_op jit(solution)/shard_map/ppermute | solution.py:25
  39.7 25.7 %collective-permute-start.6 = (bf16[464,1408]{1,0:T(8,128)(2,1)S(1)}, bf16[464,1408]{1,0:T(8,128)(2,1)S(1)}, u32[]{:S(2)}, u32[]{:S(2)}) collective-permute-start(bf16[464,1408]{1,0:T(8,128)(2,1)S(1)} %shard_map.32), channel_id=1, source_target_pairs={{0,64},{1,65},{2,66},{3,67},{4,68},{5,69},{6,70},{7,71},{8,72},{9,... | collective-permute-start | bytes 3919880 | tf_op jit(solution)/shard_map/ppermute | solution.py:25
  41.0 24.5 %collective-permute-start.7 = (bf16[464,1408]{1,0:T(8,128)(2,1)S(1)}, bf16[464,1408]{1,0:T(8,128)(2,1)S(1)}, u32[]{:S(2)}, u32[]{:S(2)}) collective-permute-start(bf16[464,1408]{1,0:T(8,128)(2,1)S(1)} %shard_map.31), channel_id=1, source_target_pairs={{0,192},{1,193},{2,194},{3,195},{4,196},{5,197},{6,198},{7,199},{8... | collective-permute-start | bytes 3919880 | tf_op jit(solution)/shard_map/ppermute | solution.py:25
  44.9 1.5 copy-start.1
  60.0 14.0 %collective-permute-start.4 = (bf16[512,896]{1,0:T(8,128)(2,1)S(1)}, bf16[512,896]{1,0:T(8,128)(2,1)S(1)}, u32[]{:S(2)}, u32[]{:S(2)}) collective-permute-start(bf16[512,896]{1,0:T(8,128)(2,1)S(1)} %collective-permute-done.2.far), channel_id=1, source_target_pairs={{0,1},{1,0},{2,3},{3,2},{4,5},{5,4},{6,7},{7,6},{8,9},{9,8},{10,11... | collective-permute-start | bytes 2752520 | tf_op jit(solution)/shard_map/ppermute | solution.py:25
  60.0 14.0 %collective-permute-start.5 = (bf16[512,896]{1,0:T(8,128)(2,1)S(1)}, bf16[512,896]{1,0:T(8,128)(2,1)S(1)}, u32[]{:S(2)}, u32[]{:S(2)}) collective-permute-start(bf16[512,896]{1,0:T(8,128)(2,1)S(1)} %collective-permute-done.near), channel_id=1, source_target_pairs={{0,1},{1,0},{2,3},{3,2},{4,5},{5,4},{6,7},{7,6},{8,9},{9,8},{10,11... | collective-permute-start | bytes 2752520 | tf_op jit(solution)/shard_map/ppermute | solution.py:25
  71.6 12.2 %collective-permute-start.11 = (bf16[112,1920]{1,0:T(8,128)(2,1)S(1)}, bf16[112,1920]{1,0:T(8,128)(2,1)S(1)}, u32[]{:S(2)}, u32[]{:S(2)}) collective-permute-start(bf16[112,1920]{1,0:T(8,128)(2,1)S(1)} %get-tuple-element.82), channel_id=1, source_target_pairs={{0,48},{1,49},{2,50},{3,51},{4,52},{5,53},{6,54},{7,55},{8,56},{9,... | collective-permute-start | bytes 1290248 | tf_op jit(solution)/shard_map/ppermute | solution.py:25
  74.0 11.7 %collective-permute-start.10 = (bf16[112,1920]{1,0:T(8,128)(2,1)S(1)}, bf16[112,1920]{1,0:T(8,128)(2,1)S(1)}, u32[]{:S(2)}, u32[]{:S(2)}) collective-permute-start(bf16[112,1920]{1,0:T(8,128)(2,1)S(1)} %get-tuple-element.71), channel_id=1, source_target_pairs={{0,16},{1,17},{2,18},{3,19},{4,20},{5,21},{6,22},{7,23},{8,24},{9,... | collective-permute-start | bytes 1290248 | tf_op jit(solution)/shard_map/ppermute | solution.py:25
  79.9 12.0 %collective-permute-start.8 = (bf16[1168,256]{1,0:T(8,128)(2,1)S(1)}, bf16[1168,256]{1,0:T(8,128)(2,1)S(1)}, u32[]{:S(2)}, u32[]{:S(2)}) collective-permute-start(bf16[1168,256]{1,0:T(8,128)(2,1)S(1)} %get-tuple-element.78), channel_id=1, source_target_pairs={{0,4},{1,5},{2,6},{3,7},{4,8},{5,9},{6,10},{7,11},{8,12},{9,13},{1... | collective-permute-start | bytes 1794056 | tf_op jit(solution)/shard_map/ppermute | solution.py:25
  79.9 13.3 %collective-permute-start.9 = (bf16[1168,256]{1,0:T(8,128)(2,1)S(1)}, bf16[1168,256]{1,0:T(8,128)(2,1)S(1)}, u32[]{:S(2)}, u32[]{:S(2)}) collective-permute-start(bf16[1168,256]{1,0:T(8,128)(2,1)S(1)} %get-tuple-element.79), channel_id=1, source_target_pairs={{0,12},{1,13},{2,14},{3,15},{4,0},{5,1},{6,2},{7,3},{8,4},{9,5},{1... | collective-permute-start | bytes 1794056 | tf_op jit(solution)/shard_map/ppermute | solution.py:25
  85.7 17.7 %collective-permute-start.12 = (bf16[1168,256]{1,0:T(8,128)(2,1)S(1)}, bf16[1168,256]{1,0:T(8,128)(2,1)S(1)}, u32[]{:S(2)}, u32[]{:S(2)}) collective-permute-start(bf16[1168,256]{1,0:T(8,128)(2,1)S(1)} %get-tuple-element.87), channel_id=1, source_target_pairs={{0,8},{1,9},{2,10},{3,11},{4,12},{5,13},{6,14},{7,15},{8,0},{9,1},... | collective-permute-start | bytes 1794056 | tf_op jit(solution)/shard_map/ppermute | solution.py:25
  93.2 43.2 %collective-permute-start.20 = (bf16[112,1920]{1,0:T(8,128)(2,1)S(1)}, bf16[112,1920]{1,0:T(8,128)(2,1)S(1)}, u32[]{:S(2)}, u32[]{:S(2)}) collective-permute-start(bf16[112,1920]{1,0:T(8,128)(2,1)S(1)} %get-tuple-element.101), channel_id=1, source_target_pairs={{0,32},{1,33},{2,34},{3,35},{4,36},{5,37},{6,38},{7,39},{8,40},{9,... | collective-permute-start | bytes 1290248 | tf_op jit(solution)/shard_map/ppermute | solution.py:25
  103.5 1.3 copy-start.2
  107.4 13.8 %collective-permute-start.13 = (bf16[400,128]{1,0:T(8,128)(2,1)S(1)}, bf16[400,128]{1,0:T(8,128)(2,1)S(1)}, u32[]{:S(2)}, u32[]{:S(2)}) collective-permute-start(bf16[400,128]{1,0:T(8,128)(2,1)S(1)} %get-tuple-element.89), channel_id=1, source_target_pairs={{0,32},{1,33},{2,34},{3,35},{4,36},{5,37},{6,38},{7,39},{8,40},{9,... | collective-permute-start | bytes 307208 | tf_op jit(solution)/shard_map/ppermute | solution.py:25
  113.8 22.6 %collective-permute-start.14 = (bf16[400,128]{1,0:T(8,128)(2,1)S(1)}, bf16[400,128]{1,0:T(8,128)(2,1)S(1)}, u32[]{:S(2)}, u32[]{:S(2)}) collective-permute-start(bf16[400,128]{1,0:T(8,128)(2,1)S(1)} %get-tuple-element.90), channel_id=1, source_target_pairs={{0,18},{1,19},{2,32},{3,33},{4,22},{5,23},{6,36},{7,37},{8,26},{9,... | collective-permute-start | bytes 307208 | tf_op jit(solution)/shard_map/ppermute | solution.py:25
  118.8 22.8 %collective-permute-start.15 = (bf16[400,128]{1,0:T(8,128)(2,1)S(1)}, bf16[400,128]{1,0:T(8,128)(2,1)S(1)}, u32[]{:S(2)}, u32[]{:S(2)}) collective-permute-start(bf16[400,128]{1,0:T(8,128)(2,1)S(1)} %get-tuple-element.91), channel_id=1, source_target_pairs={{0,34},{1,35},{2,48},{3,49},{4,38},{5,39},{6,52},{7,53},{8,42},{9,... | collective-permute-start | bytes 307208 | tf_op jit(solution)/shard_map/ppermute | solution.py:25
  118.8 22.8 %collective-permute-start.16 = (bf16[400,128]{1,0:T(8,128)(2,1)S(1)}, bf16[400,128]{1,0:T(8,128)(2,1)S(1)}, u32[]{:S(2)}, u32[]{:S(2)}) collective-permute-start(bf16[400,128]{1,0:T(8,128)(2,1)S(1)} %get-tuple-element.92), channel_id=1, source_target_pairs={{0,16},{1,17},{2,18},{3,19},{4,20},{5,21},{6,22},{7,23},{8,24},{9,... | collective-permute-start | bytes 307208 | tf_op jit(solution)/shard_map/ppermute | solution.py:25
  121.2 20.4 %collective-permute-start.17 = (bf16[400,128]{1,0:T(8,128)(2,1)S(1)}, bf16[400,128]{1,0:T(8,128)(2,1)S(1)}, u32[]{:S(2)}, u32[]{:S(2)}) collective-permute-start(bf16[400,128]{1,0:T(8,128)(2,1)S(1)} %get-tuple-element.93), channel_id=1, source_target_pairs={{0,48},{1,49},{2,50},{3,51},{4,52},{5,53},{6,54},{7,55},{8,56},{9,... | collective-permute-start | bytes 307208 | tf_op jit(solution)/shard_map/ppermute | solution.py:25
  136.4 5.2 %collective-permute-start.18 = (bf16[400,128]{1,0:T(8,128)(2,1)S(1)}, bf16[400,128]{1,0:T(8,128)(2,1)S(1)}, u32[]{:S(2)}, u32[]{:S(2)}) collective-permute-start(bf16[400,128]{1,0:T(8,128)(2,1)S(1)} %get-tuple-element.94), channel_id=1, source_target_pairs={{0,2},{1,3},{2,16},{3,17},{4,6},{5,7},{6,20},{7,21},{8,10},{9,11},... | collective-permute-start | bytes 307208 | tf_op jit(solution)/shard_map/ppermute | solution.py:25
  136.4 5.2 %collective-permute-start.19 = (bf16[400,128]{1,0:T(8,128)(2,1)S(1)}, bf16[400,128]{1,0:T(8,128)(2,1)S(1)}, u32[]{:S(2)}, u32[]{:S(2)}) collective-permute-start(bf16[400,128]{1,0:T(8,128)(2,1)S(1)} %get-tuple-element.95), channel_id=1, source_target_pairs={{0,50},{1,51},{2,0},{3,1},{4,54},{5,55},{6,4},{7,5},{8,58},{9,59},... | collective-permute-start | bytes 307208 | tf_op jit(solution)/shard_map/ppermute | solution.py:25
  141.6 18.1 %collective-permute-start.23 = (f32[112,384]{1,0:T(8,128)S(1)}, f32[112,384]{1,0:T(8,128)S(1)}, u32[]{:S(2)}, u32[]{:S(2)}) collective-permute-start(f32[112,384]{1,0:T(8,128)S(1)} %get-tuple-element.115), channel_id=1, source_target_pairs={{0,64},{1,65},{2,66},{3,67},{4,68},{5,69},{6,70},{7,71},{8,72},{9,... | collective-permute-start | bytes 516104 | tf_op jit(solution)/shard_map/ppermute | solution.py:25
  145.2 10.2 %collective-permute-start.21 = (f32[128,128]{1,0:T(8,128)S(1)}, f32[128,128]{1,0:T(8,128)S(1)}, u32[]{:S(2)}, u32[]{:S(2)}) collective-permute-start(f32[128,128]{1,0:T(8,128)S(1)} %get-tuple-element.112), channel_id=1, source_target_pairs={{0,1},{1,2},{2,3},{3,0},{4,16},{5,17},{6,18},{7,19},{8,32},{9,33},... | collective-permute-start | bytes 196616 | tf_op jit(solution)/shard_map/ppermute | solution.py:25
  145.3 14.4 %collective-permute-start.22 = (f32[128,128]{1,0:T(8,128)S(1)}, f32[128,128]{1,0:T(8,128)S(1)}, u32[]{:S(2)}, u32[]{:S(2)}) collective-permute-start(f32[128,128]{1,0:T(8,128)S(1)} %get-tuple-element.113), channel_id=1, source_target_pairs={{0,0},{1,1},{2,2},{3,3},{4,18},{5,19},{6,16},{7,17},{8,34},{9,35},... | collective-permute-start | bytes 196616 | tf_op jit(solution)/shard_map/ppermute | solution.py:25

commit v6 on v3

--- a/solution.py
+++ b/solution.py
@@ -13,7 +13,7 @@
 SIZES = (4, 4, 4, 2, 2)
 PLACES = list(itertools.product(*(range(n) for n in SIZES)))
 STEPS = (1, 3, 2)
-Z_STEPS = (1, 7, 2, 6, 3, 5, 4)
+Z_STEPS = (4, 3, 5, 2, 6, 1, 7)
 
 
 def number(place):
@@ -365,6 +365,11 @@
     )
 
 
+def last(at_ref, *refs):
+    left_last(at_ref, *refs[:4], refs[6])
+    right_last(at_ref, *refs[4:6], refs[7])
+
+
 def mirror(step):
     def to(x, zh, y, zl, core):
         if zh != y:
@@ -392,7 +397,7 @@
     half = width // 2
 
     cut = lambda parity: lax.dynamic_slice_in_dim(gradient, parity * half, half, 1)
-    near, far, gradient = barrier((cut((zh + 1) % 2), cut(zh % 2), gradient))
+    near, gradient = barrier((cut((zh + 1) % 2), gradient))
     near = send(near, lambda x, zh, y, zl, core: (x, 2 * core + (zh + 1) % 2, y, zl, zh // 2))
 
     window = [((rows, WINDOW), BF16), ((512, 512), BF16), ((512, 128), F32)]
@@ -400,14 +405,15 @@
     over_x = lambda s, v: send(v, lambda x, zh, y, zl, core: (x + s, zh, y, zl, core))
     far_1, far_3 = run(right_far, [half_part] * 2, window, at, gradient)
     far_1, far_3 = over_x(1, far_1), over_x(3, far_3)
-    near, far, far_1, far_3 = barrier((near, far, far_1, far_3))
-    far = send(far, lambda x, zh, y, zl, core: (x, 2 * core + zh % 2, y, zl, zh // 2))
     add = lambda s, v: run(
         functools.partial(right_near, s), [whole_part], window + [((BLOCK, 256), F32)], at, gradient, v
     )[0]
     code_1, code_3 = add(1, far_1), add(3, far_3)
     right_1, right_3 = over_x(1, code_1), over_x(3, code_3)
-
+    near, far, _ = barrier((near, cut(zh % 2), code_3))
+    far = send(far, lambda x, zh, y, zl, core: (x, 2 * core + zh % 2, y, zl, zh // 2))
+
+    near, far, _ = barrier((near, far, code_1))
     swap = lambda x, zh, y, zl, core: (x, zh, y, zl, 1 - core)
     far_2, near_2 = send(far, swap), send(near, swap)
 
@@ -422,9 +428,9 @@
         right_3,
     )
     over_z = lambda s, v: send(v, lambda x, zh, y, zl, core: (x, zh + s, y, zl, core))
-    right_1, right_3 = over_z(1, code_1), over_z(3, code_3)
-
-    far, near, far_2, near_2, _ = barrier((far, near, far_2, near_2, code_1))
+    right_2 = over_z(2, code_2)
+
+    far, near, far_2, near_2, _ = barrier((far, near, far_2, near_2, code_2))
     packed = (ROWS + 16, 256)
     left_1, left_3, left_2, left_own, norms = run(
         left_first,
@@ -438,9 +444,9 @@
     )
     over_y = lambda s, v: send(v, lambda x, zh, y, zl, core: (x, zh, y + s, zl, core))
     left_1, left_3 = over_y(1, left_1), over_y(3, left_3)
-    left_2, right_1, right_3 = barrier((left_2, right_1, right_3))
-    left_1, left_3, code_2, right_1, right_3 = barrier((left_1, left_3, code_2, right_1, right_3))
-    left_2, right_2 = over_y(2, left_2), over_z(2, code_2)
+    left_2, right_2 = barrier((left_2, right_2))
+    left_1, left_3, code_1, code_3, right_2 = barrier((left_1, left_3, code_1, code_3, right_2))
+    left_2, right_1, right_3 = over_y(2, left_2), over_z(1, code_1), over_z(3, code_3)
 
     piece = (400, SUB)
     codes = run(
@@ -469,7 +475,6 @@
     )
     arrived, image = barrier((arrived, image))
     image = over_x(1, image)
-    right_gram = run(right_last, [((CHUNK, width), F32)], [], at, right_base, image)[0]
 
     square = ((SUB, SUB), F32)
     base, more, same, other = run(
@@ -481,7 +486,9 @@
         *arrived,
     )
     same, other = send(same, mirror(0)), send(other, mirror(1))
-    left_gram = run(left_last, [((512, SUB), F32)], [], at, base, more, same, other)[0]
+    left_gram, right_gram = run(
+        last, [((512, SUB), F32), ((CHUNK, width), F32)], [], at, base, more, same, other, right_base, image
+    )
     return (left_gram, right_gram)
 
 

time: 170 us -> 164 us (0.965)
  waiting for transfers between devices: 84.5 us -> 72.5 us
  starting transfers between devices: 52.4 us -> 57.9 us
    ppermute x24, waiting for transfers between devices: 84.5 us -> 72.5 us  [send(): lax.ppermute(array, ('row', 'col'), [(number(p), number(to(*p))) for p in...]
    ppermute x24, starting transfers between devices: 52.4 us -> 57.9 us  [send(): lax.ppermute(array, ('row', 'col'), [(number(p), number(to(*p))) for p in...]
    pallas_call x10 -> x9, Pallas kernels: 27.7 us -> 28.3 us  [run(): pl.pallas_call(body, out_shape=[jax.ShapeDtypeStruct(shape, dtype) for sh...]
  transfers between devices with their start and end apart: 24 -> 24, of which waited for: 16 -> 10; matrix products, arithmetic and copies ran while one was open for 0% -> 0% of each run, Pallas kernels for 15% -> 16%
where the time goes in v6:
time: 164 us; the launch traced here: 163 us
  waiting for transfers between devices  72.5 us (44%)
  starting transfers between devices  57.9 us (35%)
  Pallas kernels  28.3 us (17%)
  local copies, waits for them, and re-layouts  3.75 us (2%)
    ppermute x24, waiting for transfers between devices, send(): lax.ppermute(array, ('row', 'col'), [(number(p), number(to(*p))) for p in...  72.5 us
    ppermute x24, starting transfers between devices, send(): lax.ppermute(array, ('row', 'col'), [(number(p), number(to(*p))) for p in...  57.9 us
    pallas_call x9, Pallas kernels, run(): pl.pallas_call(body, out_shape=[jax.ShapeDtypeStruct(shape, dtype) for sh...  28.3 us
  transfers between devices with their start and end apart: 24, of which 10 were waited for; matrix products, arithmetic and copies ran while one was open for 0% of the time, Pallas kernels for 16%

profile of v6, /device:TPU:25, one launch (start us, length us, event | category | flops | bytes accessed | tf_op | source)
XLA Modules:
  0.0 163.2 jit_solution(1129575834876436779)
XLA Ops:
  0.7 2.3 %constant_dynamic-slice_fusion.1 = bf16[512,896]{1,0:T(8,128)(2,1)} fusion(bf16[512,1792]{1,0:T(8,128)(2,1)} %g_ref.3, s32[]{:T(128)S(6)} %select_n.46), kind=kLoop, calls=%fused_computation.1 | loop fusion | bytes 1835012 | tf_op jit(solution)/shard_map/dynamic_slice | solution.py:399
  3.0 6.6 %collective-permute-start = (bf16[512,896]{1,0:T(8,128)(2,1)}, bf16[512,896]{1,0:T(8,128)(2,1)S(1)}, u32[]{:S(2)}, u32[]{:S(2)}) collective-permute-start(bf16[512,896]{1,0:T(8,128)(2,1)} %constant_dynamic-slice_fusion.1), channel_id=1, source_target_pairs={{0,16},{1,48},{2,18},{3,50},{4,20},{5,52},{6,22},{7,54},{8,24},{9,... | collective-permute-start | bytes 2752520 | tf_op jit(solution)/shard_map/ppermute | solution.py:25
  9.7 3.1 %shard_map.30 = (bf16[240,1408]{1,0:T(8,128)(2,1)}, bf16[240,1408]{1,0:T(8,128)(2,1)}) custom-call(s32[8]{0:T(128)S(1)} %stack.26.at_ref, bf16[512,1792]{1,0:T(8,128)(2,1)S(1)} %copy-done), custom_call_target="tpu_custom_call" | custom-call | flops 1000 | bytes 1000 | tf_op jit(solution)/shard_map/pallas_call | solution.py:68
  12.7 2.5 %collective-permute-start.1 = (bf16[240,1408]{1,0:T(8,128)(2,1)}, bf16[240,1408]{1,0:T(8,128)(2,1)}, u32[]{:S(2)}, u32[]{:S(2)}) collective-permute-start(bf16[240,1408]{1,0:T(8,128)(2,1)} %get-tuple-element.56), channel_id=1, source_target_pairs={{0,192},{1,193},{2,194},{3,195},{4,196},{5,197},{6,198},{7,199},{8... | collective-permute-start | bytes 2027528 | tf_op jit(solution)/shard_map/ppermute | solution.py:25
  15.3 13.1 %collective-permute-done.1.in_ref = bf16[240,1408]{1,0:T(8,128)(2,1)} collective-permute-done((bf16[240,1408]{1,0:T(8,128)(2,1)}, bf16[240,1408]{1,0:T(8,128)(2,1)}, u32[]{:S(2)}, u32[]{:S(2)}) %collective-permute-start.1) | collective-permute-done | bytes 675872 | tf_op jit(solution)/shard_map/ppermute | solution.py:25
  28.3 3.1 %shard_map.31 = bf16[464,1408]{1,0:T(8,128)(2,1)S(1)} custom-call(s32[8]{0:T(128)S(1)} %stack.26.at_ref, bf16[512,1792]{1,0:T(8,128)(2,1)S(1)} %copy-done, bf16[240,1408]{1,0:T(8,128)(2,1)} %collective-permute-done.1.in_ref), custom_call_target="tpu_custom_call" | custom-call | flops 1000 | bytes 1000 | tf_op jit(solution)/shard_map/pallas_call | solution.py:68
  31.5 5.8 %collective-permute-start.2 = (bf16[512,896]{1,0:T(8,128)(2,1)S(1)}, bf16[512,896]{1,0:T(8,128)(2,1)S(1)}, u32[]{:S(2)}, u32[]{:S(2)}) collective-permute-start(bf16[512,896]{1,0:T(8,128)(2,1)S(1)} %constant_dynamic-slice_fusion), channel_id=1, source_target_pairs={{0,0},{1,32},{2,2},{3,34},{4,4},{5,36},{6,6},{7,38},{8,8},{9,40},{... | collective-permute-start | bytes 2752520 | tf_op jit(solution)/shard_map/ppermute | solution.py:25
  37.3 2.5 %shard_map.32 = bf16[464,1408]{1,0:T(8,128)(2,1)S(1)} custom-call(s32[8]{0:T(128)S(1)} %stack.26.at_ref, bf16[512,1792]{1,0:T(8,128)(2,1)S(1)} %copy-done, bf16[240,1408]{1,0:T(8,128)(2,1)S(1)} %collective-permute-done.3.in_ref), custom_call_target="tpu_custom_call" | custom-call | flops 1000 | bytes 1000 | tf_op jit(solution)/shard_map/pallas_call | solution.py:68
  41.0 2.3 %collective-permute-start.7 = (bf16[464,1408]{1,0:T(8,128)(2,1)S(1)}, bf16[464,1408]{1,0:T(8,128)(2,1)S(1)}, u32[]{:S(2)}, u32[]{:S(2)}) collective-permute-start(bf16[464,1408]{1,0:T(8,128)(2,1)S(1)} %shard_map.31), channel_id=1, source_target_pairs={{0,192},{1,193},{2,194},{3,195},{4,196},{5,197},{6,198},{7,199},{8... | collective-permute-start | bytes 3919880 | tf_op jit(solution)/shard_map/ppermute | solution.py:25
  43.4 16.7 %collective-permute-done.2.far = bf16[512,896]{1,0:T(8,128)(2,1)S(1)} collective-permute-done((bf16[512,896]{1,0:T(8,128)(2,1)S(1)}, bf16[512,896]{1,0:T(8,128)(2,1)S(1)}, u32[]{:S(2)}, u32[]{:S(2)}) %collective-permute-start.2) | collective-permute-done | bytes 917536 | tf_op jit(solution)/shard_map/ppermute | solution.py:25
  60.5 5.0 %collective-permute-done.6.in_1 = bf16[464,1408]{1,0:T(8,128)(2,1)S(1)} collective-permute-done((bf16[464,1408]{1,0:T(8,128)(2,1)S(1)}, bf16[464,1408]{1,0:T(8,128)(2,1)S(1)}, u32[]{:S(2)}, u32[]{:S(2)}) %collective-permute-start.6) | collective-permute-done | bytes 1306656 | tf_op jit(solution)/shard_map/ppermute | solution.py:25
  65.5 5.5 %shard_map.33 = (bf16[112,1920]{1,0:T(8,128)(2,1)S(1)}, bf16[112,1920]{1,0:T(8,128)(2,1)S(1)}, bf16[112,1920]{1,0:T(8,128)(2,1)S(1)}, f32[112,1920]{1,0:T(8,128)S(1)}) custom-call(s32[8]{0:T(128)S(1)} %stack.26.at_ref, bf16[512,1792]{1,0:T(8,128)(2,1)} %g_ref.3, bf16[464,1408]{1,0:T(8,128)(2,1)S(1)} %collective-permute-done.6.in_1, ...), custom_call_target="tpu_custom_call" | custom-call | flops 1000 | bytes 1000 | tf_op jit(solution)/shard_map/pallas_call | solution.py:68
  71.0 2.3 %collective-permute-start.10 = (bf16[112,1920]{1,0:T(8,128)(2,1)S(1)}, bf16[112,1920]{1,0:T(8,128)(2,1)S(1)}, u32[]{:S(2)}, u32[]{:S(2)}) collective-permute-start(bf16[112,1920]{1,0:T(8,128)(2,1)S(1)} %get-tuple-element.62), channel_id=1, source_target_pairs={{0,32},{1,33},{2,34},{3,35},{4,36},{5,37},{6,38},{7,39},{8,40},{9,... | collective-permute-start | bytes 1290248 | tf_op jit(solution)/shard_map/ppermute | solution.py:25
  73.4 5.9 %shard_map.34 = (bf16[1168,256]{1,0:T(8,128)(2,1)S(1)}, bf16[1168,256]{1,0:T(8,128)(2,1)S(1)}, bf16[1168,256]{1,0:T(8,128)(2,1)S(1)}, f32[1152,256]{1,0:T(8,128)}, f32[16,128]{1,0:T(8,128)S(1)}) custom-call(s32[8]{0:T(128)S(1)} %stack.26.at_ref, bf16[512,896]{1,0:T(8,128)(2,1)S(1)} %collective-permute-done.2.far, ...), custom_call_target="tpu_custom_call" | custom-call | flops 1000 | bytes 1000 | tf_op jit(solution)/shard_map/pallas_call | solution.py:68
  79.2 1.5 collective-permute-start.9
  80.7 14.7 %collective-permute-done.10.in_2 = bf16[112,1920]{1,0:T(8,128)(2,1)S(1)} collective-permute-done((bf16[112,1920]{1,0:T(8,128)(2,1)S(1)}, bf16[112,1920]{1,0:T(8,128)(2,1)S(1)}, u32[]{:S(2)}, u32[]{:S(2)}) %collective-permute-start.10) | collective-permute-done | bytes 430112 | tf_op jit(solution)/shard_map/ppermute | solution.py:25
  96.4 3.6 %collective-permute-start.20 = (bf16[112,1920]{1,0:T(8,128)(2,1)S(1)}, bf16[112,1920]{1,0:T(8,128)(2,1)S(1)}, u32[]{:S(2)}, u32[]{:S(2)}) collective-permute-start(bf16[112,1920]{1,0:T(8,128)(2,1)S(1)} %get-tuple-element.88), channel_id=1, source_target_pairs={{0,48},{1,49},{2,50},{3,51},{4,52},{5,53},{6,54},{7,55},{8,56},{9,... | collective-permute-start | bytes 1290248 | tf_op jit(solution)/shard_map/ppermute | solution.py:25
  100.0 10.7 %collective-permute-done.11.in_2 = bf16[1168,256]{1,0:T(8,128)(2,1)S(1)} collective-permute-done((bf16[1168,256]{1,0:T(8,128)(2,1)S(1)}, bf16[1168,256]{1,0:T(8,128)(2,1)S(1)}, u32[]{:S(2)}, u32[]{:S(2)}) %collective-permute-start.11) | collective-permute-done | bytes 598048 | tf_op jit(solution)/shard_map/ppermute | solution.py:25
  110.7 1.3 copy-done.1
  112.0 2.7 %shard_map.35 = (bf16[400,128]{1,0:T(8,128)(2,1)S(1)}, bf16[400,128]{1,0:T(8,128)(2,1)S(1)}, bf16[400,128]{1,0:T(8,128)(2,1)S(1)}, bf16[400,128]{1,0:T(8,128)(2,...) custom-call(s32[8]{0:T(128)S(1)} %stack.26.at_ref, ...), custom_call_target="tpu_custom_call" | custom-call | flops 1000 | bytes 1000 | tf_op jit(solution)/shard_map/pallas_call | solution.py:68
  115.8 4.1 %collective-permute-start.13 = (bf16[400,128]{1,0:T(8,128)(2,1)S(1)}, bf16[400,128]{1,0:T(8,128)(2,1)S(1)}, u32[]{:S(2)}, u32[]{:S(2)}) collective-permute-start(bf16[400,128]{1,0:T(8,128)(2,1)S(1)} %get-tuple-element.80), channel_id=1, source_target_pairs={{0,18},{1,19},{2,32},{3,33},{4,22},{5,23},{6,36},{7,37},{8,26},{9,... | collective-permute-start | bytes 307208 | tf_op jit(solution)/shard_map/ppermute | solution.py:25
  120.6 1.7 %collective-permute-done.12.refs_1_ = bf16[400,128]{1,0:T(8,128)(2,1)S(1)} collective-permute-done((bf16[400,128]{1,0:T(8,128)(2,1)S(1)}, bf16[400,128]{1,0:T(8,128)(2,1)S(1)}, u32[]{:S(2)}, u32[]{:S(2)}) %collective-permute-start.12) | collective-permute-done | bytes 102432 | tf_op jit(solution)/shard_map/ppermute | solution.py:25
  122.3 2.5 %collective-permute-done.13.refs_2_ = bf16[400,128]{1,0:T(8,128)(2,1)S(1)} collective-permute-done((bf16[400,128]{1,0:T(8,128)(2,1)S(1)}, bf16[400,128]{1,0:T(8,128)(2,1)S(1)}, u32[]{:S(2)}, u32[]{:S(2)}) %collective-permute-start.13) | collective-permute-done | bytes 102432 | tf_op jit(solution)/shard_map/ppermute | solution.py:25
  124.8 13.0 %collective-permute-start.16 = (bf16[400,128]{1,0:T(8,128)(2,1)S(1)}, bf16[400,128]{1,0:T(8,128)(2,1)S(1)}, u32[]{:S(2)}, u32[]{:S(2)}) collective-permute-start(bf16[400,128]{1,0:T(8,128)(2,1)S(1)} %get-tuple-element.83), channel_id=1, source_target_pairs={{0,48},{1,49},{2,50},{3,51},{4,52},{5,53},{6,54},{7,55},{8,56},{9,... | collective-permute-start | bytes 307208 | tf_op jit(solution)/shard_map/ppermute | solution.py:25
  137.8 2.7 %collective-permute-start.18 = (bf16[400,128]{1,0:T(8,128)(2,1)S(1)}, bf16[400,128]{1,0:T(8,128)(2,1)S(1)}, u32[]{:S(2)}, u32[]{:S(2)}) collective-permute-start(bf16[400,128]{1,0:T(8,128)(2,1)S(1)} %get-tuple-element.85), channel_id=1, source_target_pairs={{0,50},{1,51},{2,0},{3,1},{4,54},{5,55},{6,4},{7,5},{8,58},{9,59},... | collective-permute-start | bytes 307208 | tf_op jit(solution)/shard_map/ppermute | solution.py:25
  140.5 2.5 %shard_map.36 = (f32[112,1408]{1,0:T(8,128)S(1)}, f32[112,384]{1,0:T(8,128)S(1)}) custom-call(s32[8]{0:T(128)S(1)} %stack.26.at_ref, f32[112,1920]{1,0:T(8,128)S(1)} %get-tuple-element.86.own_ref, bf16[112,1920]{1,0:T(8,128)(2,1)S(1)} %collective-permute-done.19.in_1, bf16[112,1920]{1,0:T(8,128)(2,1)S(1)} %collective-permute-done.20.in_3, ...), custom_call_target="tpu_custom_call" | custom-call | flops 1000 | bytes 1000 | tf_op jit(solution)/shard_map/pallas_call | solution.py:68
  143.5 2.4 %collective-permute-start.23 = (f32[112,384]{1,0:T(8,128)S(1)}, f32[112,384]{1,0:T(8,128)S(1)}, u32[]{:S(2)}, u32[]{:S(2)}) collective-permute-start(f32[112,384]{1,0:T(8,128)S(1)} %get-tuple-element.105), channel_id=1, source_target_pairs={{0,64},{1,65},{2,66},{3,67},{4,68},{5,69},{6,70},{7,71},{8,72},{9,... | collective-permute-start | bytes 516104 | tf_op jit(solution)/shard_map/ppermute | solution.py:25
  145.9 1.4 shard_map.37
  147.4 6.4 %collective-permute-start.22 = (f32[128,128]{1,0:T(8,128)S(1)}, f32[128,128]{1,0:T(8,128)S(1)}, u32[]{:S(2)}, u32[]{:S(2)}) collective-permute-start(f32[128,128]{1,0:T(8,128)S(1)} %get-tuple-element.103), channel_id=1, source_target_pairs={{0,0},{1,1},{2,2},{3,3},{4,18},{5,19},{6,16},{7,17},{8,34},{9,35},... | collective-permute-start | bytes 196616 | tf_op jit(solution)/shard_map/ppermute | solution.py:25
  153.9 2.5 %collective-permute-done.21.refs_2_ = f32[128,128]{1,0:T(8,128)S(1)} collective-permute-done((f32[128,128]{1,0:T(8,128)S(1)}, f32[128,128]{1,0:T(8,128)S(1)}, u32[]{:S(2)}, u32[]{:S(2)}) %collective-permute-start.21) | collective-permute-done | bytes 65568 | tf_op jit(solution)/shard_map/ppermute | solution.py:25
  156.3 5.2 %collective-permute-done.22.refs_3_ = f32[128,128]{1,0:T(8,128)S(1)} collective-permute-done((f32[128,128]{1,0:T(8,128)S(1)}, f32[128,128]{1,0:T(8,128)S(1)}, u32[]{:S(2)}, u32[]{:S(2)}) %collective-permute-start.22) | collective-permute-done | bytes 65568 | tf_op jit(solution)/shard_map/ppermute | solution.py:25
  161.5 1.6 %shard_map.38 = (f32[512,128]{1,0:T(8,128)}, f32[112,1792]{1,0:T(8,128)}) custom-call(s32[8]{0:T(128)S(1)} %stack.26.at_ref, f32[256,128]{1,0:T(8,128)S(1)} %get-tuple-element.100.refs_0_, f32[128,128]{1,0:T(8,128)S(1)} %get-tuple-element.101.refs_1_, f32[128,128]{1,0:T(8,128)S(1)} %collective-permute-done.21.refs_2_, ...), custom_call_target="tpu_custom_call" | custom-call | flops 1000 | bytes 1000 | tf_op jit(solution)/shard_map/pallas_call | solution.py:68
  (32 shorter events, 5.4 us)
Async XLA Ops:
  0.6 9.0 %copy-start = (bf16[512,1792]{1,0:T(8,128)(2,1)S(1)}, bf16[512,1792]{1,0:T(8,128)(2,1)}, u32[]{:S(2)}) copy-start(bf16[512,1792]{1,0:T(8,128)(2,1)} %g_ref.3) | copy-start | bytes 5505028
  3.0 28.5 %collective-permute-start = (bf16[512,896]{1,0:T(8,128)(2,1)}, bf16[512,896]{1,0:T(8,128)(2,1)S(1)}, u32[]{:S(2)}, u32[]{:S(2)}) collective-permute-start(bf16[512,896]{1,0:T(8,128)(2,1)} %constant_dynamic-slice_fusion.1), channel_id=1, source_target_pairs={{0,16},{1,48},{2,18},{3,50},{4,20},{5,52},{6,22},{7,54},{8,24},{9,... | collective-permute-start | bytes 2752520 | tf_op jit(solution)/shard_map/ppermute | solution.py:25
  12.7 15.6 %collective-permute-start.1 = (bf16[240,1408]{1,0:T(8,128)(2,1)}, bf16[240,1408]{1,0:T(8,128)(2,1)}, u32[]{:S(2)}, u32[]{:S(2)}) collective-permute-start(bf16[240,1408]{1,0:T(8,128)(2,1)} %get-tuple-element.56), channel_id=1, source_target_pairs={{0,192},{1,193},{2,194},{3,195},{4,196},{5,197},{6,198},{7,199},{8... | collective-permute-start | bytes 2027528 | tf_op jit(solution)/shard_map/ppermute | solution.py:25
  15.2 22.1 %collective-permute-start.3 = (bf16[240,1408]{1,0:T(8,128)(2,1)}, bf16[240,1408]{1,0:T(8,128)(2,1)S(1)}, u32[]{:S(2)}, u32[]{:S(2)}) collective-permute-start(bf16[240,1408]{1,0:T(8,128)(2,1)} %get-tuple-element.59), channel_id=1, source_target_pairs={{0,64},{1,65},{2,66},{3,67},{4,68},{5,69},{6,70},{7,71},{8,72},{9,... | collective-permute-start | bytes 2027528 | tf_op jit(solution)/shard_map/ppermute | solution.py:25
  31.5 28.5 %collective-permute-start.2 = (bf16[512,896]{1,0:T(8,128)(2,1)S(1)}, bf16[512,896]{1,0:T(8,128)(2,1)S(1)}, u32[]{:S(2)}, u32[]{:S(2)}) collective-permute-start(bf16[512,896]{1,0:T(8,128)(2,1)S(1)} %constant_dynamic-slice_fusion), channel_id=1, source_target_pairs={{0,0},{1,32},{2,2},{3,34},{4,4},{5,36},{6,6},{7,38},{8,8},{9,40},{... | collective-permute-start | bytes 2752520 | tf_op jit(solution)/shard_map/ppermute | solution.py:25
  39.8 25.7 %collective-permute-start.6 = (bf16[464,1408]{1,0:T(8,128)(2,1)S(1)}, bf16[464,1408]{1,0:T(8,128)(2,1)S(1)}, u32[]{:S(2)}, u32[]{:S(2)}) collective-permute-start(bf16[464,1408]{1,0:T(8,128)(2,1)S(1)} %shard_map.32), channel_id=1, source_target_pairs={{0,64},{1,65},{2,66},{3,67},{4,68},{5,69},{6,70},{7,71},{8,72},{9,... | collective-permute-start | bytes 3919880 | tf_op jit(solution)/shard_map/ppermute | solution.py:25
  41.0 24.5 %collective-permute-start.7 = (bf16[464,1408]{1,0:T(8,128)(2,1)S(1)}, bf16[464,1408]{1,0:T(8,128)(2,1)S(1)}, u32[]{:S(2)}, u32[]{:S(2)}) collective-permute-start(bf16[464,1408]{1,0:T(8,128)(2,1)S(1)} %shard_map.31), channel_id=1, source_target_pairs={{0,192},{1,193},{2,194},{3,195},{4,196},{5,197},{6,198},{7,199},{8... | collective-permute-start | bytes 3919880 | tf_op jit(solution)/shard_map/ppermute | solution.py:25
  60.0 13.3 %collective-permute-start.4 = (bf16[512,896]{1,0:T(8,128)(2,1)S(1)}, bf16[512,896]{1,0:T(8,128)(2,1)S(1)}, u32[]{:S(2)}, u32[]{:S(2)}) collective-permute-start(bf16[512,896]{1,0:T(8,128)(2,1)S(1)} %collective-permute-done.2.far), channel_id=1, source_target_pairs={{0,1},{1,0},{2,3},{3,2},{4,5},{5,4},{6,7},{7,6},{8,9},{9,8},{10,11... | collective-permute-start | bytes 2752520 | tf_op jit(solution)/shard_map/ppermute | solution.py:25
  60.0 13.3 %collective-permute-start.5 = (bf16[512,896]{1,0:T(8,128)(2,1)S(1)}, bf16[512,896]{1,0:T(8,128)(2,1)S(1)}, u32[]{:S(2)}, u32[]{:S(2)}) collective-permute-start(bf16[512,896]{1,0:T(8,128)(2,1)S(1)} %collective-permute-done.near), channel_id=1, source_target_pairs={{0,1},{1,0},{2,3},{3,2},{4,5},{5,4},{6,7},{7,6},{8,9},{9,8},{10,11... | collective-permute-start | bytes 2752520 | tf_op jit(solution)/shard_map/ppermute | solution.py:25
  71.0 24.4 %collective-permute-start.10 = (bf16[112,1920]{1,0:T(8,128)(2,1)S(1)}, bf16[112,1920]{1,0:T(8,128)(2,1)S(1)}, u32[]{:S(2)}, u32[]{:S(2)}) collective-permute-start(bf16[112,1920]{1,0:T(8,128)(2,1)S(1)} %get-tuple-element.62), channel_id=1, source_target_pairs={{0,32},{1,33},{2,34},{3,35},{4,36},{5,37},{6,38},{7,39},{8,40},{9,... | collective-permute-start | bytes 1290248 | tf_op jit(solution)/shard_map/ppermute | solution.py:25
  79.2 17.2 %collective-permute-start.8 = (bf16[1168,256]{1,0:T(8,128)(2,1)S(1)}, bf16[1168,256]{1,0:T(8,128)(2,1)S(1)}, u32[]{:S(2)}, u32[]{:S(2)}) collective-permute-start(bf16[1168,256]{1,0:T(8,128)(2,1)S(1)} %get-tuple-element.69), channel_id=1, source_target_pairs={{0,4},{1,5},{2,6},{3,7},{4,8},{5,9},{6,10},{7,11},{8,12},{9,13},{1... | collective-permute-start | bytes 1794056 | tf_op jit(solution)/shard_map/ppermute | solution.py:25
  79.2 17.2 %collective-permute-start.9 = (bf16[1168,256]{1,0:T(8,128)(2,1)S(1)}, bf16[1168,256]{1,0:T(8,128)(2,1)S(1)}, u32[]{:S(2)}, u32[]{:S(2)}) collective-permute-start(bf16[1168,256]{1,0:T(8,128)(2,1)S(1)} %get-tuple-element.70), channel_id=1, source_target_pairs={{0,12},{1,13},{2,14},{3,15},{4,0},{5,1},{6,2},{7,3},{8,4},{9,5},{1... | collective-permute-start | bytes 1794056 | tf_op jit(solution)/shard_map/ppermute | solution.py:25
  95.4 15.3 %collective-permute-start.11 = (bf16[1168,256]{1,0:T(8,128)(2,1)S(1)}, bf16[1168,256]{1,0:T(8,128)(2,1)S(1)}, u32[]{:S(2)}, u32[]{:S(2)}) collective-permute-start(bf16[1168,256]{1,0:T(8,128)(2,1)S(1)} %get-tuple-element.77), channel_id=1, source_target_pairs={{0,8},{1,9},{2,10},{3,11},{4,12},{5,13},{6,14},{7,15},{8,0},{9,1},... | collective-permute-start | bytes 1794056 | tf_op jit(solution)/shard_map/ppermute | solution.py:25
  96.4 41.4 %collective-permute-start.19 = (bf16[112,1920]{1,0:T(8,128)(2,1)S(1)}, bf16[112,1920]{1,0:T(8,128)(2,1)S(1)}, u32[]{:S(2)}, u32[]{:S(2)}) collective-permute-start(bf16[112,1920]{1,0:T(8,128)(2,1)S(1)} %get-tuple-element.87), channel_id=1, source_target_pairs={{0,16},{1,17},{2,18},{3,19},{4,20},{5,21},{6,22},{7,23},{8,24},{9,... | collective-permute-start | bytes 1290248 | tf_op jit(solution)/shard_map/ppermute | solution.py:25
  96.4 41.4 %collective-permute-start.20 = (bf16[112,1920]{1,0:T(8,128)(2,1)S(1)}, bf16[112,1920]{1,0:T(8,128)(2,1)S(1)}, u32[]{:S(2)}, u32[]{:S(2)}) collective-permute-start(bf16[112,1920]{1,0:T(8,128)(2,1)S(1)} %get-tuple-element.88), channel_id=1, source_target_pairs={{0,48},{1,49},{2,50},{3,51},{4,52},{5,53},{6,54},{7,55},{8,56},{9,... | collective-permute-start | bytes 1290248 | tf_op jit(solution)/shard_map/ppermute | solution.py:25
  110.7 1.3 copy-start.1
  114.6 7.7 %collective-permute-start.12 = (bf16[400,128]{1,0:T(8,128)(2,1)S(1)}, bf16[400,128]{1,0:T(8,128)(2,1)S(1)}, u32[]{:S(2)}, u32[]{:S(2)}) collective-permute-start(bf16[400,128]{1,0:T(8,128)(2,1)S(1)} %get-tuple-element.79), channel_id=1, source_target_pairs={{0,32},{1,33},{2,34},{3,35},{4,36},{5,37},{6,38},{7,39},{8,40},{9,... | collective-permute-start | bytes 307208 | tf_op jit(solution)/shard_map/ppermute | solution.py:25
  115.8 9.0 %collective-permute-start.13 = (bf16[400,128]{1,0:T(8,128)(2,1)S(1)}, bf16[400,128]{1,0:T(8,128)(2,1)S(1)}, u32[]{:S(2)}, u32[]{:S(2)}) collective-permute-start(bf16[400,128]{1,0:T(8,128)(2,1)S(1)} %get-tuple-element.80), channel_id=1, source_target_pairs={{0,18},{1,19},{2,32},{3,33},{4,22},{5,23},{6,36},{7,37},{8,26},{9,... | collective-permute-start | bytes 307208 | tf_op jit(solution)/shard_map/ppermute | solution.py:25
  119.9 23.1 %collective-permute-start.14 = (bf16[400,128]{1,0:T(8,128)(2,1)S(1)}, bf16[400,128]{1,0:T(8,128)(2,1)S(1)}, u32[]{:S(2)}, u32[]{:S(2)}) collective-permute-start(bf16[400,128]{1,0:T(8,128)(2,1)S(1)} %get-tuple-element.81), channel_id=1, source_target_pairs={{0,34},{1,35},{2,48},{3,49},{4,38},{5,39},{6,52},{7,53},{8,42},{9,... | collective-permute-start | bytes 307208 | tf_op jit(solution)/shard_map/ppermute | solution.py:25
  122.3 20.7 %collective-permute-start.15 = (bf16[400,128]{1,0:T(8,128)(2,1)S(1)}, bf16[400,128]{1,0:T(8,128)(2,1)S(1)}, u32[]{:S(2)}, u32[]{:S(2)}) collective-permute-start(bf16[400,128]{1,0:T(8,128)(2,1)S(1)} %get-tuple-element.82), channel_id=1, source_target_pairs={{0,16},{1,17},{2,18},{3,19},{4,20},{5,21},{6,22},{7,23},{8,24},{9,... | collective-permute-start | bytes 307208 | tf_op jit(solution)/shard_map/ppermute | solution.py:25
  124.8 18.2 %collective-permute-start.16 = (bf16[400,128]{1,0:T(8,128)(2,1)S(1)}, bf16[400,128]{1,0:T(8,128)(2,1)S(1)}, u32[]{:S(2)}, u32[]{:S(2)}) collective-permute-start(bf16[400,128]{1,0:T(8,128)(2,1)S(1)} %get-tuple-element.83), channel_id=1, source_target_pairs={{0,48},{1,49},{2,50},{3,51},{4,52},{5,53},{6,54},{7,55},{8,56},{9,... | collective-permute-start | bytes 307208 | tf_op jit(solution)/shard_map/ppermute | solution.py:25
  137.8 5.7 %collective-permute-start.17 = (bf16[400,128]{1,0:T(8,128)(2,1)S(1)}, bf16[400,128]{1,0:T(8,128)(2,1)S(1)}, u32[]{:S(2)}, u32[]{:S(2)}) collective-permute-start(bf16[400,128]{1,0:T(8,128)(2,1)S(1)} %get-tuple-element.84), channel_id=1, source_target_pairs={{0,2},{1,3},{2,16},{3,17},{4,6},{5,7},{6,20},{7,21},{8,10},{9,11},... | collective-permute-start | bytes 307208 | tf_op jit(solution)/shard_map/ppermute | solution.py:25
  137.8 5.7 %collective-permute-start.18 = (bf16[400,128]{1,0:T(8,128)(2,1)S(1)}, bf16[400,128]{1,0:T(8,128)(2,1)S(1)}, u32[]{:S(2)}, u32[]{:S(2)}) collective-permute-start(bf16[400,128]{1,0:T(8,128)(2,1)S(1)} %get-tuple-element.85), channel_id=1, source_target_pairs={{0,50},{1,51},{2,0},{3,1},{4,54},{5,55},{6,4},{7,5},{8,58},{9,59},... | collective-permute-start | bytes 307208 | tf_op jit(solution)/shard_map/ppermute | solution.py:25
  143.5 18.0 %collective-permute-start.23 = (f32[112,384]{1,0:T(8,128)S(1)}, f32[112,384]{1,0:T(8,128)S(1)}, u32[]{:S(2)}, u32[]{:S(2)}) collective-permute-start(f32[112,384]{1,0:T(8,128)S(1)} %get-tuple-element.105), channel_id=1, source_target_pairs={{0,64},{1,65},{2,66},{3,67},{4,68},{5,69},{6,70},{7,71},{8,72},{9,... | collective-permute-start | bytes 516104 | tf_op jit(solution)/shard_map/ppermute | solution.py:25
  147.3 9.0 %collective-permute-start.21 = (f32[128,128]{1,0:T(8,128)S(1)}, f32[128,128]{1,0:T(8,128)S(1)}, u32[]{:S(2)}, u32[]{:S(2)}) collective-permute-start(f32[128,128]{1,0:T(8,128)S(1)} %get-tuple-element.102), channel_id=1, source_target_pairs={{0,1},{1,2},{2,3},{3,0},{4,16},{5,17},{6,18},{7,19},{8,32},{9,33},... | collective-permute-start | bytes 196616 | tf_op jit(solution)/shard_map/ppermute | solution.py:25
  147.4 14.1 %collective-permute-start.22 = (f32[128,128]{1,0:T(8,128)S(1)}, f32[128,128]{1,0:T(8,128)S(1)}, u32[]{:S(2)}, u32[]{:S(2)}) collective-permute-start(f32[128,128]{1,0:T(8,128)S(1)} %get-tuple-element.103), channel_id=1, source_target_pairs={{0,0},{1,1},{2,2},{3,3},{4,18},{5,19},{6,16},{7,17},{8,34},{9,35},... | collective-permute-start | bytes 196616 | tf_op jit(solution)/shard_map/ppermute | solution.py:25

commit v7 on v5

--- a/solution.py
+++ b/solution.py
@@ -13,7 +13,7 @@
 SIZES = (4, 4, 4, 2, 2)
 PLACES = list(itertools.product(*(range(n) for n in SIZES)))
 STEPS = (1, 3, 2)
-Z_STEPS = (4, 3, 5, 2, 6, 1, 7)
+Z_STEPS = (1, 4, 7, 3, 5, 2, 6)
 
 
 def number(place):

time: 162 us -> 164 us (1.012); the launches traced: 161 us -> 160 us
  starting transfers between devices: 57.3 us -> 50.2 us
  waiting for transfers between devices: 67.6 us -> 73.8 us
    ppermute x24, starting transfers between devices: 57.3 us -> 50.2 us  [send(): lax.ppermute(array, ('row', 'col'), [(number(p), number(to(*p))) for p in...]
    ppermute x24, waiting for transfers between devices: 67.6 us -> 73.8 us  [send(): lax.ppermute(array, ('row', 'col'), [(number(p), number(to(*p))) for p in...]
  transfers between devices with their start and end apart: 24 -> 24, of which waited for: 11 -> 13; matrix products, arithmetic and copies ran while one was open for 0% -> 0% of each run, Pallas kernels for 18% -> 18%
where the time goes in v7:
time: 164 us; the launch traced here: 160 us
  waiting for transfers between devices  73.8 us (45%)
  starting transfers between devices  50.2 us (31%)
  Pallas kernels  30.5 us (19%)
  local copies, waits for them, and re-layouts  5.23 us (3%)
    ppermute x24, waiting for transfers between devices, send(): lax.ppermute(array, ('row', 'col'), [(number(p), number(to(*p))) for p in...  73.8 us
    ppermute x24, starting transfers between devices, send(): lax.ppermute(array, ('row', 'col'), [(number(p), number(to(*p))) for p in...  50.2 us
    pallas_call x10, Pallas kernels, run(): pl.pallas_call(body, out_shape=[jax.ShapeDtypeStruct(shape, dtype) for sh...  30.5 us
  transfers between devices with their start and end apart: 24, of which 13 were waited for; matrix products, arithmetic and copies ran while one was open for 0% of the time, Pallas kernels for 18%

profile of v7, /device:TPU:25, one launch (start us, length us, event | category | flops | bytes accessed | tf_op | source)
XLA Modules:
  0.0 160.5 jit_solution(17315301281327046498)
XLA Ops:
  0.7 2.3 %constant_dynamic-slice_fusion.1 = bf16[512,896]{1,0:T(8,128)(2,1)} fusion(bf16[512,1792]{1,0:T(8,128)(2,1)} %g_ref.3, s32[]{:T(128)S(6)} %select_n.46), kind=kLoop, calls=%fused_computation.1 | loop fusion | bytes 1835012 | tf_op jit(solution)/shard_map/dynamic_slice | solution.py:406
  3.0 6.6 %collective-permute-start = (bf16[512,896]{1,0:T(8,128)(2,1)}, bf16[512,896]{1,0:T(8,128)(2,1)S(1)}, u32[]{:S(2)}, u32[]{:S(2)}) collective-permute-start(bf16[512,896]{1,0:T(8,128)(2,1)} %constant_dynamic-slice_fusion.1), channel_id=1, source_target_pairs={{0,16},{1,48},{2,18},{3,50},{4,20},{5,52},{6,22},{7,54},{8,24},{9,... | collective-permute-start | bytes 2752520 | tf_op jit(solution)/shard_map/ppermute | solution.py:25
  9.7 3.0 %shard_map.30 = (bf16[240,1408]{1,0:T(8,128)(2,1)}, bf16[240,1408]{1,0:T(8,128)(2,1)}) custom-call(s32[8]{0:T(128)S(1)} %stack.26.at_ref, bf16[512,1792]{1,0:T(8,128)(2,1)S(1)} %copy-done), custom_call_target="tpu_custom_call" | custom-call | flops 1000 | bytes 1000 | tf_op jit(solution)/shard_map/pallas_call | solution.py:68
  12.7 2.5 %collective-permute-start.1 = (bf16[240,1408]{1,0:T(8,128)(2,1)}, bf16[240,1408]{1,0:T(8,128)(2,1)}, u32[]{:S(2)}, u32[]{:S(2)}) collective-permute-start(bf16[240,1408]{1,0:T(8,128)(2,1)} %get-tuple-element.61), channel_id=1, source_target_pairs={{0,192},{1,193},{2,194},{3,195},{4,196},{5,197},{6,198},{7,199},{8... | collective-permute-start | bytes 2027528 | tf_op jit(solution)/shard_map/ppermute | solution.py:25
  15.3 13.1 %collective-permute-done.1.in_ref = bf16[240,1408]{1,0:T(8,128)(2,1)} collective-permute-done((bf16[240,1408]{1,0:T(8,128)(2,1)}, bf16[240,1408]{1,0:T(8,128)(2,1)}, u32[]{:S(2)}, u32[]{:S(2)}) %collective-permute-start.1) | collective-permute-done | bytes 675872 | tf_op jit(solution)/shard_map/ppermute | solution.py:25
  28.3 3.1 %shard_map.31 = bf16[464,1408]{1,0:T(8,128)(2,1)S(1)} custom-call(s32[8]{0:T(128)S(1)} %stack.26.at_ref, bf16[512,1792]{1,0:T(8,128)(2,1)S(1)} %copy-done, bf16[240,1408]{1,0:T(8,128)(2,1)} %collective-permute-done.1.in_ref), custom_call_target="tpu_custom_call" | custom-call | flops 1000 | bytes 1000 | tf_op jit(solution)/shard_map/pallas_call | solution.py:68
  31.5 5.8 %collective-permute-start.2 = (bf16[512,896]{1,0:T(8,128)(2,1)S(1)}, bf16[512,896]{1,0:T(8,128)(2,1)S(1)}, u32[]{:S(2)}, u32[]{:S(2)}) collective-permute-start(bf16[512,896]{1,0:T(8,128)(2,1)S(1)} %constant_dynamic-slice_fusion), channel_id=1, source_target_pairs={{0,0},{1,32},{2,2},{3,34},{4,4},{5,36},{6,6},{7,38},{8,8},{9,40},{... | collective-permute-start | bytes 2752520 | tf_op jit(solution)/shard_map/ppermute | solution.py:25
  37.3 2.5 %shard_map.32 = bf16[464,1408]{1,0:T(8,128)(2,1)S(1)} custom-call(s32[8]{0:T(128)S(1)} %stack.26.at_ref, bf16[512,1792]{1,0:T(8,128)(2,1)S(1)} %copy-done, bf16[240,1408]{1,0:T(8,128)(2,1)S(1)} %collective-permute-done.3.in_ref), custom_call_target="tpu_custom_call" | custom-call | flops 1000 | bytes 1000 | tf_op jit(solution)/shard_map/pallas_call | solution.py:68
  41.0 2.3 %collective-permute-start.7 = (bf16[464,1408]{1,0:T(8,128)(2,1)S(1)}, bf16[464,1408]{1,0:T(8,128)(2,1)S(1)}, u32[]{:S(2)}, u32[]{:S(2)}) collective-permute-start(bf16[464,1408]{1,0:T(8,128)(2,1)S(1)} %shard_map.31), channel_id=1, source_target_pairs={{0,192},{1,193},{2,194},{3,195},{4,196},{5,197},{6,198},{7,199},{8... | collective-permute-start | bytes 3919880 | tf_op jit(solution)/shard_map/ppermute | solution.py:25
  43.3 1.6 %shard_map.33 = (f32[448,1408]{1,0:T(8,128)S(1)}, f32[8,1408]{1,0:T(8,128)S(1)}) custom-call(s32[8]{0:T(128)S(1)} %stack.26.at_ref, bf16[512,1792]{1,0:T(8,128)(2,1)S(1)} %copy-done), custom_call_target="tpu_custom_call" | custom-call | flops 1000 | bytes 1000 | tf_op jit(solution)/shard_map/pallas_call | solution.py:68
  45.0 1.5 copy-done.1
  46.4 13.6 %collective-permute-done.2.far = bf16[512,896]{1,0:T(8,128)(2,1)S(1)} collective-permute-done((bf16[512,896]{1,0:T(8,128)(2,1)S(1)}, bf16[512,896]{1,0:T(8,128)(2,1)S(1)}, u32[]{:S(2)}, u32[]{:S(2)}) %collective-permute-start.2) | collective-permute-done | bytes 917536 | tf_op jit(solution)/shard_map/ppermute | solution.py:25
  60.5 4.9 %collective-permute-done.6.in_1 = bf16[464,1408]{1,0:T(8,128)(2,1)S(1)} collective-permute-done((bf16[464,1408]{1,0:T(8,128)(2,1)S(1)}, bf16[464,1408]{1,0:T(8,128)(2,1)S(1)}, u32[]{:S(2)}, u32[]{:S(2)}) %collective-permute-start.6) | collective-permute-done | bytes 1306656 | tf_op jit(solution)/shard_map/ppermute | solution.py:25
  65.5 6.1 %shard_map.34 = (bf16[112,1920]{1,0:T(8,128)(2,1)S(1)}, bf16[112,1920]{1,0:T(8,128)(2,1)S(1)}, bf16[112,1920]{1,0:T(8,128)(2,1)S(1)}, f32[112,1920]{1,0:T(8,128)S(1)}) custom-call(s32[8]{0:T(128)S(1)} %stack.26.at_ref, f32[448,1408]{1,0:T(8,128)} %copy-done.1, f32[8,1408]{1,0:T(8,128)S(1)} %get-tuple-element.70.norm_ref, ...), custom_call_target="tpu_custom_call" | custom-call | flops 1000 | bytes 1000 | tf_op jit(solution)/shard_map/pallas_call | solution.py:68
  71.6 2.4 %collective-permute-start.11 = (bf16[112,1920]{1,0:T(8,128)(2,1)S(1)}, bf16[112,1920]{1,0:T(8,128)(2,1)S(1)}, u32[]{:S(2)}, u32[]{:S(2)}) collective-permute-start(bf16[112,1920]{1,0:T(8,128)(2,1)S(1)} %get-tuple-element.82), channel_id=1, source_target_pairs={{0,48},{1,49},{2,50},{3,51},{4,52},{5,53},{6,54},{7,55},{8,56},{9,... | collective-permute-start | bytes 1290248 | tf_op jit(solution)/shard_map/ppermute | solution.py:25
  74.0 5.9 %shard_map.35 = (bf16[1168,256]{1,0:T(8,128)(2,1)S(1)}, bf16[1168,256]{1,0:T(8,128)(2,1)S(1)}, bf16[1168,256]{1,0:T(8,128)(2,1)S(1)}, f32[1152,256]{1,0:T(8,128)}, f32[16,128]{1,0:T(8,128)S(1)}) custom-call(s32[8]{0:T(128)S(1)} %stack.26.at_ref, bf16[512,896]{1,0:T(8,128)(2,1)S(1)} %collective-permute-done.2.far, ...), custom_call_target="tpu_custom_call" | custom-call | flops 1000 | bytes 1000 | tf_op jit(solution)/shard_map/pallas_call | solution.py:68
  81.4 2.4 %collective-permute-done.11.in_3 = bf16[112,1920]{1,0:T(8,128)(2,1)S(1)} collective-permute-done((bf16[112,1920]{1,0:T(8,128)(2,1)S(1)}, bf16[112,1920]{1,0:T(8,128)(2,1)S(1)}, u32[]{:S(2)}, u32[]{:S(2)}) %collective-permute-start.11) | collective-permute-done | bytes 430112 | tf_op jit(solution)/shard_map/ppermute | solution.py:25
  83.8 1.9 %collective-permute-done.10.in_1 = bf16[112,1920]{1,0:T(8,128)(2,1)S(1)} collective-permute-done((bf16[112,1920]{1,0:T(8,128)(2,1)S(1)}, bf16[112,1920]{1,0:T(8,128)(2,1)S(1)}, u32[]{:S(2)}, u32[]{:S(2)}) %collective-permute-start.10) | collective-permute-done | bytes 430112 | tf_op jit(solution)/shard_map/ppermute | solution.py:25
  86.7 5.3 %collective-permute-done.8.in_1 = bf16[1168,256]{1,0:T(8,128)(2,1)S(1)} collective-permute-done((bf16[1168,256]{1,0:T(8,128)(2,1)S(1)}, bf16[1168,256]{1,0:T(8,128)(2,1)S(1)}, u32[]{:S(2)}, u32[]{:S(2)}) %collective-permute-start.8) | collective-permute-done | bytes 598048 | tf_op jit(solution)/shard_map/ppermute | solution.py:25
  93.2 2.6 %collective-permute-start.20 = (bf16[112,1920]{1,0:T(8,128)(2,1)S(1)}, bf16[112,1920]{1,0:T(8,128)(2,1)S(1)}, u32[]{:S(2)}, u32[]{:S(2)}) collective-permute-start(bf16[112,1920]{1,0:T(8,128)(2,1)S(1)} %get-tuple-element.101), channel_id=1, source_target_pairs={{0,32},{1,33},{2,34},{3,35},{4,36},{5,37},{6,38},{7,39},{8,40},{9,... | collective-permute-start | bytes 1290248 | tf_op jit(solution)/shard_map/ppermute | solution.py:25
  95.8 7.7 %collective-permute-done.12.in_2 = bf16[1168,256]{1,0:T(8,128)(2,1)S(1)} collective-permute-done((bf16[1168,256]{1,0:T(8,128)(2,1)S(1)}, bf16[1168,256]{1,0:T(8,128)(2,1)S(1)}, u32[]{:S(2)}, u32[]{:S(2)}) %collective-permute-start.12) | collective-permute-done | bytes 598048 | tf_op jit(solution)/shard_map/ppermute | solution.py:25
  104.7 2.7 %shard_map.36 = (bf16[400,128]{1,0:T(8,128)(2,1)S(1)}, bf16[400,128]{1,0:T(8,128)(2,1)S(1)}, bf16[400,128]{1,0:T(8,128)(2,1)S(1)}, bf16[400,128]{1,0:T(8,128)(2,...) custom-call(s32[8]{0:T(128)S(1)} %stack.26.at_ref, ...), custom_call_target="tpu_custom_call" | custom-call | flops 1000 | bytes 1000 | tf_op jit(solution)/shard_map/pallas_call | solution.py:68
  107.4 7.1 %collective-permute-start.13 = (bf16[400,128]{1,0:T(8,128)(2,1)S(1)}, bf16[400,128]{1,0:T(8,128)(2,1)S(1)}, u32[]{:S(2)}, u32[]{:S(2)}) collective-permute-start(bf16[400,128]{1,0:T(8,128)(2,1)S(1)} %get-tuple-element.89), channel_id=1, source_target_pairs={{0,2},{1,3},{2,16},{3,17},{4,6},{5,7},{6,20},{7,21},{8,10},{9,11},... | collective-permute-start | bytes 307208 | tf_op jit(solution)/shard_map/ppermute | solution.py:25
  114.5 4.0 %collective-permute-start.14 = (bf16[400,128]{1,0:T(8,128)(2,1)S(1)}, bf16[400,128]{1,0:T(8,128)(2,1)S(1)}, u32[]{:S(2)}, u32[]{:S(2)}) collective-permute-start(bf16[400,128]{1,0:T(8,128)(2,1)S(1)} %get-tuple-element.90), channel_id=1, source_target_pairs={{0,32},{1,33},{2,34},{3,35},{4,36},{5,37},{6,38},{7,39},{8,40},{9,... | collective-permute-start | bytes 307208 | tf_op jit(solution)/shard_map/ppermute | solution.py:25
  120.2 11.5 %collective-permute-done.13.refs_1_ = bf16[400,128]{1,0:T(8,128)(2,1)S(1)} collective-permute-done((bf16[400,128]{1,0:T(8,128)(2,1)S(1)}, bf16[400,128]{1,0:T(8,128)(2,1)S(1)}, u32[]{:S(2)}, u32[]{:S(2)}) %collective-permute-start.13) | collective-permute-done | bytes 102432 | tf_op jit(solution)/shard_map/ppermute | solution.py:25
  132.9 2.4 %collective-permute-start.19 = (bf16[400,128]{1,0:T(8,128)(2,1)S(1)}, bf16[400,128]{1,0:T(8,128)(2,1)S(1)}, u32[]{:S(2)}, u32[]{:S(2)}) collective-permute-start(bf16[400,128]{1,0:T(8,128)(2,1)S(1)} %get-tuple-element.95), channel_id=1, source_target_pairs={{0,48},{1,49},{2,50},{3,51},{4,52},{5,53},{6,54},{7,55},{8,56},{9,... | collective-permute-start | bytes 307208 | tf_op jit(solution)/shard_map/ppermute | solution.py:25
  135.3 2.5 %shard_map.37 = (f32[112,1408]{1,0:T(8,128)S(1)}, f32[112,384]{1,0:T(8,128)S(1)}) custom-call(s32[8]{0:T(128)S(1)} %stack.26.at_ref, f32[112,1920]{1,0:T(8,128)S(1)} %get-tuple-element.96.own_ref, bf16[112,1920]{1,0:T(8,128)(2,1)S(1)} %collective-permute-done.10.in_1, bf16[112,1920]{1,0:T(8,128)(2,1)S(1)} %collective-permute-done.11.in_3, ...), custom_call_target="tpu_custom_call" | custom-call | flops 1000 | bytes 1000 | tf_op jit(solution)/shard_map/pallas_call | solution.py:68
  137.8 1.6 collective-permute-done.18.refs_6_
  139.4 4.2 %collective-permute-done.19.refs_7_ = bf16[400,128]{1,0:T(8,128)(2,1)S(1)} collective-permute-done((bf16[400,128]{1,0:T(8,128)(2,1)S(1)}, bf16[400,128]{1,0:T(8,128)(2,1)S(1)}, u32[]{:S(2)}, u32[]{:S(2)}) %collective-permute-start.19) | collective-permute-done | bytes 102432 | tf_op jit(solution)/shard_map/ppermute | solution.py:25
  145.2 7.4 %collective-permute-start.22 = (f32[128,128]{1,0:T(8,128)S(1)}, f32[128,128]{1,0:T(8,128)S(1)}, u32[]{:S(2)}, u32[]{:S(2)}) collective-permute-start(f32[128,128]{1,0:T(8,128)S(1)} %get-tuple-element.113), channel_id=1, source_target_pairs={{0,0},{1,1},{2,2},{3,3},{4,18},{5,19},{6,16},{7,17},{8,34},{9,35},... | collective-permute-start | bytes 196616 | tf_op jit(solution)/shard_map/ppermute | solution.py:25
  153.1 5.8 %collective-permute-done.22.refs_3_ = f32[128,128]{1,0:T(8,128)S(1)} collective-permute-done((f32[128,128]{1,0:T(8,128)S(1)}, f32[128,128]{1,0:T(8,128)S(1)}, u32[]{:S(2)}, u32[]{:S(2)}) %collective-permute-start.22) | collective-permute-done | bytes 65568 | tf_op jit(solution)/shard_map/ppermute | solution.py:25
  158.8 1.6 %shard_map.39 = (f32[512,128]{1,0:T(8,128)}, f32[112,1792]{1,0:T(8,128)}) custom-call(s32[8]{0:T(128)S(1)} %stack.26.at_ref, f32[256,128]{1,0:T(8,128)S(1)} %get-tuple-element.110.refs_0_, f32[128,128]{1,0:T(8,128)S(1)} %get-tuple-element.111.refs_1_, f32[128,128]{1,0:T(8,128)S(1)} %collective-permute-done.21.refs_2_, ...), custom_call_target="tpu_custom_call" | custom-call | flops 1000 | bytes 1000 | tf_op jit(solution)/shard_map/pallas_call | solution.py:68
  (35 shorter events, 12.0 us)
Async XLA Ops:
  0.6 9.0 %copy-start = (bf16[512,1792]{1,0:T(8,128)(2,1)S(1)}, bf16[512,1792]{1,0:T(8,128)(2,1)}, u32[]{:S(2)}) copy-start(bf16[512,1792]{1,0:T(8,128)(2,1)} %g_ref.3) | copy-start | bytes 5505028
  3.0 28.5 %collective-permute-start = (bf16[512,896]{1,0:T(8,128)(2,1)}, bf16[512,896]{1,0:T(8,128)(2,1)S(1)}, u32[]{:S(2)}, u32[]{:S(2)}) collective-permute-start(bf16[512,896]{1,0:T(8,128)(2,1)} %constant_dynamic-slice_fusion.1), channel_id=1, source_target_pairs={{0,16},{1,48},{2,18},{3,50},{4,20},{5,52},{6,22},{7,54},{8,24},{9,... | collective-permute-start | bytes 2752520 | tf_op jit(solution)/shard_map/ppermute | solution.py:25
  12.7 15.6 %collective-permute-start.1 = (bf16[240,1408]{1,0:T(8,128)(2,1)}, bf16[240,1408]{1,0:T(8,128)(2,1)}, u32[]{:S(2)}, u32[]{:S(2)}) collective-permute-start(bf16[240,1408]{1,0:T(8,128)(2,1)} %get-tuple-element.61), channel_id=1, source_target_pairs={{0,192},{1,193},{2,194},{3,195},{4,196},{5,197},{6,198},{7,199},{8... | collective-permute-start | bytes 2027528 | tf_op jit(solution)/shard_map/ppermute | solution.py:25
  15.2 22.1 %collective-permute-start.3 = (bf16[240,1408]{1,0:T(8,128)(2,1)}, bf16[240,1408]{1,0:T(8,128)(2,1)S(1)}, u32[]{:S(2)}, u32[]{:S(2)}) collective-permute-start(bf16[240,1408]{1,0:T(8,128)(2,1)} %get-tuple-element.64), channel_id=1, source_target_pairs={{0,64},{1,65},{2,66},{3,67},{4,68},{5,69},{6,70},{7,71},{8,72},{9,... | collective-permute-start | bytes 2027528 | tf_op jit(solution)/shard_map/ppermute | solution.py:25
  31.5 28.6 %collective-permute-start.2 = (bf16[512,896]{1,0:T(8,128)(2,1)S(1)}, bf16[512,896]{1,0:T(8,128)(2,1)S(1)}, u32[]{:S(2)}, u32[]{:S(2)}) collective-permute-start(bf16[512,896]{1,0:T(8,128)(2,1)S(1)} %constant_dynamic-slice_fusion), channel_id=1, source_target_pairs={{0,0},{1,32},{2,2},{3,34},{4,4},{5,36},{6,6},{7,38},{8,8},{9,40},{... | collective-permute-start | bytes 2752520 | tf_op jit(solution)/shard_map/ppermute | solution.py:25
  39.7 25.7 %collective-permute-start.6 = (bf16[464,1408]{1,0:T(8,128)(2,1)S(1)}, bf16[464,1408]{1,0:T(8,128)(2,1)S(1)}, u32[]{:S(2)}, u32[]{:S(2)}) collective-permute-start(bf16[464,1408]{1,0:T(8,128)(2,1)S(1)} %shard_map.32), channel_id=1, source_target_pairs={{0,64},{1,65},{2,66},{3,67},{4,68},{5,69},{6,70},{7,71},{8,72},{9,... | collective-permute-start | bytes 3919880 | tf_op jit(solution)/shard_map/ppermute | solution.py:25
  41.0 24.5 %collective-permute-start.7 = (bf16[464,1408]{1,0:T(8,128)(2,1)S(1)}, bf16[464,1408]{1,0:T(8,128)(2,1)S(1)}, u32[]{:S(2)}, u32[]{:S(2)}) collective-permute-start(bf16[464,1408]{1,0:T(8,128)(2,1)S(1)} %shard_map.31), channel_id=1, source_target_pairs={{0,192},{1,193},{2,194},{3,195},{4,196},{5,197},{6,198},{7,199},{8... | collective-permute-start | bytes 3919880 | tf_op jit(solution)/shard_map/ppermute | solution.py:25
  44.9 1.5 copy-start.1
  60.0 14.0 %collective-permute-start.4 = (bf16[512,896]{1,0:T(8,128)(2,1)S(1)}, bf16[512,896]{1,0:T(8,128)(2,1)S(1)}, u32[]{:S(2)}, u32[]{:S(2)}) collective-permute-start(bf16[512,896]{1,0:T(8,128)(2,1)S(1)} %collective-permute-done.2.far), channel_id=1, source_target_pairs={{0,1},{1,0},{2,3},{3,2},{4,5},{5,4},{6,7},{7,6},{8,9},{9,8},{10,11... | collective-permute-start | bytes 2752520 | tf_op jit(solution)/shard_map/ppermute | solution.py:25
  60.0 14.0 %collective-permute-start.5 = (bf16[512,896]{1,0:T(8,128)(2,1)S(1)}, bf16[512,896]{1,0:T(8,128)(2,1)S(1)}, u32[]{:S(2)}, u32[]{:S(2)}) collective-permute-start(bf16[512,896]{1,0:T(8,128)(2,1)S(1)} %collective-permute-done.near), channel_id=1, source_target_pairs={{0,1},{1,0},{2,3},{3,2},{4,5},{5,4},{6,7},{7,6},{8,9},{9,8},{10,11... | collective-permute-start | bytes 2752520 | tf_op jit(solution)/shard_map/ppermute | solution.py:25
  71.6 12.2 %collective-permute-start.11 = (bf16[112,1920]{1,0:T(8,128)(2,1)S(1)}, bf16[112,1920]{1,0:T(8,128)(2,1)S(1)}, u32[]{:S(2)}, u32[]{:S(2)}) collective-permute-start(bf16[112,1920]{1,0:T(8,128)(2,1)S(1)} %get-tuple-element.82), channel_id=1, source_target_pairs={{0,48},{1,49},{2,50},{3,51},{4,52},{5,53},{6,54},{7,55},{8,56},{9,... | collective-permute-start | bytes 1290248 | tf_op jit(solution)/shard_map/ppermute | solution.py:25
  74.0 11.7 %collective-permute-start.10 = (bf16[112,1920]{1,0:T(8,128)(2,1)S(1)}, bf16[112,1920]{1,0:T(8,128)(2,1)S(1)}, u32[]{:S(2)}, u32[]{:S(2)}) collective-permute-start(bf16[112,1920]{1,0:T(8,128)(2,1)S(1)} %get-tuple-element.71), channel_id=1, source_target_pairs={{0,16},{1,17},{2,18},{3,19},{4,20},{5,21},{6,22},{7,23},{8,24},{9,... | collective-permute-start | bytes 1290248 | tf_op jit(solution)/shard_map/ppermute | solution.py:25
  79.9 12.0 %collective-permute-start.8 = (bf16[1168,256]{1,0:T(8,128)(2,1)S(1)}, bf16[1168,256]{1,0:T(8,128)(2,1)S(1)}, u32[]{:S(2)}, u32[]{:S(2)}) collective-permute-start(bf16[1168,256]{1,0:T(8,128)(2,1)S(1)} %get-tuple-element.78), channel_id=1, source_target_pairs={{0,4},{1,5},{2,6},{3,7},{4,8},{5,9},{6,10},{7,11},{8,12},{9,13},{1... | collective-permute-start | bytes 1794056 | tf_op jit(solution)/shard_map/ppermute | solution.py:25
  79.9 13.3 %collective-permute-start.9 = (bf16[1168,256]{1,0:T(8,128)(2,1)S(1)}, bf16[1168,256]{1,0:T(8,128)(2,1)S(1)}, u32[]{:S(2)}, u32[]{:S(2)}) collective-permute-start(bf16[1168,256]{1,0:T(8,128)(2,1)S(1)} %get-tuple-element.79), channel_id=1, source_target_pairs={{0,12},{1,13},{2,14},{3,15},{4,0},{5,1},{6,2},{7,3},{8,4},{9,5},{1... | collective-permute-start | bytes 1794056 | tf_op jit(solution)/shard_map/ppermute | solution.py:25
  85.7 17.7 %collective-permute-start.12 = (bf16[1168,256]{1,0:T(8,128)(2,1)S(1)}, bf16[1168,256]{1,0:T(8,128)(2,1)S(1)}, u32[]{:S(2)}, u32[]{:S(2)}) collective-permute-start(bf16[1168,256]{1,0:T(8,128)(2,1)S(1)} %get-tuple-element.87), channel_id=1, source_target_pairs={{0,8},{1,9},{2,10},{3,11},{4,12},{5,13},{6,14},{7,15},{8,0},{9,1},... | collective-permute-start | bytes 1794056 | tf_op jit(solution)/shard_map/ppermute | solution.py:25
  93.2 39.7 %collective-permute-start.20 = (bf16[112,1920]{1,0:T(8,128)(2,1)S(1)}, bf16[112,1920]{1,0:T(8,128)(2,1)S(1)}, u32[]{:S(2)}, u32[]{:S(2)}) collective-permute-start(bf16[112,1920]{1,0:T(8,128)(2,1)S(1)} %get-tuple-element.101), channel_id=1, source_target_pairs={{0,32},{1,33},{2,34},{3,35},{4,36},{5,37},{6,38},{7,39},{8,40},{9,... | collective-permute-start | bytes 1290248 | tf_op jit(solution)/shard_map/ppermute | solution.py:25
  103.5 1.3 copy-start.2
  107.4 24.3 %collective-permute-start.13 = (bf16[400,128]{1,0:T(8,128)(2,1)S(1)}, bf16[400,128]{1,0:T(8,128)(2,1)S(1)}, u32[]{:S(2)}, u32[]{:S(2)}) collective-permute-start(bf16[400,128]{1,0:T(8,128)(2,1)S(1)} %get-tuple-element.89), channel_id=1, source_target_pairs={{0,2},{1,3},{2,16},{3,17},{4,6},{5,7},{6,20},{7,21},{8,10},{9,11},... | collective-permute-start | bytes 307208 | tf_op jit(solution)/shard_map/ppermute | solution.py:25
  114.5 17.3 %collective-permute-start.14 = (bf16[400,128]{1,0:T(8,128)(2,1)S(1)}, bf16[400,128]{1,0:T(8,128)(2,1)S(1)}, u32[]{:S(2)}, u32[]{:S(2)}) collective-permute-start(bf16[400,128]{1,0:T(8,128)(2,1)S(1)} %get-tuple-element.90), channel_id=1, source_target_pairs={{0,32},{1,33},{2,34},{3,35},{4,36},{5,37},{6,38},{7,39},{8,40},{9,... | collective-permute-start | bytes 307208 | tf_op jit(solution)/shard_map/ppermute | solution.py:25
  118.4 19.4 %collective-permute-start.15 = (bf16[400,128]{1,0:T(8,128)(2,1)S(1)}, bf16[400,128]{1,0:T(8,128)(2,1)S(1)}, u32[]{:S(2)}, u32[]{:S(2)}) collective-permute-start(bf16[400,128]{1,0:T(8,128)(2,1)S(1)} %get-tuple-element.91), channel_id=1, source_target_pairs={{0,50},{1,51},{2,0},{3,1},{4,54},{5,55},{6,4},{7,5},{8,58},{9,59},... | collective-permute-start | bytes 307208 | tf_op jit(solution)/shard_map/ppermute | solution.py:25
  119.2 18.6 %collective-permute-start.16 = (bf16[400,128]{1,0:T(8,128)(2,1)S(1)}, bf16[400,128]{1,0:T(8,128)(2,1)S(1)}, u32[]{:S(2)}, u32[]{:S(2)}) collective-permute-start(bf16[400,128]{1,0:T(8,128)(2,1)S(1)} %get-tuple-element.92), channel_id=1, source_target_pairs={{0,18},{1,19},{2,32},{3,33},{4,22},{5,23},{6,36},{7,37},{8,26},{9,... | collective-permute-start | bytes 307208 | tf_op jit(solution)/shard_map/ppermute | solution.py:25
  131.7 6.1 %collective-permute-start.17 = (bf16[400,128]{1,0:T(8,128)(2,1)S(1)}, bf16[400,128]{1,0:T(8,128)(2,1)S(1)}, u32[]{:S(2)}, u32[]{:S(2)}) collective-permute-start(bf16[400,128]{1,0:T(8,128)(2,1)S(1)} %get-tuple-element.93), channel_id=1, source_target_pairs={{0,34},{1,35},{2,48},{3,49},{4,38},{5,39},{6,52},{7,53},{8,42},{9,... | collective-permute-start | bytes 307208 | tf_op jit(solution)/shard_map/ppermute | solution.py:25
  131.7 7.7 %collective-permute-start.18 = (bf16[400,128]{1,0:T(8,128)(2,1)S(1)}, bf16[400,128]{1,0:T(8,128)(2,1)S(1)}, u32[]{:S(2)}, u32[]{:S(2)}) collective-permute-start(bf16[400,128]{1,0:T(8,128)(2,1)S(1)} %get-tuple-element.94), channel_id=1, source_target_pairs={{0,16},{1,17},{2,18},{3,19},{4,20},{5,21},{6,22},{7,23},{8,24},{9,... | collective-permute-start | bytes 307208 | tf_op jit(solution)/shard_map/ppermute | solution.py:25
  132.9 10.7 %collective-permute-start.19 = (bf16[400,128]{1,0:T(8,128)(2,1)S(1)}, bf16[400,128]{1,0:T(8,128)(2,1)S(1)}, u32[]{:S(2)}, u32[]{:S(2)}) collective-permute-start(bf16[400,128]{1,0:T(8,128)(2,1)S(1)} %get-tuple-element.95), channel_id=1, source_target_pairs={{0,48},{1,49},{2,50},{3,51},{4,52},{5,53},{6,54},{7,55},{8,56},{9,... | collective-permute-start | bytes 307208 | tf_op jit(solution)/shard_map/ppermute | solution.py:25
  143.6 15.2 %collective-permute-start.23 = (f32[112,384]{1,0:T(8,128)S(1)}, f32[112,384]{1,0:T(8,128)S(1)}, u32[]{:S(2)}, u32[]{:S(2)}) collective-permute-start(f32[112,384]{1,0:T(8,128)S(1)} %get-tuple-element.115), channel_id=1, source_target_pairs={{0,64},{1,65},{2,66},{3,67},{4,68},{5,69},{6,70},{7,71},{8,72},{9,... | collective-permute-start | bytes 516104 | tf_op jit(solution)/shard_map/ppermute | solution.py:25
  145.1 8.0 %collective-permute-start.21 = (f32[128,128]{1,0:T(8,128)S(1)}, f32[128,128]{1,0:T(8,128)S(1)}, u32[]{:S(2)}, u32[]{:S(2)}) collective-permute-start(f32[128,128]{1,0:T(8,128)S(1)} %get-tuple-element.112), channel_id=1, source_target_pairs={{0,1},{1,2},{2,3},{3,0},{4,16},{5,17},{6,18},{7,19},{8,32},{9,33},... | collective-permute-start | bytes 196616 | tf_op jit(solution)/shard_map/ppermute | solution.py:25
  145.2 13.7 %collective-permute-start.22 = (f32[128,128]{1,0:T(8,128)S(1)}, f32[128,128]{1,0:T(8,128)S(1)}, u32[]{:S(2)}, u32[]{:S(2)}) collective-permute-start(f32[128,128]{1,0:T(8,128)S(1)} %get-tuple-element.113), channel_id=1, source_target_pairs={{0,0},{1,1},{2,2},{3,3},{4,18},{5,19},{6,16},{7,17},{8,34},{9,35},... | collective-permute-start | bytes 196616 | tf_op jit(solution)/shard_map/ppermute | solution.py:25
